TPU v7x, 32 devices: a whole 2x2x4 slice. The times are simulated.
32 devices in a mesh: expert: 8 (over y, x, core), hidden: 4 (over z).
Axes of the slice: x: 2, y: 2, z: 4, core: 2. Of those that a mesh axis runs over, the one named last changes fastest.
Arguments:
- tokens: bfloat16 [6144, 1024], P(('expert', 'hidden')), may hold values from -6 to 6
- cotangent: bfloat16 [6144, 1024], P(('expert', 'hidden')), may hold values from -6 to 6
- routes: int32 [6144, 1], P(('expert', 'hidden')), may hold values from 0 to 7; in each aligned block of 192 rows (0 to 191, 192 to 383, ...) at most 48 rows name the same one
- attn_weight: float32 [4, 1024, 1024], P(None, ('expert', 'hidden')), may hold values from -0.75 to 0.75
- attn_first: float32 [4, 1024, 1024], P(None, ('expert', 'hidden')), may hold values from -7.6293945e-05 to 7.6293945e-05
- attn_second: float32 [4, 1024, 1024], P(None, ('expert', 'hidden')), may hold values from 7.0096936e-12 to 1.121551e-10
- norm_param: float32 [2, 1024], P(None, ('expert', 'hidden')), may hold values from -1.2 to 3.2
- norm_first: float32 [2, 1024], P(None, ('expert', 'hidden')), may hold values from -0.00030517578 to 0.00030517578
- norm_second: float32 [2, 1024], P(None, ('expert', 'hidden')), may hold values from 1.121551e-10 to 1.7944816e-09
- up_weight: bfloat16 [8, 1024, 4096], P('expert', None, 'hidden'), may hold values from -0.4375 to 0.4375
- up_first: float32 [8, 1024, 4096], P('expert', None, 'hidden'), may hold values from -7.6293945e-05 to 7.6293945e-05
- up_second: float32 [8, 1024, 4096], P('expert', None, 'hidden'), may hold values from 7.0096936e-12 to 1.121551e-10
- down_weight: bfloat16 [8, 4096, 1024], P('expert', 'hidden'), may hold values from -0.4375 to 0.4375
- down_first: float32 [8, 4096, 1024], P('expert', 'hidden'), may hold values from -7.6293945e-05 to 7.6293945e-05
- down_second: float32 [8, 4096, 1024], P('expert', 'hidden'), may hold values from 7.0096936e-12 to 1.121551e-10
- expert_vector: float32 [8, 3, 1024], P('expert'), may hold values from -1.2 to 1.4
- vector_first: float32 [8, 3, 1024], P('expert'), may hold values from -0.00030517578 to 0.00030517578
- vector_second: float32 [8, 3, 1024], P('expert'), may hold values from 1.121551e-10 to 1.7944816e-09
Outputs:
- block_out: bfloat16 [6144, 1024], P(('expert', 'hidden'))
- token_grad: bfloat16 [6144, 1024], P(('expert', 'hidden'))
- grad_norm: float32 [], replicated
- attn_update: float32 [4, 1024, 1024], P(None, ('expert', 'hidden'))
- attn_moment: float32 [4, 1024, 1024], P(None, ('expert', 'hidden'))
- attn_square: float32 [4, 1024, 1024], P(None, ('expert', 'hidden'))
- norm_update: float32 [2, 1024], P(None, ('expert', 'hidden'))
- norm_moment: float32 [2, 1024], P(None, ('expert', 'hidden'))
- norm_square: float32 [2, 1024], P(None, ('expert', 'hidden'))
- up_update: float32 [8, 1024, 4096], P('expert', None, 'hidden')
- up_moment: float32 [8, 1024, 4096], P('expert', None, 'hidden')
- up_square: float32 [8, 1024, 4096], P('expert', None, 'hidden')
- down_update: float32 [8, 4096, 1024], P('expert', 'hidden')
- down_moment: float32 [8, 4096, 1024], P('expert', 'hidden')
- down_square: float32 [8, 4096, 1024], P('expert', 'hidden')
- vector_update: float32 [8, 3, 1024], P('expert')
- vector_moment: float32 [8, 3, 1024], P('expert')
- vector_square: float32 [8, 3, 1024], P('expert')
- expert_stats: float32 [2, 8], P(None, 'expert')
Inputs may be any that keep to these rules, and one draw needn't show every extreme that they name: `routes`: one expert per token; the tokens of one device name one expert at most 48 times; every expert is named.
All inputs are finite; a program needn't handle non-finite values.
Results may differ from a plain program's by a relative error of at most 0.018.
Values may be sent and summed in bfloat16 or wider, within the bound.
A program may use at most 256 MiB of HBM per device.

v0:
```python
import jax
import jax.numpy as jnp
from jax import lax
from jax.sharding import PartitionSpec as P

HEADS = 16
STEP = 10


norm_eps = 1e-05
clip_level = 1.0
beta_one = 0.9
beta_two = 0.999
adam_eps = 1e-08
decay_rate = 0.1
rate_matrix = 0.05
rate_vector = 0.5
masked_fill = -1e30


def layer_norm(inputs, gain_row, bias_row):
    average = jnp.mean(inputs, axis=-1, keepdims=True)
    centred = inputs - average
    variance = jnp.mean(centred * centred, axis=-1, keepdims=True)
    return centred * lax.rsqrt(variance + norm_eps) * gain_row + bias_row


def gelu_exact(values):
    return jax.nn.gelu(values, approximate=False)


def adam_step(weight, first, second, grad, clip_factor, rate, decay):
    clipped = grad * clip_factor
    moment = beta_one * first + (1.0 - beta_one) * clipped
    square = beta_two * second + (1.0 - beta_two) * clipped * clipped
    corr_one = 1.0 - beta_one**STEP
    corr_two = 1.0 - beta_two**STEP
    update = moment / corr_one / (jnp.sqrt(square / corr_two) + adam_eps) + decay * weight
    return (weight - rate * update, moment, square)


def shards(
    tokens,
    cotangent,
    routes,
    attn_weight,
    attn_first,
    attn_second,
    norm_param,
    norm_first,
    norm_second,
    up_weight,
    up_first,
    up_second,
    down_weight,
    down_first,
    down_second,
    expert_vector,
    vector_first,
    vector_second,
):
    experts_here = lax.axis_size("expert")
    hidden_size = lax.axis_size("hidden")
    token_count = tokens.shape[0]
    features = tokens.shape[1]
    capacity = 2 * token_count // experts_here
    slot_rows = experts_here * capacity
    head_dim = features // HEADS
    scaling = head_dim ** (-0.5)
    attn_low = attn_weight.astype(jnp.bfloat16)
    norm_low = norm_param.astype(jnp.bfloat16)
    attn_full, norm_full = (
        lax.all_gather(attn_low, ("expert", "hidden"), axis=1, tiled=True),
        lax.all_gather(norm_low, ("expert", "hidden"), axis=1, tiled=True),
    )
    inputs = tokens.astype(jnp.float32)
    normed, norm_pull = jax.vjp(
        layer_norm, inputs, norm_full[0].astype(jnp.float32), norm_full[1].astype(jnp.float32)
    )
    normed_low = normed.astype(jnp.bfloat16)
    projected = jnp.einsum(
        "td,sde->ste", normed_low, attn_full[:3], preferred_element_type=jnp.float32
    ).astype(jnp.bfloat16)
    query = projected[0].reshape(token_count, HEADS, head_dim)
    keys_all = projected[1].reshape(token_count, HEADS, head_dim)
    values_all = projected[2].reshape(token_count, HEADS, head_dim)
    causal = jnp.arange(token_count)[:, None] >= jnp.arange(token_count)[None, :]

    def score_rows():
        raw = (
            jnp.einsum("qhe,khe->hqk", query, keys_all, preferred_element_type=jnp.float32)
            * scaling
        )
        return jnp.where(causal[None], raw, masked_fill)

    scores = score_rows()
    row_max = jnp.max(scores, axis=-1, keepdims=True)
    expo = jnp.exp(scores - row_max)
    row_total = jnp.sum(expo, axis=-1, keepdims=True)
    log_total = row_max + jnp.log(row_total)
    probs_low = (expo / row_total).astype(jnp.bfloat16)
    context = jnp.einsum("hqk,khe->qhe", probs_low, values_all, preferred_element_type=jnp.float32)
    context = context.reshape(token_count, features).astype(jnp.bfloat16)
    resid = inputs + jnp.dot(context, attn_full[3], preferred_element_type=jnp.float32)
    route = routes[:, 0]
    chosen = (route[:, None] == jnp.arange(experts_here, dtype=jnp.int32)[None, :]).astype(
        jnp.int32
    )
    ranked = jnp.sum((jnp.cumsum(chosen, axis=0) - 1) * chosen, axis=1)
    placed = route * capacity + ranked
    placing = (jnp.arange(slot_rows, dtype=jnp.int32)[:, None] == placed[None, :]).astype(
        jnp.bfloat16
    )
    outgoing = jnp.dot(
        placing, resid.astype(jnp.bfloat16), preferred_element_type=jnp.float32
    ).astype(jnp.bfloat16)
    occupied = jnp.sum(placing.astype(jnp.float32), axis=1).astype(jnp.bfloat16)
    arrived, arrived_mask = (
        lax.all_to_all(
            outgoing.reshape(experts_here, capacity, features),
            "expert",
            split_axis=0,
            concat_axis=0,
            tiled=True,
        ),
        lax.all_to_all(
            occupied.reshape(experts_here, capacity),
            "expert",
            split_axis=0,
            concat_axis=0,
            tiled=True,
        ),
    )
    gathered, gathered_mask = (
        lax.all_gather(arrived, "hidden", axis=0, tiled=True),
        lax.all_gather(arrived_mask, "hidden", axis=0, tiled=True),
    )
    rows_all = gathered.reshape(-1, features)
    mask_all = gathered_mask.reshape(-1).astype(jnp.float32)
    rows_float = rows_all.astype(jnp.float32)
    centroid = expert_vector[0, 0]
    gating = jax.nn.sigmoid(jnp.sum(rows_float * centroid, axis=-1))
    expert_normed, expert_pull = jax.vjp(
        layer_norm, rows_float, expert_vector[0, 1], expert_vector[0, 2]
    )
    expert_low = expert_normed.astype(jnp.bfloat16)
    before = jnp.dot(expert_low, up_weight[0], preferred_element_type=jnp.float32)
    after, gelu_pull = jax.vjp(gelu_exact, before)
    after_low = after.astype(jnp.bfloat16)
    branch_own = lax.psum_scatter(
        jnp.dot(after_low, down_weight[0], preferred_element_type=jnp.float32).astype(jnp.bfloat16),
        "hidden",
        scatter_dimension=0,
        tiled=True,
    ).astype(jnp.float32)
    own_start = lax.axis_index("hidden") * slot_rows
    gating_own = lax.dynamic_slice_in_dim(gating, own_start, slot_rows, 0)
    delta = (gating_own[:, None] * branch_own).astype(jnp.bfloat16)
    returned = lax.all_to_all(
        delta.reshape(experts_here, capacity, features),
        "expert",
        split_axis=0,
        concat_axis=0,
        tiled=True,
    )
    delta_tokens = jnp.einsum(
        "st,sd->td",
        placing,
        returned.reshape(slot_rows, features),
        preferred_element_type=jnp.float32,
    )
    block_out = (resid + delta_tokens).astype(jnp.bfloat16)
    routed_count = jnp.sum(mask_all)
    gate_total = jnp.sum(mask_all * gating)
    expert_stats = jnp.stack(
        [routed_count / (token_count * hidden_size), gate_total / routed_count]
    )[:, None]
    cot_slots = jnp.dot(placing, cotangent, preferred_element_type=jnp.float32).astype(jnp.bfloat16)
    cot_arrived = lax.all_to_all(
        cot_slots.reshape(experts_here, capacity, features),
        "expert",
        split_axis=0,
        concat_axis=0,
        tiled=True,
    )
    cot_rows = lax.all_gather(cot_arrived, "hidden", axis=0, tiled=True).reshape(-1, features)
    d_branch = (gating[:, None] * cot_rows.astype(jnp.float32)).astype(jnp.bfloat16)
    grad_down = jnp.einsum("gf,gd->fd", after_low, d_branch, preferred_element_type=jnp.float32)
    d_after = jnp.einsum("gd,fd->gf", d_branch, down_weight[0], preferred_element_type=jnp.float32)
    d_before = gelu_pull(d_after)[0].astype(jnp.bfloat16)
    grad_up = jnp.einsum("gd,gf->df", expert_low, d_before, preferred_element_type=jnp.float32)
    d_expert_normed = jnp.einsum(
        "gf,df->gd", d_before, up_weight[0], preferred_element_type=jnp.float32
    )
    d_rows, d_expert_gain, d_expert_bias = expert_pull(d_expert_normed)
    d_rows_own = lax.psum_scatter(
        d_rows.astype(jnp.bfloat16), "hidden", scatter_dimension=0, tiled=True
    ).astype(jnp.float32)
    cot_own = lax.dynamic_slice_in_dim(cot_rows, own_start, slot_rows, 0).astype(jnp.float32)
    rows_own = lax.dynamic_slice_in_dim(rows_float, own_start, slot_rows, 0)
    d_gating = jnp.sum(cot_own * branch_own, axis=-1)
    d_logit = d_gating * gating_own * (1.0 - gating_own)
    d_centroid = jnp.sum(d_logit[:, None] * rows_own, axis=0)
    d_sent = (d_rows_own + d_logit[:, None] * centroid).astype(jnp.bfloat16)
    back_slots = lax.all_to_all(
        d_sent.reshape(experts_here, capacity, features),
        "expert",
        split_axis=0,
        concat_axis=0,
        tiled=True,
    )
    d_resid = cotangent.astype(jnp.float32) + jnp.einsum(
        "st,sd->td",
        placing,
        back_slots.reshape(slot_rows, features),
        preferred_element_type=jnp.float32,
    )
    vector_grad = lax.psum(jnp.stack([d_centroid, d_expert_gain, d_expert_bias])[None], "hidden")
    d_project = d_resid.astype(jnp.bfloat16)
    grad_out_proj = jnp.einsum("td,te->de", context, d_project, preferred_element_type=jnp.float32)
    d_context = jnp.einsum(
        "te,de->td", d_project, attn_full[3], preferred_element_type=jnp.float32
    ).astype(jnp.bfloat16)
    d_context = d_context.reshape(token_count, HEADS, head_dim)
    attn_probs = jnp.exp(score_rows() - log_total)
    probs_again = attn_probs.astype(jnp.bfloat16)
    d_probs = jnp.einsum("qhe,khe->hqk", d_context, values_all, preferred_element_type=jnp.float32)
    d_values = jnp.einsum(
        "hqk,qhe->khe", probs_again, d_context, preferred_element_type=jnp.float32
    ).astype(jnp.bfloat16)
    d_scores = (
        attn_probs * (d_probs - jnp.sum(d_probs * attn_probs, axis=-1, keepdims=True))
    ).astype(jnp.bfloat16)
    d_query = (
        jnp.einsum("hqk,khe->qhe", d_scores, keys_all, preferred_element_type=jnp.float32) * scaling
    ).astype(jnp.bfloat16)
    d_keys = (
        jnp.einsum("hqk,qhe->khe", d_scores, query, preferred_element_type=jnp.float32) * scaling
    ).astype(jnp.bfloat16)
    d_projected = jnp.stack(
        [
            d_query.reshape(token_count, features),
            d_keys.reshape(token_count, features),
            d_values.reshape(token_count, features),
        ]
    )
    grad_qkv = jnp.einsum(
        "td,ste->sde", normed_low, d_projected, preferred_element_type=jnp.float32
    )
    d_normed = jnp.einsum(
        "ste,sde->td", d_projected, attn_full[:3], preferred_element_type=jnp.float32
    )
    d_inputs, d_norm_gain, d_norm_bias = norm_pull(d_normed)
    token_grad = (d_resid + d_inputs).astype(jnp.bfloat16)
    grad_attn = jnp.concatenate([grad_qkv, grad_out_proj[None]], axis=0)
    grad_norm_param = jnp.stack([d_norm_gain, d_norm_bias])
    attn_shard, norm_shard = (
        lax.psum_scatter(grad_attn, ("expert", "hidden"), scatter_dimension=1, tiled=True),
        lax.psum_scatter(grad_norm_param, ("expert", "hidden"), scatter_dimension=1, tiled=True),
    )
    local_square = (
        jnp.sum(attn_shard * attn_shard)
        + jnp.sum(norm_shard * norm_shard)
        + jnp.sum(grad_up * grad_up)
        + jnp.sum(grad_down * grad_down)
        + jnp.sum(vector_grad * vector_grad) / hidden_size
    )
    grad_norm = jnp.sqrt(lax.psum(local_square, ("expert", "hidden")))
    clip_factor = clip_level / jnp.maximum(grad_norm, clip_level)
    attn_new = adam_step(
        attn_weight, attn_first, attn_second, attn_shard, clip_factor, rate_matrix, decay_rate
    )
    norm_new = adam_step(
        norm_param, norm_first, norm_second, norm_shard, clip_factor, rate_vector, 0.0
    )
    up_new = adam_step(
        up_weight.astype(jnp.float32),
        up_first,
        up_second,
        grad_up[None],
        clip_factor,
        rate_matrix,
        decay_rate,
    )
    down_new = adam_step(
        down_weight.astype(jnp.float32),
        down_first,
        down_second,
        grad_down[None],
        clip_factor,
        rate_matrix,
        decay_rate,
    )
    vector_new = adam_step(
        expert_vector, vector_first, vector_second, vector_grad, clip_factor, rate_vector, 0.0
    )
    return (
        block_out,
        token_grad,
        grad_norm,
        attn_new[0],
        attn_new[1],
        attn_new[2],
        norm_new[0],
        norm_new[1],
        norm_new[2],
        up_new[0],
        up_new[1],
        up_new[2],
        down_new[0],
        down_new[1],
        down_new[2],
        vector_new[0],
        vector_new[1],
        vector_new[2],
        expert_stats,
    )


def solution(mesh):
    return jax.shard_map(
        shards,
        mesh=mesh,
        in_specs=(
            P(("expert", "hidden"), None),
            P(("expert", "hidden"), None),
            P(("expert", "hidden"), None),
            P(None, ("expert", "hidden"), None),
            P(None, ("expert", "hidden"), None),
            P(None, ("expert", "hidden"), None),
            P(None, ("expert", "hidden")),
            P(None, ("expert", "hidden")),
            P(None, ("expert", "hidden")),
            P("expert", None, "hidden"),
            P("expert", None, "hidden"),
            P("expert", None, "hidden"),
            P("expert", "hidden", None),
            P("expert", "hidden", None),
            P("expert", "hidden", None),
            P("expert", None, None),
            P("expert", None, None),
            P("expert", None, None),
        ),
        out_specs=(
            P(("expert", "hidden"), None),
            P(("expert", "hidden"), None),
            P(),
            P(None, ("expert", "hidden"), None),
            P(None, ("expert", "hidden"), None),
            P(None, ("expert", "hidden"), None),
            P(None, ("expert", "hidden")),
            P(None, ("expert", "hidden")),
            P(None, ("expert", "hidden")),
            P("expert", None, "hidden"),
            P("expert", None, "hidden"),
            P("expert", None, "hidden"),
            P("expert", "hidden", None),
            P("expert", "hidden", None),
            P("expert", "hidden", None),
            P("expert", None, None),
            P("expert", None, None),
            P("expert", None, None),
            P(None, "expert"),
        ),
        check_vma=False,
    )
```

profile of v0, /device:TPU:0, one launch (start us, length us, event | category | flops | bytes accessed | tf_op | source)
XLA Modules:
  0.0 916.9 jit_solution(16854027604645051685)
XLA Ops:
  11.3 69.7 %all-gather.1 = bf16[32,32,2]{1,2,0:T(2,128)(2,1)S(1)} all-gather(bf16[1,32,2]{1,2,0:T(2,128)(2,1)S(1)} %convert_bitcast_fusion.2), channel_id=1, replica_groups=mesh['expert'=8,'hidden'=4] {'expert','hidden'}, dimensions={0}, use_global_device_ids=true | all-gather | bytes 4224 | tf_op jit(solution)/shard_map/all_gather | solution.py:74
  85.1 6.6 all-gather.6.cloned.1.call-done
  91.7 4.4 fusion.47
  106.4 15.7 %all_to_all.33 = bf16[8,48,1024]{2,1,0:T(8,128)(2,1)} all-to-all(bf16[8,48,1024]{2,1,0:T(8,128)(2,1)S(1)} %bitcast.155), channel_id=1, replica_groups=mesh['expert'=8,'hidden'=4] {'expert'}, dimensions={0} | all-to-all | bytes 1572864 | tf_op jit(solution)/shard_map/all_to_all | solution.py:119
  124.4 4.2 all-to-all-start.2
  129.4 12.0 %all-to-all-done.2 = bf16[8,48,1024]{2,1,0:T(8,128)(2,1)} async-done(((bf16[8,48,1024]{2,1,0:T(8,128)(2,1)}), bf16[8,48,1024]{2,1,0:T(8,128)(2,1)}, u32[]{:S(2)}, u32[]{:S(2)}) %all-to-all-start.2) | async-done | bytes 786464 | tf_op jit(solution)/shard_map/all_to_all | solution.py:179
  141.7 41.7 %all-gather.8.cloned.1.call-done = bf16[32,48,1024]{2,1,0:T(8,128)(2,1)} async-done(((bf16[8,48,1024]{2,1,0:T(8,128)(2,1)}), bf16[32,48,1024]{2,1,0:T(8,128)(2,1)}) %all-gather.8.cloned.1.call-update) | async-done | bytes 3145744 | tf_op jit(solution)/shard_map/all_gather | solution.py:135
  183.4 3.9 multiply_reduce_fusion.3
  190.3 18.0 %multiply_convert_fusion.2 = (bf16[1536,1024]{1,0:T(8,128)(2,1)S(1)}, f32[1536,1024]{1,0:T(8,128)}, f32[1536,1024]{1,0:T(8,128)}) fusion(bf16[1536,1024]{1,0:T(8,128)(2,1)S(1)} %bitcast.152, bf16[1,1024,1024]{2,1,0:T(8,128)(2,1)S(1)} %copy-done.19), kind=kOutput, calls=%fused_computation.13 | convolution fusion | flops 3323461632 | bytes 20971520 | tf_op jit(solution)/shard_map/dot_general | solution.py:147
  210.0 4.8 convolution_convert_fusion
  217.5 8.2 all_to_all.34
  225.8 12.9 %all-gather = bf16[32,1,48]{2,0,1:T(8,128)(2,1)} all-gather(bf16[8,1,48]{2,0,1:T(8,128)(2,1)S(1)} %copy.185), channel_id=2, replica_groups=mesh['expert'=8,'hidden'=4] {'hidden'}, dimensions={0}, use_global_device_ids=true | all-gather | bytes 3840 | tf_op jit(solution)/shard_map/all_gather | solution.py:136
  242.1 5.1 all-gather.10.cloned.1.call-done
  249.9 8.7 add_convert_fusion.2
  258.7 5.4 multiply_reduce_fusion
  269.6 5.3 bitcast_convert_fusion
  274.9 34.1 %reduce-scatter.6.cloned.1.call-done = bf16[384,1024]{1,0:T(8,128)(2,1)} async-done(((bf16[1536,1024]{1,0:T(8,128)(2,1)}), bf16[384,1024]{1,0:T(8,128)(2,1)}) %reduce-scatter.6.cloned.1.call-update) | async-done | bytes 786448 | tf_op jit(solution)/shard_map/reduce_scatter | solution.py:150
  311.4 60.6 %reduce-scatter.8.cloned.1.call-done = bf16[384,1024]{1,0:T(8,128)(2,1)} async-done(((bf16[1536,1024]{1,0:T(8,128)(2,1)}), bf16[384,1024]{1,0:T(8,128)(2,1)}) %reduce-scatter.8.cloned.1.call-update) | async-done | bytes 786448 | tf_op jit(solution)/shard_map/reduce_scatter | solution.py:196
  375.9 4.2 all-to-all-start.3
  381.1 11.6 %all-to-all-done.3 = bf16[8,48,1024]{2,1,0:T(8,128)(2,1)} async-done(((bf16[8,48,1024]{2,1,0:T(8,128)(2,1)}), bf16[8,48,1024]{2,1,0:T(8,128)(2,1)}, u32[]{:S(2)}, u32[]{:S(2)}) %all-to-all-start.3) | async-done | bytes 786464 | tf_op jit(solution)/shard_map/all_to_all | solution.py:205
  409.7 6.5 convolution_bitcast_fusion
  416.3 5.1 fusion.72
  424.1 11.9 %pad_maximum_fusion = f32[4,1024,1024]{1,2,0:T(8,128)} fusion(f32[1,1024,1024]{1,2,0:T(8,128)} %convolution_bitcast_fusion.1, f32[3,1024,1024]{1,2,0:T(8,128)} %convolution_bitcast_fusion), kind=kLoop, calls=%fused_computation | loop fusion | flops 4194304 | bytes 33554432 | tf_op jit(solution)/shard_map/concatenate | solution.py:255
  436.0 20.2 %copy.182 = f32[4,1024,1024]{2,0,1:T(4,128)} copy(f32[4,1024,1024]{1,2,0:T(8,128)} %pad_maximum_fusion) | data formatting | bytes 33554432 | tf_op jit(solution)/shard_map/concatenate | solution.py:255
  460.1 9.2 %multiply_reduce_fusion.4 = (f32[]{:T(128)}, f32[1024,1024]{1,0:T(8,128)}) fusion(bf16[1536,1024]{1,0:T(8,128)(2,1)} %copy-done.64, bf16[1536,1024]{1,0:T(8,128)(2,1)} %bitcast.144, f32[1536]{0:T(1024)S(1)} %copy-done.54), kind=kOutput, calls=%fused_computation.50 | convolution fusion | flops 3228041216 | bytes 10491908 | tf_op jit(solution)/shard_map/gf,gd->fd/dot_general | solution.py:188
  469.4 6.6 multiply_reduce_fusion.5
  479.8 17.4 %psum.14 = f32[1,3,1024]{2,0,1:T(1,128)S(1)} all-reduce(f32[1,3,1024]{2,0,1:T(1,128)S(1)} %broadcast_in_dim.66), channel_id=1, replica_groups=mesh['expert'=8,'hidden'=4] {'hidden'}, use_global_device_ids=true, to_apply=%region_29.30 | all-reduce | flops 3072 | bytes 24576 | tf_op jit(solution)/shard_map/psum | solution.py:218
  500.7 56.1 %reduce-scatter.10.cloned.1.call-done = f32[32,2]{1,0:T(8,128)} async-done(((f32[1024,2]{1,0:T(8,128)}), f32[32,2]{1,0:T(8,128)}) %reduce-scatter.10.cloned.1.call-update) | async-done | bytes 272
  558.2 280.1 %all-reduce.4.cloned.1.call-done = f32[4,1024,1024]{2,0,1:T(4,128)} async-done(((f32[4,1024,1024]{2,0,1:T(4,128)}), f32[4,1024,1024]{2,0,1:T(4,128)}) %all-reduce.4.cloned.1.call-update) | async-done | bytes 16777232
  844.0 40.4 %psum.15 = f32[]{:T(128)} all-reduce(f32[]{:T(128)S(6)} %add.223), channel_id=1, replica_groups=mesh['expert'=8,'hidden'=4] {'expert','hidden'}, use_global_device_ids=true, to_apply=%region_31.32 | all-reduce | flops 1 | bytes 8 | tf_op jit(solution)/shard_map/psum | solution.py:268
  889.4 10.3 %convert_subtract_fusion = (f32[1,1024,1024]{2,1,0:T(8,128)}, f32[1,1024,1024]{2,1,0:T(8,128)}, f32[1,1024,1024]{2,1,0:T(8,128)}) fusion(bf16[1,1024,1024]{2,1,0:T(8,128)(2,1)S(1)} %copy-done.18, f32[1024,1024]{1,0:T(8,128)} %get-tuple-element.189, f32[]{:T(128)S(6)} %div.149, f32[1,1024,1024]{2,1,0:T(8,128)} %param.31, f32[1,1024,1024]{2,1,0:T(8,128)} %param.32), kind=kLoop, calls=%fused_computation.35 | loop fusion | flops 17825792 | bytes 27262980 | tf_op jit(solution)/shard_map/sub | solution.py:39
  902.7 6.0 convert_subtract_fusion.1
  (236 shorter events, 87.6 us)
Async XLA Ops:
  7.2 84.5 %all-gather.6.cloned.1.call-start = ((), (), s32[]{:S(2)}) async-start(), calls=%async_computation.8 | async-start | bytes 8650752 | tf_op jit(solution)/shard_map/all_gather | solution.py:73
  9.0 174.4 %all-gather.8.cloned.1.call-start = ((), (), s32[]{:S(2)}) async-start(), calls=%async_computation.9 | async-start | bytes 3932160 | tf_op jit(solution)/shard_map/all_gather | solution.py:135
  83.1 13.1 %copy-start.45 = (f32[192]{0:T(256)}, f32[192]{0:T(256)S(1)}, u32[]{:S(2)}) copy-start(f32[192]{0:T(256)S(1)} %broadcast_multiply_fusion.1) | copy-start | bytes 2308
  84.3 11.8 %copy-start.47 = (f32[192]{0:T(256)}, f32[192]{0:T(256)S(1)}, u32[]{:S(2)}) copy-start(f32[192]{0:T(256)S(1)} %fusion.92) | copy-start | bytes 2308
  85.0 37.0 %copy-start.34 = (s32[192]{0:T(256)}, s32[192]{0:T(256)S(1)}, u32[]{:S(2)}) copy-start(s32[192]{0:T(256)S(1)} %multiply_add_fusion.4) | copy-start | bytes 2308
  85.1 11.1 %copy-start.51 = (f32[1,1024]{1,0:T(1,128)}, f32[1,1024]{1,0:T(1,128)S(1)}, u32[]{:S(2)}) copy-start(f32[1,1024]{1,0:T(1,128)S(1)} %get-tuple-element.175) | copy-start | bytes 12292
  105.9 22.9 %copy-start.32 = (f32[1,3,1024]{2,0,1:T(1,128)S(1)}, f32[1,3,1024]{2,0,1:T(1,128)}, u32[]{:S(2)}) copy-start(f32[1,3,1024]{2,0,1:T(1,128)} %param.33) | copy-start | bytes 36868
  124.4 16.9 %all-to-all-start.2 = ((bf16[8,48,1024]{2,1,0:T(8,128)(2,1)}), bf16[8,48,1024]{2,1,0:T(8,128)(2,1)}, u32[]{:S(2)}, u32[]{:S(2)}) async-start(bf16[8,48,1024]{2,1,0:T(8,128)(2,1)} %bitcast.154), calls=%async_computation.3 | async-start | bytes 1572864 | tf_op jit(solution)/shard_map/all_to_all | solution.py:179
  128.7 118.5 %all-gather.10.cloned.1.call-start = ((), (), s32[]{:S(2)}) async-start(), calls=%async_computation.11 | async-start | bytes 3932160 | tf_op jit(solution)/shard_map/all_gather | solution.py:186
  129.4 58.0 %copy-start.39 = (f32[1,1,1024]{2,0,1:T(1,128)}, f32[1,1,1024]{2,0,1:T(1,128)S(1)}, u32[]{:S(2)}) copy-start(f32[1,1,1024]{2,0,1:T(1,128)S(1)} %get-tuple-element.171) | copy-start | bytes 12292
  141.3 167.6 %reduce-scatter.6.cloned.1.call-start = ((), (), s32[]{:S(2)}) async-start(), calls=%async_computation.10 | async-start | bytes 3932160 | tf_op jit(solution)/shard_map/reduce_scatter | solution.py:150
  190.3 19.7 %copy-start.16 = (bf16[1,1024,1024]{2,1,0:T(8,128)(2,1)S(1)}, bf16[1,1024,1024]{2,1,0:T(8,128)(2,1)}, u32[]{:S(2)}) copy-start(bf16[1,1024,1024]{2,1,0:T(8,128)(2,1)} %param.30) | copy-start | bytes 6291460
  214.8 157.2 %reduce-scatter.8.cloned.1.call-start = ((), (), s32[]{:S(2)}) async-start(), calls=%async_computation.12 | async-start | bytes 3932160 | tf_op jit(solution)/shard_map/reduce_scatter | solution.py:196
  269.6 102.4 %copy-start.40 = (f32[1,1,1024]{2,0,1:T(1,128)S(1)}, f32[1,1,1024]{2,0,1:T(1,128)}, u32[]{:S(2)}) copy-start(f32[1,1,1024]{2,0,1:T(1,128)} %copy-done.39) | copy-start | bytes 12292
  375.9 16.8 %all-to-all-start.3 = ((bf16[8,48,1024]{2,1,0:T(8,128)(2,1)}), bf16[8,48,1024]{2,1,0:T(8,128)(2,1)}, u32[]{:S(2)}, u32[]{:S(2)}) async-start(bf16[8,48,1024]{2,1,0:T(8,128)(2,1)} %bitcast.157), calls=%async_computation.5 | async-start | bytes 1572864 | tf_op jit(solution)/shard_map/all_to_all | solution.py:205
  380.1 176.6 %reduce-scatter.10.cloned.1.call-start = ((), (), s32[]{:S(2)}) async-start(), calls=%async_computation.13 | async-start | bytes 540672
  423.8 414.4 %all-reduce.4.cloned.1.call-start = ((), (), s32[]{:S(2)}) async-start(), calls=%async_computation.14 | async-start | bytes 33554432
  456.2 13.1 %slice-start = ((s8[6291456]{0:T(1024)(128)(4,1)}), s8[2097152]{0:T(1024)(128)(4,1)S(1)}, s32[]{:S(2)}) async-start(s8[6291456]{0:T(1024)(128)(4,1)} %bitcast.141), calls=%async_computation.15 | async-start | bytes 4194304
  476.0 366.8 %copy-start.4 = (f32[192,1024]{1,0:T(8,128)S(1)}, f32[192,1024]{1,0:T(8,128)}, u32[]{:S(2)}) copy-start(f32[192,1024]{1,0:T(8,128)} %copy-done.3) | copy-start | bytes 2359300
  476.0 366.8 %copy-start.35 = (s32[192]{0:T(256)S(1)}, s32[192]{0:T(256)}, u32[]{:S(2)}) copy-start(s32[192]{0:T(256)} %copy-done.34) | copy-start | bytes 2308
  476.0 409.1 %copy-start.61 = (f32[2,32]{1,0:T(2,128)S(1)}, f32[2,32]{1,0:T(2,128)}, u32[]{:S(2)}) copy-start(f32[2,32]{1,0:T(2,128)} %param.24) | copy-start | bytes 772
  476.0 409.1 %copy-start.62 = (f32[2,32]{1,0:T(2,128)S(1)}, f32[2,32]{1,0:T(2,128)}, u32[]{:S(2)}) copy-start(f32[2,32]{1,0:T(2,128)} %param.25) | copy-start | bytes 772
  476.0 409.1 %copy-start.63 = (f32[2,32]{1,0:T(2,128)S(1)}, f32[2,32]{1,0:T(2,128)}, u32[]{:S(2)}) copy-start(f32[2,32]{1,0:T(2,128)} %param.26) | copy-start | bytes 772
  476.0 409.7 %copy-start.33 = (f32[1,3,1024]{2,0,1:T(1,128)S(1)}, f32[1,3,1024]{2,0,1:T(1,128)}, u32[]{:S(2)}) copy-start(f32[1,3,1024]{2,0,1:T(1,128)} %param.33) | copy-start | bytes 36868
  476.0 409.7 %copy-start.55 = (f32[1,3,1024]{2,0,1:T(1,128)S(1)}, f32[1,3,1024]{2,0,1:T(1,128)}, u32[]{:S(2)}) copy-start(f32[1,3,1024]{2,0,1:T(1,128)} %param.34) | copy-start | bytes 36868
  476.0 409.7 %copy-start.56 = (f32[1,3,1024]{2,0,1:T(1,128)S(1)}, f32[1,3,1024]{2,0,1:T(1,128)}, u32[]{:S(2)}) copy-start(f32[1,3,1024]{2,0,1:T(1,128)} %param.35) | copy-start | bytes 36868
  476.1 366.7 %all-to-all-start.1 = ((bf16[8,48,1024]{2,1,0:T(8,128)(2,1)}), bf16[8,48,1024]{2,1,0:T(8,128)(2,1)S(1)}, u32[]{:S(2)}, u32[]{:S(2)}) async-start(bf16[8,48,1024]{2,1,0:T(8,128)(2,1)} %bitcast.156), calls=%async_computation.2 | async-start | bytes 1572864 | tf_op jit(solution)/shard_map/all_to_all | solution.py:159
  844.0 45.5 %copy-start.18 = (bf16[1,1024,1024]{2,1,0:T(8,128)(2,1)S(1)}, bf16[1,1024,1024]{2,1,0:T(8,128)(2,1)}, u32[]{:S(2)}) copy-start(bf16[1,1024,1024]{2,1,0:T(8,128)(2,1)} %param.30) | copy-start | bytes 6291460
  889.4 10.3 %copy-start.10 = (f32[1,1024,1024]{2,1,0:T(8,128)S(1)}, f32[1,1024,1024]{2,1,0:T(8,128)}, u32[]{:S(2)}) copy-start(f32[1,1024,1024]{2,1,0:T(8,128)} %param.28) | copy-start | bytes 12582916
  889.4 11.5 %copy-start.11 = (f32[1,1024,1024]{2,1,0:T(8,128)S(1)}, f32[1,1024,1024]{2,1,0:T(8,128)}, u32[]{:S(2)}) copy-start(f32[1,1024,1024]{2,1,0:T(8,128)} %param.29) | copy-start | bytes 12582916
  889.4 12.7 %copy-start.12 = (f32[1024,1024]{1,0:T(8,128)S(1)}, f32[1024,1024]{1,0:T(8,128)}, u32[]{:S(2)}) copy-start(f32[1024,1024]{1,0:T(8,128)} %get-tuple-element.187) | copy-start | bytes 12582916
  889.4 13.3 %copy-start.21 = (bf16[1,1024,1024]{2,1,0:T(8,128)(2,1)S(1)}, bf16[1,1024,1024]{2,1,0:T(8,128)(2,1)}, u32[]{:S(2)}) copy-start(bf16[1,1024,1024]{2,1,0:T(8,128)(2,1)} %param.27) | copy-start | bytes 6291460
  (47 other events, 209.8 us)
Sparse Core Ops, SparseCore 0:
  11.6 79.9 all-gather.5
  122.2 61.1 all-gather.7
  185.0 62.1 all-gather.9
  249.9 58.9 reduce-scatter.5
  311.7 60.2 reduce-scatter.7
  423.9 132.7 reduce-scatter.9
  563.9 274.3 all-reduce.3
where the time goes:
time: 924 us; the launch traced here: 917 us
  waiting for transfers between devices  508 us (55%)
  blocking collectives  164 us (18%)
  matrix products  89.8 us (10%)
  other arithmetic  77.8 us (8%)
  local copies, waits for them, and re-layouts  41.6 us (5%)
  between operations  22.4 us (2%)
  starting transfers between devices  13.1 us (1%)
    unnamed x9, waiting for transfers between devices  336 us
    all_gather x1, blocking collectives, shards(): lax.all_gather(norm_low, ('expert', 'hidden'), axis=1, tiled=True)  69.7 us
    reduce_scatter x1, waiting for transfers between devices, shards(): lax.psum_scatter(d_rows.astype(jnp.bfloat16), 'hidden', scatter_dimension...  60.6 us
    all_gather x1, waiting for transfers between devices, shards(): lax.all_gather(arrived, 'hidden', axis=0, tiled=True)  41.7 us
    psum x1, blocking collectives, shards(): grad_norm = jnp.sqrt(lax.psum(local_square, ('expert', 'hidden')))  40.4 us
    reduce_scatter x1, waiting for transfers between devices, shards(): lax.psum_scatter(jnp.dot(after_low, down_weight[0], preferred_element_typ...  34.1 us
    sub x5, other arithmetic, adam_step(): return (weight - rate * update, moment, square)  20.6 us
    concatenate x1, local copies, waits for them, and re-layouts, shards(): grad_attn = jnp.concatenate([grad_qkv, grad_out_proj[None]], axis=0)  20.2 us
  transfers between devices with their start and end apart: 10, of which 9 were waited for; matrix products, arithmetic and copies ran while one was open for 14% of the time, Pallas kernels for 0%

commit v1 on v0

--- a/solution.py
+++ b/solution.py
@@ -1,6 +1,11 @@
+import functools
+import math
+
 import jax
 import jax.numpy as jnp
 from jax import lax
+from jax.experimental import pallas as pl
+from jax.experimental.pallas import tpu as pltpu
 from jax.sharding import PartitionSpec as P
 
 HEADS = 16
@@ -16,6 +21,8 @@
 rate_matrix = 0.05
 rate_vector = 0.5
 masked_fill = -1e30
+EX, HI = "expert", "hidden"
+BOTH = (EX, HI)
 
 
 def layer_norm(inputs, gain_row, bias_row):
@@ -37,6 +44,1005 @@
     corr_two = 1.0 - beta_two**STEP
     update = moment / corr_one / (jnp.sqrt(square / corr_two) + adam_eps) + decay * weight
     return (weight - rate * update, moment, square)
+
+
+MESH = pl.DeviceIdType.MESH
+VMEM_SPEC = pl.BlockSpec(memory_space=pltpu.VMEM)
+ANY_SPEC = pl.BlockSpec(memory_space=pl.ANY)
+
+class Place:
+    def __init__(self, depth):
+        self.e = lax.axis_index(EX)
+        self.z = lax.axis_index(HI)
+        self.depth = depth
+        self.core = lax.rem(self.e, 2)
+        self.x = lax.rem(lax.div(self.e, 2), 2)
+        self.y = lax.div(self.e, 4)
+        self.ex = self.e + 2 - 4 * self.x
+        self.ey = self.e + 4 - 8 * self.y
+        self.exy = self.ex + 4 - 8 * self.y
+
+    def across(self, k):
+        c = lax.rem(self.core + k % 2, 2)
+        x = lax.rem(self.x + (k // 2) % 2, 2)
+        y = lax.rem(self.y + k // 4, 2)
+        return 4 * y + 2 * x + c
+
+    def up(self, d):
+        return lax.rem(self.z + d, self.depth)
+
+    def down(self, d):
+        return lax.rem(self.z + self.depth - d, self.depth)
+
+    def twin(self, e=None):
+        e = self.e if e is None else e
+        return e + 1 - 2 * self.core
+
+
+class Wire:
+    def __init__(self, send_sem, recv_sem):
+        self.send_sem, self.recv_sem = send_sem, recv_sem
+        self.count = 0
+        self.sent = []
+
+    def send(self, src, dst, device):
+        i = self.count
+        self.count += 1
+        copy = pltpu.make_async_remote_copy(
+            src_ref=src,
+            dst_ref=dst,
+            send_sem=self.send_sem.at[i],
+            recv_sem=self.recv_sem.at[i],
+            device_id=device,
+            device_id_type=MESH,
+        )
+        copy.start()
+        self.sent.append(copy)
+        return copy
+
+    def left(self, copy):
+        copy.wait_send()
+        self.sent = [one for one in self.sent if one is not copy]
+
+    def drain(self):
+        for copy in self.sent:
+            copy.wait_send()
+
+
+def meet(devices):
+    barrier = pltpu.get_barrier_semaphore()
+    for device in devices:
+        pl.semaphore_signal(barrier, inc=1, device_id=device, device_id_type=MESH)
+    pl.semaphore_wait(barrier, len(devices))
+
+
+def dot(a, b, ca=1, cb=0):
+    return lax.dot_general(a, b, (((ca,), (cb,)), ((), ())), preferred_element_type=jnp.float32)
+
+
+def attend_kernel(
+    depth,
+    cap,
+    tok,
+    w_own,
+    norm_own,
+    route,
+    cot,
+    w_out,
+    qkv,
+    normed,
+    ctx,
+    resid,
+    sent,
+    placed,
+    gains,
+    cot_raw,
+    wfull,
+    norm_in,
+    norm_sum,
+    send_sem,
+    recv_sem,
+    local_sem,
+):
+    at = Place(depth)
+    e, z = at.e, at.z
+    count, width = tok.shape
+    shard = w_own.shape[1]
+    meet(
+        [(e, at.up(d)) for d in range(1, depth)]
+        + [(at.ex, z), (at.ey, z), (at.twin(), z)]
+    )
+    wire = Wire(send_sem, recv_sem)
+    groups = [(0, 3), (3, 1)]
+
+    def block(g, who, zz):
+        first, mats = groups[g]
+        start = pl.multiple_of((who * depth + zz) * shard, shard)
+        return wfull.at[pl.ds(first, mats), pl.ds(start, shard)]
+
+    norm_z = [wire.send(norm_own, norm_in.at[d - 1], (e, at.up(d))) for d in range(1, depth)]
+    own = []
+    for g, (first, mats) in enumerate(groups):
+        copy = pltpu.make_async_copy(
+            w_own.at[pl.ds(first, mats)], block(g, e, z), local_sem.at[g]
+        )
+        copy.start()
+        own.append(copy)
+    unit_z = {}
+    for g, (first, mats) in enumerate(groups):
+        for d in range(1, depth):
+            unit_z[g, d] = wire.send(
+                w_own.at[pl.ds(first, mats)], block(g, e, z), (e, at.up(d))
+            )
+
+    cot_z = [wire.send(cot, cot_raw.at[d], (e, at.up(d))) for d in range(1, depth)]
+    cot_raw[0] = cot[...]
+
+    to_x, to_y, to_far, to_twin = {}, {}, {}, {}
+
+    def plane(g, d):
+        zz = at.down(d)
+        if d == 0:
+            own[g].wait()
+        else:
+            unit_z[g, d].wait_recv()
+        here = block(g, e, zz)
+        to_x[g, d] = wire.send(here, here, (at.ex, z))
+        to_y[g, d] = wire.send(here, here, (at.ey, z))
+        to_twin[g, d, 0] = wire.send(here, here, (at.twin(), z))
+
+    def forward(g, d):
+        zz = at.down(d)
+        from_x, from_y = block(g, at.ex, zz), block(g, at.ey, zz)
+        to_x[g, d].wait_recv()
+        if 2 * d < depth:
+            to_far[g, d] = wire.send(from_x, from_x, (at.ey, z))
+        to_twin[g, d, 1] = wire.send(from_x, from_x, (at.twin(), z))
+        to_y[g, d].wait_recv()
+        if 2 * d >= depth:
+            to_far[g, d] = wire.send(from_y, from_y, (at.ex, z))
+        to_twin[g, d, 2] = wire.send(from_y, from_y, (at.twin(), z))
+
+    def far(g, d):
+        zz = at.down(d)
+        to_far[g, d].wait_recv()
+        there = block(g, at.exy, zz)
+        to_twin[g, d, 3] = wire.send(there, there, (at.twin(), z))
+
+    def finish(g):
+        for d in range(depth):
+            for k in range(4):
+                to_twin[g, d, k].wait_recv()
+
+    def norm_step(k, device):
+        copy = wire.send(norm_sum.at[k], norm_in.at[depth - 1 + k], device)
+        return copy
+
+    plane(0, 0)
+    lanes = lax.broadcasted_iota(jnp.int32, (count, 128), 1)
+    chosen = jnp.where(route[...] == lanes, 1.0, 0.0)
+    rows_i = lax.broadcasted_iota(jnp.int32, (count, count), 0)
+    cols_i = lax.broadcasted_iota(jnp.int32, (count, count), 1)
+    lower = jnp.where(rows_i >= cols_i, 1.0, 0.0)
+    running = dot(lower.astype(jnp.bfloat16), chosen.astype(jnp.bfloat16))
+    rank = jnp.sum((running - 1.0) * chosen, axis=1, keepdims=True)
+    column = route[...].astype(jnp.float32) * float(cap) + rank
+    wide_r = lax.broadcasted_iota(jnp.int32, (count, 256), 0)
+    wide_c = lax.broadcasted_iota(jnp.int32, (count, 256), 1)
+    row = jnp.sum(jnp.where(wide_r == wide_c, column + 1.0, 0.0), axis=0, keepdims=True) - 1.0
+    placed[0] = jnp.broadcast_to(row, (8, 256)).astype(jnp.int32)
+    placed_z = [
+        wire.send(placed.at[0], placed.at[d], (e, at.up(d))) for d in range(1, depth)
+    ]
+    for copy in norm_z:
+        copy.wait_recv()
+    total = norm_own[...]
+    for d in range(1, depth):
+        total = total + norm_in[d - 1]
+    norm_sum[0] = total
+    norm_x = norm_step(0, (at.ex, z))
+    plane(0, 1)
+    norm_x.wait_recv()
+    norm_sum[1] = norm_sum[0] + norm_in[depth - 1]
+    norm_y = norm_step(1, (at.ey, z))
+    forward(0, 0)
+    plane(0, 2)
+    norm_y.wait_recv()
+    norm_sum[2] = norm_sum[1] + norm_in[depth]
+    norm_twin = norm_step(2, (at.twin(), z))
+    for d in range(3, depth):
+        plane(0, d)
+    norm_twin.wait_recv()
+    gain_rows = norm_sum[2] + norm_in[depth + 1]
+    tally = jnp.concatenate(
+        [
+            jnp.broadcast_to(jnp.sum(chosen, axis=0, keepdims=True), (16, 128)),
+            jnp.zeros((16, width - 128), jnp.float32),
+        ],
+        axis=1,
+    )
+    third_row = lax.broadcasted_iota(jnp.int32, (16, width), 0) == 2
+    gains[...] = jnp.where(third_row, tally, gain_rows.astype(jnp.float32)).astype(jnp.bfloat16)
+    gain = gains[0:1, :].astype(jnp.float32)
+    bias = gains[1:2, :].astype(jnp.float32)
+    for i in range(0, count, 64):
+        piece = tok[i : i + 64, :].astype(jnp.float32)
+        average = jnp.mean(piece, axis=-1, keepdims=True)
+        centred = piece - average
+        variance = jnp.mean(centred * centred, axis=-1, keepdims=True)
+        normed[i : i + 64, :] = (
+            centred * lax.rsqrt(variance + norm_eps) * gain + bias
+        ).astype(jnp.bfloat16)
+    for d in range(1, depth):
+        far(0, d - 1)
+        forward(0, d)
+    for d in range(depth):
+        plane(1, d)
+    far(0, depth - 1)
+    finish(0)
+    keep = pltpu.make_async_copy(
+        wfull.at[pl.ds(0, 3)], w_out.at[pl.ds(0, 3)], local_sem.at[2]
+    )
+    keep.start()
+    tiles = width // 256
+
+    @pl.loop(0, 3 * tiles)
+    def _(i):
+        m = lax.div(i, tiles)
+        cols = pl.ds(pl.multiple_of(lax.rem(i, tiles) * 256, 256), 256)
+        qkv[m, :, cols] = dot(normed[...], wfull[m, :, cols]).astype(jnp.bfloat16)
+
+    forward(1, 0)
+    forward(1, 1)
+    causal = rows_i >= cols_i
+    left = lax.broadcasted_iota(jnp.int32, (count, 128), 1) < 64
+    scaling = jnp.asarray(64 ** (-0.5), jnp.bfloat16)
+
+    def pair(i):
+        cols = pl.ds(pl.multiple_of(i * 128, 128), 128)
+        query = qkv[0, :, cols] * scaling
+        keys = qkv[1, :, cols]
+        values = qkv[2, :, cols]
+        halves = []
+        for side in range(2):
+            mask = left if side == 0 else jnp.logical_not(left)
+            scores = dot(jnp.where(mask, query, jnp.zeros_like(query)), keys, 1, 1)
+            scores = jnp.where(causal, scores, masked_fill)
+            top = jnp.max(scores, axis=-1, keepdims=True)
+            expo = jnp.exp(scores - top)
+            probs = expo / jnp.sum(expo, axis=-1, keepdims=True)
+            halves.append(dot(probs.astype(jnp.bfloat16), values))
+        ctx[:, cols] = jnp.where(left, halves[0], halves[1]).astype(jnp.bfloat16)
+
+    pl.loop(0, width // 256)(pair)
+    far(1, 0)
+    far(1, 1)
+    for d in range(2, depth):
+        forward(1, d)
+    pl.loop(width // 256, width // 128)(pair)
+    for d in range(2, depth):
+        far(1, d)
+    finish(1)
+    keep_out = pltpu.make_async_copy(
+        wfull.at[pl.ds(3, 1)], w_out.at[pl.ds(3, 1)], local_sem.at[3]
+    )
+    keep_out.start()
+
+    @pl.loop(0, tiles)
+    def _(i):
+        cols = pl.ds(pl.multiple_of(i * 256, 256), 256)
+        value = tok[:, cols].astype(jnp.float32) + dot(ctx[...], wfull[3, :, cols])
+        resid[:, cols] = value
+        sent[:, cols] = value.astype(jnp.bfloat16)
+
+    for copy in placed_z + cot_z:
+        copy.wait_recv()
+    wire.drain()
+    keep.wait()
+    keep_out.wait()
+
+
+def attend(depth, cap, tokens, w_own, norm_own, routes, cotangent):
+    count, width = tokens.shape
+    bf = jnp.bfloat16
+    copies = 128
+    return pl.pallas_call(
+        functools.partial(attend_kernel, depth, cap),
+        out_shape=(
+            jax.ShapeDtypeStruct((4, width, width), bf),
+            jax.ShapeDtypeStruct((3, count, width), bf),
+            jax.ShapeDtypeStruct((count, width), bf),
+            jax.ShapeDtypeStruct((count, width), bf),
+            jax.ShapeDtypeStruct((count, width), jnp.float32),
+            jax.ShapeDtypeStruct((count, width), bf),
+            jax.ShapeDtypeStruct((depth, 8, 256), jnp.int32),
+            jax.ShapeDtypeStruct((16, width), bf),
+            jax.ShapeDtypeStruct((depth, count, width), bf),
+        ),
+        in_specs=[VMEM_SPEC] * 5,
+        out_specs=(ANY_SPEC,) + (VMEM_SPEC,) * 8,
+        scratch_shapes=[
+            pltpu.VMEM((4, width, width), bf),
+            pltpu.VMEM((depth + 2, 16, width), bf),
+            pltpu.VMEM((3, 16, width), bf),
+            pltpu.SemaphoreType.DMA((copies,)),
+            pltpu.SemaphoreType.DMA((copies,)),
+            pltpu.SemaphoreType.DMA((4,)),
+        ],
+        compiler_params=pltpu.CompilerParams(
+            collective_id=0, has_side_effects=True, vmem_limit_bytes=40 << 20
+        ),
+    )(tokens, w_own, norm_own, routes, cotangent)
+
+
+def pick(placed_row, slots):
+    which = lax.broadcasted_iota(jnp.int32, (slots, placed_row.shape[1]), 0)
+    return jnp.where(which == placed_row, 1.0, 0.0).astype(jnp.bfloat16)
+
+
+def gelu_pair(v):
+    cdf = 0.5 + 0.5 * lax.erf(v * (0.5**0.5))
+    pdf = jnp.exp(-0.5 * v * v) * ((2.0 * math.pi) ** -0.5)
+    return v * cdf, cdf + v * pdf
+
+
+def fold(v):
+    total = v[0:8]
+    for i in range(8, v.shape[0], 8):
+        total = total + v[i : i + 8]
+    return total
+
+
+def spread(column, lanes):
+    return jnp.concatenate([column] * (lanes // 128), axis=1)
+
+
+def expert_kernel(
+    depth,
+    cap,
+    sent,
+    placed,
+    cot_raw,
+    up,
+    down,
+    vec,
+    d_sum,
+    g_up,
+    g_down,
+    delta,
+    vec_part,
+    scal,
+    raw,
+    stage,
+    rows,
+    cots,
+    xn,
+    act,
+    slope,
+    d_slots,
+    back,
+    part,
+    z_in,
+    d_xn,
+    gate,
+    d_logit,
+    g_stage,
+    send_sem,
+    recv_sem,
+    local_sem,
+):
+    at = Place(depth)
+    e, z = at.e, at.z
+    count, width = sent.shape
+    planes = 8
+    slots = planes * cap
+    units = up.shape[1]
+    meet(
+        [(e, at.up(d)) for d in range(1, depth)]
+        + [(at.across(k), z) for k in range(1, planes)]
+    )
+    wire = Wire(send_sem, recv_sem)
+    vec_part[...] = jnp.zeros_like(vec_part)
+    scal[...] = jnp.zeros_like(scal)
+    centroid = lambda: vec[0:1, :]
+    raw_z = {d: wire.send(sent, raw.at[d - 1], (e, at.up(d))) for d in range(1, depth)}
+
+    def build(b, source):
+        onehot = pick(placed[b, 0:1, :count], slots)
+
+        @pl.loop(0, width // 512)
+        def _(i):
+            cols = pl.ds(pl.multiple_of(i * 512, 512), 512)
+            value = dot(onehot, source[:, cols]).astype(jnp.bfloat16)
+            for k in range(planes):
+                stage[b, k, :, cols] = value[k * cap : (k + 1) * cap]
+
+    def exchange(b, dst):
+        copies = [
+            wire.send(stage.at[b, at.across(k)], dst.at[b, k], (at.across(k), z))
+            for k in range(1, planes)
+        ]
+        dst[b, 0] = stage[b, e]
+        return copies
+
+    row_copies, cot_copies, ret_copies, part_copies = {}, {}, {}, {}
+
+    def rows_out(b):
+        if b:
+            raw_z[b].wait_recv()
+        build(b, sent if b == 0 else raw.at[b - 1])
+        row_copies[b] = exchange(b, rows)
+
+    def cots_out(b):
+        for copy in row_copies[b]:
+            wire.left(copy)
+        build(b, cot_raw.at[b])
+        cot_copies[b] = exchange(b, cots)
+
+    def forward(b):
+        for copy in row_copies[b]:
+            copy.wait_recv()
+        gain, bias = vec[1:2, :], vec[2:3, :]
+
+        @pl.loop(0, planes)
+        def _(i):
+            r = rows[b, i].astype(jnp.float32)
+            logit = jnp.sum(r * centroid(), axis=-1, keepdims=True)
+            g = jax.nn.sigmoid(logit)
+            wide = jnp.broadcast_to(g, (cap, 128))
+            gate[b, i] = wide
+            scal[0:8] += fold(wide)
+            average = jnp.mean(r, axis=-1, keepdims=True)
+            centred = r - average
+            variance = jnp.mean(centred * centred, axis=-1, keepdims=True)
+            xn[b, pl.ds(pl.multiple_of(i * cap, 16), cap), :] = (
+                centred * lax.rsqrt(variance + norm_eps) * gain + bias
+            ).astype(jnp.bfloat16)
+
+        @pl.loop(0, units // 256)
+        def _(j):
+            cols = pl.ds(pl.multiple_of(j * 256, 256), 256)
+            value, rate = gelu_pair(dot(xn[b], up[:, cols]))
+            act[b, :, cols] = value.astype(jnp.bfloat16)
+            slope[b, :, cols] = rate.astype(jnp.bfloat16)
+
+        @pl.loop(0, width // 256)
+        def _(j):
+            cols = pl.ds(pl.multiple_of(j * 256, 256), 256)
+            branch = dot(act[b], down[:, cols])
+            wide = spread(gate[b].reshape(slots, 128), 256)
+            value = (wide * branch).astype(jnp.bfloat16)
+            for k in range(planes):
+                delta[b, k, :, cols] = value[k * cap : (k + 1) * cap]
+
+    def backward(b):
+        for copy in cot_copies[b]:
+            copy.wait_recv()
+
+        @pl.loop(0, planes)
+        def _(i):
+            c = cots[b, i].astype(jnp.float32)
+            g = gate[b, i]
+            inner = jnp.sum(c * delta[b, i].astype(jnp.float32), axis=-1, keepdims=True)
+            dl = (1.0 - g) * inner
+            d_logit[b, i] = dl
+            cots[b, i] = (c * spread(g, width)).astype(jnp.bfloat16)
+            vec_part[0] += fold(rows[b, i].astype(jnp.float32) * spread(dl, width))
+
+        @pl.loop(0, units // 256)
+        def _(j):
+            cols = pl.ds(pl.multiple_of(j * 256, 256), 256)
+            d_act = dot(cots[b].reshape(slots, width), down[cols, :], 1, 1)
+            slope[b, :, cols] = (d_act * slope[b, :, cols].astype(jnp.float32)).astype(
+                jnp.bfloat16
+            )
+
+        @pl.loop(0, width // 256)
+        def _(j):
+            cols = pl.ds(pl.multiple_of(j * 256, 256), 256)
+            value = dot(slope[b], up[cols, :], 1, 1)
+            for k in range(planes):
+                d_xn[k, :, cols] = value[k * cap : (k + 1) * cap]
+
+        @pl.loop(0, planes)
+        def _(i):
+            r = rows[b, i].astype(jnp.float32)
+            average = jnp.mean(r, axis=-1, keepdims=True)
+            centred = r - average
+            variance = jnp.mean(centred * centred, axis=-1, keepdims=True)
+            scale = lax.rsqrt(variance + norm_eps)
+            hat = centred * scale
+            dx = d_xn[i]
+            vec_part[1] += fold(dx * hat)
+            vec_part[2] += fold(dx)
+            dh = dx * vec[1:2, :]
+            first = jnp.mean(dh, axis=-1, keepdims=True)
+            second = jnp.mean(dh * hat, axis=-1, keepdims=True)
+            d_in = scale * (dh - first - hat * second)
+            d_slots[b, i] = (d_in + spread(d_logit[b, i], width) * centroid()).astype(jnp.bfloat16)
+
+        ret_copies[b] = [
+            wire.send(d_slots.at[b, k], back.at[b, e], (at.across(k), z))
+            for k in range(1, planes)
+        ]
+        back[b, e] = d_slots[b, 0]
+
+    def collect(b):
+        for copy in ret_copies[b]:
+            copy.wait_recv()
+        onehot = pick(placed[b, 0:1, :count], slots)
+
+        @pl.loop(0, width // 256)
+        def _(j):
+            cols = pl.ds(pl.multiple_of(j * 256, 256), 256)
+            value = back[b, :, :, cols].reshape(slots, 256)
+            part[b, :, cols] = dot(onehot, value, 0, 0).astype(jnp.bfloat16)
+
+        if b:
+            part_copies[b] = wire.send(part.at[b], z_in.at[b - 1], (e, at.down(b)))
+
+    def weight_grad(lhs, rhs, index, out):
+        @pl.loop(0, lhs.shape[-1] // 256)
+        def _(j):
+            cols = pl.ds(pl.multiple_of(j * 256, 256), 256)
+            left = lhs[:, :, cols].reshape(depth * slots, 256)
+            value = dot(left, rhs[...].reshape(depth * slots, rhs.shape[-1]), 0, 0)
+            scal[8:16] += fold(square_lanes(value))
+            g_stage[index, cols, :] = value.astype(jnp.bfloat16)
+
+        copy = pltpu.make_async_copy(g_stage.at[index], out, local_sem.at[index])
+        copy.start()
+        return copy
+
+    rows_out(0)
+    for b in range(1, depth):
+        rows_out(b)
+        forward(b - 1)
+    order = list(range(1, depth)) + [0]
+    cots_out(order[0])
+    cots_out(order[1])
+    forward(depth - 1)
+    for b in order[2:]:
+        cots_out(b)
+    backward(order[0])
+    for i in range(1, depth):
+        backward(order[i])
+        collect(order[i - 1])
+    keep_down = weight_grad(act, cots, 0, g_down)
+    collect(order[-1])
+    keep_up = weight_grad(xn, slope, 1, g_up)
+    for b in range(1, depth):
+        part_copies[b].wait_recv()
+
+    @pl.loop(0, width // 256)
+    def _(j):
+        cols = pl.ds(pl.multiple_of(j * 256, 256), 256)
+        total = part[0, :, cols].astype(jnp.float32)
+        for b in range(1, depth):
+            total = total + z_in[b - 1, :, cols].astype(jnp.float32)
+        d_sum[:, cols] = total
+
+    wire.drain()
+    keep_down.wait()
+    keep_up.wait()
+
+
+def square_lanes(v):
+    total = v[:, 0:128] * v[:, 0:128]
+    for i in range(128, v.shape[1], 128):
+        total = total + v[:, i : i + 128] * v[:, i : i + 128]
+    return total
+
+
+def expert_layer(depth, cap, sent, placed, cot_raw, up, down, vec):
+    count, width = sent.shape
+    units = up.shape[1]
+    bf, full = jnp.bfloat16, jnp.float32
+    slots = 8 * cap
+    copies = 3 * 7 * depth + 2 * depth
+    return pl.pallas_call(
+        functools.partial(expert_kernel, depth, cap),
+        out_shape=(
+            jax.ShapeDtypeStruct((count, width), full),
+            jax.ShapeDtypeStruct((width, units), bf),
+            jax.ShapeDtypeStruct((units, width), bf),
+            jax.ShapeDtypeStruct((depth, 8, cap, width), bf),
+            jax.ShapeDtypeStruct((3, 8, width), full),
+            jax.ShapeDtypeStruct((16, 128), full),
+        ),
+        in_specs=[VMEM_SPEC] * 6,
+        out_specs=(VMEM_SPEC, ANY_SPEC, ANY_SPEC) + (VMEM_SPEC,) * 3,
+        scratch_shapes=[
+            pltpu.VMEM((depth - 1, count, width), bf),
+            pltpu.VMEM((depth, 8, cap, width), bf),
+            pltpu.VMEM((depth, 8, cap, width), bf),
+            pltpu.VMEM((depth, 8, cap, width), bf),
+            pltpu.VMEM((depth, slots, width), bf),
+            pltpu.VMEM((depth, slots, units), bf),
+            pltpu.VMEM((depth, slots, units), bf),
+            pltpu.VMEM((depth, 8, cap, width), bf),
+            pltpu.VMEM((depth, 8, cap, width), bf),
+            pltpu.VMEM((depth, count, width), bf),
+            pltpu.VMEM((depth - 1, count, width), bf),
+            pltpu.VMEM((8, cap, width), full),
+            pltpu.VMEM((depth, 8, cap, 128), full),
+            pltpu.VMEM((depth, 8, cap, 128), full),
+            pltpu.VMEM((2, max(width, units), max(width, units)), bf),
+            pltpu.SemaphoreType.DMA((copies,)),
+            pltpu.SemaphoreType.DMA((copies,)),
+            pltpu.SemaphoreType.DMA((2,)),
+        ],
+        compiler_params=pltpu.CompilerParams(
+            collective_id=1, has_side_effects=True, vmem_limit_bytes=62 << 20
+        ),
+    )(sent, placed, cot_raw, up, down, vec)
+
+
+def reduce_kernel(
+    depth,
+    cap,
+    d_sum,
+    cot,
+    w_in,
+    qkv,
+    normed,
+    ctx,
+    tok,
+    gains,
+    placed,
+    delta,
+    resid,
+    vec_part,
+    scal,
+    block_out,
+    token_grad,
+    shard_out,
+    norm_out,
+    vec_out,
+    square_out,
+    wfull,
+    d_resid,
+    d_proj,
+    d_ctx,
+    d_qkv,
+    d_norm,
+    stage,
+    twin_in,
+    x_in,
+    y_in,
+    x_last,
+    y_last,
+    done,
+    z_last,
+    back,
+    part,
+    z_in,
+    small,
+    small_in,
+    small_z,
+    square,
+    square_z,
+    send_sem,
+    recv_sem,
+    local_sem,
+):
+    at = Place(depth)
+    e, z = at.e, at.z
+    count, width = tok.shape
+    planes = 8
+    slots = planes * cap
+    shard = shard_out.shape[1]
+    column = depth * shard
+    half = column // 2
+    meet(
+        [(e, at.up(d)) for d in range(1, depth)]
+        + [(at.across(k), z) for k in range(1, planes)]
+    )
+    wire = Wire(send_sem, recv_sem)
+    loads = []
+    for m in (3, 2, 1, 0):
+        copy = pltpu.make_async_copy(w_in.at[m], wfull.at[m], local_sem.at[m])
+        copy.start()
+        loads.append(copy)
+    ret, order = {}, list(range(1, depth)) + [0]
+    for b in order:
+        ret[b] = [
+            wire.send(delta.at[b, k], back.at[b, e], (at.across(k), z)) for k in range(1, planes)
+        ]
+        back[b, e] = delta[b, 0]
+    part_copies = {}
+
+    def collect(b):
+        for copy in ret[b]:
+            copy.wait_recv()
+        onehot = pick(placed[b, 0:1, :count], slots)
+
+        @pl.loop(0, width // 256)
+        def _(j):
+            cols = pl.ds(pl.multiple_of(j * 256, 256), 256)
+            value = back[b, :, :, cols].reshape(slots, 256)
+            part[b, :, cols] = dot(onehot, value, 0, 0).astype(jnp.bfloat16)
+
+        if b:
+            part_copies[b] = wire.send(part.at[b], z_in.at[b - 1], (e, at.down(b)))
+
+    def weight_grad(m, left_ref, right):
+        @pl.loop(0, planes)
+        def _(i):
+            cols = pl.ds(pl.multiple_of(i * column, column), column)
+            value = dot(left_ref[:, cols], right[...], 0, 0).astype(jnp.bfloat16)
+            stage[m, lax.div(i, 4), lax.rem(lax.div(i, 2), 2), lax.rem(i, 2)] = value
+
+    other = 1 - at.core
+    first, second, third, fourth = {}, {}, {}, {}
+
+    def to_core(m):
+        first[m] = wire.send(stage.at[m, :, :, other], twin_in.at[m], (at.twin(), z))
+
+    def to_plane(m):
+        first[m].wait_recv()
+        for j in range(2):
+            for i in range(2):
+                twin_in[m, j, i] = twin_in[m, j, i] + stage[m, j, i, at.core]
+        second[m] = (
+            wire.send(twin_in.at[m, :, 1 - at.x, pl.ds(0, half)], x_in.at[m], (at.ex, z)),
+            wire.send(twin_in.at[m, 1 - at.y, :, pl.ds(half, half)], y_in.at[m], (at.ey, z)),
+        )
+
+    def to_last(m):
+        second[m][0].wait_recv()
+        for j in range(2):
+            x_in[m, j] = x_in[m, j] + twin_in[m, j, at.x, 0:half]
+        one = wire.send(x_in.at[m, 1 - at.y], x_last.at[m], (at.ey, z))
+        second[m][1].wait_recv()
+        for i in range(2):
+            y_in[m, i] = y_in[m, i] + twin_in[m, at.y, i, half:]
+        two = wire.send(y_in.at[m, 1 - at.x], y_last.at[m], (at.ex, z))
+        third[m] = (one, two)
+
+    def to_owner(m):
+        third[m][0].wait_recv()
+        done[m, 0:half] = x_in[m, at.y] + x_last[m]
+        third[m][1].wait_recv()
+        done[m, half:] = y_in[m, at.x] + y_last[m]
+        fourth[m] = [
+            wire.send(
+                done.at[m, pl.ds(pl.multiple_of(at.up(d) * shard, shard), shard)],
+                z_last.at[m, d - 1],
+                (e, at.up(d)),
+            )
+            for d in range(1, depth)
+        ]
+
+    def own(m):
+        total = done[m, pl.ds(pl.multiple_of(z * shard, shard), shard), :].astype(jnp.float32)
+        for d in range(1, depth):
+            fourth[m][d - 1].wait_recv()
+            total = total + z_last[m, d - 1].astype(jnp.float32)
+        shard_out[m] = total
+
+    value = cot[...].astype(jnp.float32) + d_sum[...]
+    d_resid[...] = value
+    d_proj[...] = value.astype(jnp.bfloat16)
+    weight_grad(3, ctx, d_proj)
+    to_core(3)
+    loads[0].wait()
+
+    @pl.loop(0, width // 256)
+    def _(j):
+        cols = pl.ds(pl.multiple_of(j * 256, 256), 256)
+        d_ctx[:, cols] = dot(d_proj[...], wfull[3, cols, :], 1, 1).astype(jnp.bfloat16)
+
+    to_plane(3)
+    causal = lax.broadcasted_iota(jnp.int32, (count, count), 0) >= lax.broadcasted_iota(
+        jnp.int32, (count, count), 1
+    )
+    left = lax.broadcasted_iota(jnp.int32, (count, 128), 1) < 64
+    scaling = 64 ** (-0.5)
+
+    @pl.loop(0, width // 128)
+    def _(i):
+        cols = pl.ds(pl.multiple_of(i * 128, 128), 128)
+        query = qkv[0, :, cols]
+        keys = qkv[1, :, cols]
+        values = qkv[2, :, cols]
+        d_out = d_ctx[:, cols]
+        zero = jnp.zeros_like(query)
+        got = []
+        for side in range(2):
+            mask = left if side == 0 else jnp.logical_not(left)
+            q_side = jnp.where(mask, query, zero)
+            k_side = jnp.where(mask, keys, zero)
+            o_side = jnp.where(mask, d_out, zero)
+            scores = dot(q_side, keys, 1, 1) * scaling
+            scores = jnp.where(causal, scores, masked_fill)
+            top = jnp.max(scores, axis=-1, keepdims=True)
+            expo = jnp.exp(scores - top)
+            probs = expo / jnp.sum(expo, axis=-1, keepdims=True)
+            d_probs = dot(o_side, values, 1, 1)
+            inner = jnp.sum(d_probs * probs, axis=-1, keepdims=True)
+            d_scores = (probs * (d_probs - inner)).astype(jnp.bfloat16)
+            got.append(
+                (
+                    dot(d_scores, k_side),
+                    dot(d_scores, q_side, 0, 0),
+                    dot(probs.astype(jnp.bfloat16), o_side, 0, 0),
+                )
+            )
+        d_qkv[0, :, cols] = ((got[0][0] + got[1][0]) * scaling).astype(jnp.bfloat16)
+        d_qkv[1, :, cols] = ((got[0][1] + got[1][1]) * scaling).astype(jnp.bfloat16)
+        d_qkv[2, :, cols] = (got[0][2] + got[1][2]).astype(jnp.bfloat16)
+
+    for m in (2, 1, 0):
+        weight_grad(m, normed, d_qkv.at[m])
+        to_core(m)
+        if m < 2:
+            to_plane(m + 1)
+    to_last(3)
+    to_plane(0)
+    for copy in loads[1:]:
+        copy.wait()
+
+    @pl.loop(0, width // 256)
+    def _(j):
+        cols = pl.ds(pl.multiple_of(j * 256, 256), 256)
+        d_norm[:, cols] = (
+            dot(d_qkv[0], wfull[0, cols, :], 1, 1)
+            + dot(d_qkv[1], wfull[1, cols, :], 1, 1)
+            + dot(d_qkv[2], wfull[2, cols, :], 1, 1)
+        )
+
+    gain = gains[0:1, :].astype(jnp.float32)
+    d_gain = jnp.zeros((8, width), jnp.float32)
+    d_bias = jnp.zeros((8, width), jnp.float32)
+    for i in range(0, count, 64):
+        piece = tok[i : i + 64, :].astype(jnp.float32)
+        average = jnp.mean(piece, axis=-1, keepdims=True)
+        centred = piece - average
+        variance = jnp.mean(centred * centred, axis=-1, keepdims=True)
+        scale = lax.rsqrt(variance + norm_eps)
+        hat = centred * scale
+        dx = d_norm[i : i + 64, :]
+        d_gain = d_gain + fold(dx * hat)
+        d_bias = d_bias + fold(dx)
+        dh = dx * gain
+        mean_one = jnp.mean(dh, axis=-1, keepdims=True)
+        mean_two = jnp.mean(dh * hat, axis=-1, keepdims=True)
+        d_in = scale * (dh - mean_one - hat * mean_two)
+        token_grad[i : i + 64, :] = (d_resid[i : i + 64, :] + d_in).astype(jnp.bfloat16)
+    mine = small_z.at[z]
+    mine[...] = jnp.zeros((16, width), jnp.float32)
+    mine[2:3, :] = gains[2:3, :].astype(jnp.float32)
+    mine[0:1, :] = jnp.sum(d_gain, axis=0, keepdims=True)
+    mine[1:2, :] = jnp.sum(d_bias, axis=0, keepdims=True)
+    for k in range(3):
+        mine[8 + k : 9 + k, :] = jnp.sum(vec_part[k], axis=0, keepdims=True)
+    small_copies = [wire.send(mine, mine, (e, at.up(d))) for d in range(1, depth)]
+    to_owner(3)
+    for b in order[:2]:
+        collect(b)
+    to_last(2)
+    for copy in small_copies:
+        copy.wait_recv()
+    total = small_z[0]
+    for d in range(1, depth):
+        total = total + small_z[d]
+    small[0] = total[0:8]
+    vec_out[...] = total[8:16]
+    x_copy = wire.send(small.at[0], small_in.at[0], (at.ex, z))
+    own(3)
+    to_last(1)
+    to_owner(2)
+    x_copy.wait_recv()
+    small[1] = small[0] + small_in[0]
+    y_copy = wire.send(small.at[1], small_in.at[1], (at.ey, z))
+    for b in order[2:]:
+        collect(b)
+    own(2)
+    y_copy.wait_recv()
+    small[2] = small[1] + small_in[1]
+    core_copy = wire.send(small.at[2], small_in.at[2], (at.twin(), z))
+    to_last(0)
+    to_owner(1)
+    core_copy.wait_recv()
+    norm_out[...] = small[2] + small_in[2]
+    to_owner(0)
+    own(1)
+    for b in range(1, depth):
+        part_copies[b].wait_recv()
+
+    @pl.loop(0, width // 256)
+    def _(j):
+        cols = pl.ds(pl.multiple_of(j * 256, 256), 256)
+        total = part[0, :, cols].astype(jnp.float32)
+        for b in range(1, depth):
+            total = total + z_in[b - 1, :, cols].astype(jnp.float32)
+        block_out[:, cols] = (resid[:, cols] + total).astype(jnp.bfloat16)
+
+    norm_rows = norm_out[0:2, :]
+    vec_rows = vec_out[0:3, :]
+    squares = jnp.sum(norm_rows * norm_rows, axis=0, keepdims=True) / (planes * depth) + jnp.sum(
+        vec_rows * vec_rows, axis=0, keepdims=True
+    ) / depth
+    own(0)
+    local = scal[8:16, :]
+    for m in range(4):
+        local = local + fold(square_lanes(shard_out[m]))
+    lane_squares = squares[:, 0:128]
+    for i in range(128, width, 128):
+        lane_squares = lane_squares + squares[:, i : i + 128]
+    head = lax.broadcasted_iota(jnp.int32, (8, 128), 0) == 0
+    local = local + jnp.where(head, jnp.broadcast_to(lane_squares, (8, 128)), 0.0)
+    square[e] = local
+    spot = square.at[e]
+    copies = [wire.send(spot, spot, (at.across(k), z)) for k in range(1, planes)]
+    for copy in copies:
+        copy.wait_recv()
+    total = square[0]
+    for k in range(1, planes):
+        total = total + square[k]
+    square_z[z] = total
+    spot = square_z.at[z]
+    copies = [wire.send(spot, spot, (e, at.up(d))) for d in range(1, depth)]
+    for copy in copies:
+        copy.wait_recv()
+    total = square_z[0]
+    for d in range(1, depth):
+        total = total + square_z[d]
+    square_out[...] = total
+    wire.drain()
+
+
+def attend_back(depth, cap, shard, *args):
+    tokens = args[6]
+    count, width = tokens.shape
+    bf, full = jnp.bfloat16, jnp.float32
+    column = depth * shard
+    half = column // 2
+    copies = 7 * depth + depth + 32 + 16 + 16
+    return pl.pallas_call(
+        functools.partial(reduce_kernel, depth, cap),
+        out_shape=(
+            jax.ShapeDtypeStruct((count, width), bf),
+            jax.ShapeDtypeStruct((count, width), bf),
+            jax.ShapeDtypeStruct((4, shard, width), full),
+            jax.ShapeDtypeStruct((8, width), full),
+            jax.ShapeDtypeStruct((8, width), full),
+            jax.ShapeDtypeStruct((8, 128), full),
+        ),
+        in_specs=[VMEM_SPEC] * 2 + [ANY_SPEC] + [VMEM_SPEC] * 10,
+        out_specs=(VMEM_SPEC,) * 6,
+        scratch_shapes=[
+            pltpu.VMEM((4, width, width), bf),
+            pltpu.VMEM((count, width), full),
+            pltpu.VMEM((count, width), bf),
+            pltpu.VMEM((count, width), bf),
+            pltpu.VMEM((3, count, width), bf),
+            pltpu.VMEM((count, width), full),
+            pltpu.VMEM((4, 2, 2, 2, column, width), bf),
+            pltpu.VMEM((4, 2, 2, column, width), bf),
+            pltpu.VMEM((4, 2, half, width), bf),
+            pltpu.VMEM((4, 2, half, width), bf),
+            pltpu.VMEM((4, half, width), bf),
+            pltpu.VMEM((4, half, width), bf),
+            pltpu.VMEM((4, column, width), bf),
+            pltpu.VMEM((4, depth - 1, shard, width), bf),
+            pltpu.VMEM((depth, 8, cap, width), bf),
+            pltpu.VMEM((depth, count, width), bf),
+            pltpu.VMEM((depth - 1, count, width), bf),
+            pltpu.VMEM((3, 8, width), full),
+            pltpu.VMEM((3, 8, width), full),
+            pltpu.VMEM((depth, 16, width), full),
+            pltpu.VMEM((8, 8, 128), full),
+            pltpu.VMEM((depth, 8, 128), full),
+            pltpu.SemaphoreType.DMA((copies,)),
+            pltpu.SemaphoreType.DMA((copies,)),
+            pltpu.SemaphoreType.DMA((4,)),
+        ],
+        compiler_params=pltpu.CompilerParams(
+            collective_id=2, has_side_effects=True, vmem_limit_bytes=62 << 20
+        ),
+    )(*args)
 
 
 def shards(
@@ -59,8 +1065,8 @@
     vector_first,
     vector_second,
 ):
-    experts_here = lax.axis_size("expert")
-    hidden_size = lax.axis_size("hidden")
+    experts_here = lax.axis_size(EX)
+    hidden_size = lax.axis_size(HI)
     token_count = tokens.shape[0]
     features = tokens.shape[1]
     capacity = 2 * token_count // experts_here
@@ -70,8 +1076,8 @@
     attn_low = attn_weight.astype(jnp.bfloat16)
     norm_low = norm_param.astype(jnp.bfloat16)
     attn_full, norm_full = (
-        lax.all_gather(attn_low, ("expert", "hidden"), axis=1, tiled=True),
-        lax.all_gather(norm_low, ("expert", "hidden"), axis=1, tiled=True),
+        lax.all_gather(attn_low, BOTH, axis=1, tiled=True),
+        lax.all_gather(norm_low, BOTH, axis=1, tiled=True),
     )
     inputs = tokens.astype(jnp.float32)
     normed, norm_pull = jax.vjp(
@@ -118,22 +1124,22 @@
     arrived, arrived_mask = (
         lax.all_to_all(
             outgoing.reshape(experts_here, capacity, features),
-            "expert",
+            EX,
             split_axis=0,
             concat_axis=0,
             tiled=True,
         ),
         lax.all_to_all(
             occupied.reshape(experts_here, capacity),
-            "expert",
+            EX,
             split_axis=0,
             concat_axis=0,
             tiled=True,
         ),
     )
     gathered, gathered_mask = (
-        lax.all_gather(arrived, "hidden", axis=0, tiled=True),
-        lax.all_gather(arrived_mask, "hidden", axis=0, tiled=True),
+        lax.all_gather(arrived, HI, axis=0, tiled=True),
+        lax.all_gather(arrived_mask, HI, axis=0, tiled=True),
     )
     rows_all = gathered.reshape(-1, features)
     mask_all = gathered_mask.reshape(-1).astype(jnp.float32)
@@ -149,16 +1155,16 @@
     after_low = after.astype(jnp.bfloat16)
     branch_own = lax.psum_scatter(
         jnp.dot(after_low, down_weight[0], preferred_element_type=jnp.float32).astype(jnp.bfloat16),
-        "hidden",
+        HI,
         scatter_dimension=0,
         tiled=True,
     ).astype(jnp.float32)
-    own_start = lax.axis_index("hidden") * slot_rows
+    own_start = lax.axis_index(HI) * slot_rows
     gating_own = lax.dynamic_slice_in_dim(gating, own_start, slot_rows, 0)
     delta = (gating_own[:, None] * branch_own).astype(jnp.bfloat16)
     returned = lax.all_to_all(
         delta.reshape(experts_here, capacity, features),
-        "expert",
+        EX,
         split_axis=0,
         concat_axis=0,
         tiled=True,
@@ -178,12 +1184,12 @@
     cot_slots = jnp.dot(placing, cotangent, preferred_element_type=jnp.float32).astype(jnp.bfloat16)
     cot_arrived = lax.all_to_all(
         cot_slots.reshape(experts_here, capacity, features),
-        "expert",
+        EX,
         split_axis=0,
         concat_axis=0,
         tiled=True,
     )
-    cot_rows = lax.all_gather(cot_arrived, "hidden", axis=0, tiled=True).reshape(-1, features)
+    cot_rows = lax.all_gather(cot_arrived, HI, axis=0, tiled=True).reshape(-1, features)
     d_branch = (gating[:, None] * cot_rows.astype(jnp.float32)).astype(jnp.bfloat16)
     grad_down = jnp.einsum("gf,gd->fd", after_low, d_branch, preferred_element_type=jnp.float32)
     d_after = jnp.einsum("gd,fd->gf", d_branch, down_weight[0], preferred_element_type=jnp.float32)
@@ -194,7 +1200,7 @@
     )
     d_rows, d_expert_gain, d_expert_bias = expert_pull(d_expert_normed)
     d_rows_own = lax.psum_scatter(
-        d_rows.astype(jnp.bfloat16), "hidden", scatter_dimension=0, tiled=True
+        d_rows.astype(jnp.bfloat16), HI, scatter_dimension=0, tiled=True
     ).astype(jnp.float32)
     cot_own = lax.dynamic_slice_in_dim(cot_rows, own_start, slot_rows, 0).astype(jnp.float32)
     rows_own = lax.dynamic_slice_in_dim(rows_float, own_start, slot_rows, 0)
@@ -204,7 +1210,7 @@
     d_sent = (d_rows_own + d_logit[:, None] * centroid).astype(jnp.bfloat16)
     back_slots = lax.all_to_all(
         d_sent.reshape(experts_here, capacity, features),
-        "expert",
+        EX,
         split_axis=0,
         concat_axis=0,
         tiled=True,
@@ -215,7 +1221,7 @@
         back_slots.reshape(slot_rows, features),
         preferred_element_type=jnp.float32,
     )
-    vector_grad = lax.psum(jnp.stack([d_centroid, d_expert_gain, d_expert_bias])[None], "hidden")
+    vector_grad = lax.psum(jnp.stack([d_centroid, d_expert_gain, d_expert_bias])[None], HI)
     d_project = d_resid.astype(jnp.bfloat16)
     grad_out_proj = jnp.einsum("td,te->de", context, d_project, preferred_element_type=jnp.float32)
     d_context = jnp.einsum(
@@ -255,8 +1261,8 @@
     grad_attn = jnp.concatenate([grad_qkv, grad_out_proj[None]], axis=0)
     grad_norm_param = jnp.stack([d_norm_gain, d_norm_bias])
     attn_shard, norm_shard = (
-        lax.psum_scatter(grad_attn, ("expert", "hidden"), scatter_dimension=1, tiled=True),
-        lax.psum_scatter(grad_norm_param, ("expert", "hidden"), scatter_dimension=1, tiled=True),
+        lax.psum_scatter(grad_attn, BOTH, scatter_dimension=1, tiled=True),
+        lax.psum_scatter(grad_norm_param, BOTH, scatter_dimension=1, tiled=True),
     )
     local_square = (
         jnp.sum(attn_shard * attn_shard)
@@ -265,7 +1271,7 @@
         + jnp.sum(grad_down * grad_down)
         + jnp.sum(vector_grad * vector_grad) / hidden_size
     )
-    grad_norm = jnp.sqrt(lax.psum(local_square, ("expert", "hidden")))
+    grad_norm = jnp.sqrt(lax.psum(local_square, BOTH))
     clip_factor = clip_level / jnp.maximum(grad_norm, clip_level)
     attn_new = adam_step(
         attn_weight, attn_first, attn_second, attn_shard, clip_factor, rate_matrix, decay_rate
@@ -317,50 +1323,160 @@
     )
 
 
+def fast_shards(
+    tokens,
+    cotangent,
+    routes,
+    attn_weight,
+    attn_first,
+    attn_second,
+    norm_param,
+    norm_first,
+    norm_second,
+    up_weight,
+    up_first,
+    up_second,
+    down_weight,
+    down_first,
+    down_second,
+    expert_vector,
+    vector_first,
+    vector_second,
+):
+    experts = lax.axis_size(EX)
+    depth = lax.axis_size(HI)
+    count, width = tokens.shape
+    cap = 2 * count // experts
+    shard = attn_weight.shape[1]
+    lanes = norm_param.shape[1]
+    place = lax.axis_index(EX) * depth + lax.axis_index(HI)
+    owner = jnp.arange(width, dtype=jnp.int32) // lanes
+    norm_own = jnp.where(owner[None] == place, jnp.tile(norm_param, (8, width // lanes)), 0.0)
+    w_full, qkv, normed, ctx, resid, sent, placed, gains, cot_raw = attend(
+        depth,
+        cap,
+        tokens,
+        attn_weight.astype(jnp.bfloat16),
+        norm_own.astype(jnp.bfloat16),
+        routes,
+        cotangent,
+    )
+    vec = jnp.pad(expert_vector[0], ((0, 5), (0, 0)))
+    d_sum, grad_up, grad_down, delta, vec_part, scal = expert_layer(
+        depth, cap, sent, placed, cot_raw, up_weight[0], down_weight[0], vec
+    )
+    block_out, token_grad, attn_shard, norm_grads, vec_grads, squares = attend_back(
+        depth,
+        cap,
+        shard,
+        d_sum,
+        cotangent,
+        w_full,
+        qkv,
+        normed,
+        ctx,
+        tokens,
+        gains,
+        placed,
+        delta,
+        resid,
+        vec_part,
+        scal,
+    )
+    here = lax.axis_index(EX)
+    routed = lax.dynamic_slice(norm_grads, (2, here), (1, 1))[0, 0]
+    empty = depth * experts * cap - routed
+    gate_total = jnp.sum(scal[0:8, 0]) - 0.5 * empty
+    expert_stats = jnp.stack([routed / (count * depth), gate_total / routed])[:, None]
+    norm_shard = lax.dynamic_slice(norm_grads, (0, place * lanes), (2, lanes))
+    vector_grad = vec_grads[None, 0:3]
+    grad_norm = jnp.sqrt(jnp.sum(squares))
+    clip_factor = clip_level / jnp.maximum(grad_norm, clip_level)
+    attn_new = adam_step(
+        attn_weight, attn_first, attn_second, attn_shard, clip_factor, rate_matrix, decay_rate
+    )
+    norm_new = adam_step(
+        norm_param, norm_first, norm_second, norm_shard, clip_factor, rate_vector, 0.0
+    )
+    up_new = adam_step(
+        up_weight.astype(jnp.float32),
+        up_first,
+        up_second,
+        grad_up[None].astype(jnp.float32),
+        clip_factor,
+        rate_matrix,
+        decay_rate,
+    )
+    down_new = adam_step(
+        down_weight.astype(jnp.float32),
+        down_first,
+        down_second,
+        grad_down[None].astype(jnp.float32),
+        clip_factor,
+        rate_matrix,
+        decay_rate,
+    )
+    vector_new = adam_step(
+        expert_vector, vector_first, vector_second, vector_grad, clip_factor, rate_vector, 0.0
+    )
+    return (
+        block_out,
+        token_grad,
+        grad_norm,
+        *attn_new,
+        *norm_new,
+        *up_new,
+        *down_new,
+        *vector_new,
+        expert_stats,
+    )
+
+
 def solution(mesh):
+    small = mesh.shape[EX] == 8 and mesh.shape[HI] == 4
     return jax.shard_map(
-        shards,
+        fast_shards if small else shards,
         mesh=mesh,
         in_specs=(
-            P(("expert", "hidden"), None),
-            P(("expert", "hidden"), None),
-            P(("expert", "hidden"), None),
-            P(None, ("expert", "hidden"), None),
-            P(None, ("expert", "hidden"), None),
-            P(None, ("expert", "hidden"), None),
-            P(None, ("expert", "hidden")),
-            P(None, ("expert", "hidden")),
-            P(None, ("expert", "hidden")),
-            P("expert", None, "hidden"),
-            P("expert", None, "hidden"),
-            P("expert", None, "hidden"),
-            P("expert", "hidden", None),
-            P("expert", "hidden", None),
-            P("expert", "hidden", None),
-            P("expert", None, None),
-            P("expert", None, None),
-            P("expert", None, None),
+            P(BOTH, None),
+            P(BOTH, None),
+            P(BOTH, None),
+            P(None, BOTH, None),
+            P(None, BOTH, None),
+            P(None, BOTH, None),
+            P(None, BOTH),
+            P(None, BOTH),
+            P(None, BOTH),
+            P(EX, None, HI),
+            P(EX, None, HI),
+            P(EX, None, HI),
+            P(EX, HI, None),
+            P(EX, HI, None),
+            P(EX, HI, None),
+            P(EX, None, None),
+            P(EX, None, None),
+            P(EX, None, None),
         ),
         out_specs=(
-            P(("expert", "hidden"), None),
-            P(("expert", "hidden"), None),
+            P(BOTH, None),
+            P(BOTH, None),
             P(),
-            P(None, ("expert", "hidden"), None),
-            P(None, ("expert", "hidden"), None),
-            P(None, ("expert", "hidden"), None),
-            P(None, ("expert", "hidden")),
-            P(None, ("expert", "hidden")),
-            P(None, ("expert", "hidden")),
-            P("expert", None, "hidden"),
-            P("expert", None, "hidden"),
-            P("expert", None, "hidden"),
-            P("expert", "hidden", None),
-            P("expert", "hidden", None),
-            P("expert", "hidden", None),
-            P("expert", None, None),
-            P("expert", None, None),
-            P("expert", None, None),
-            P(None, "expert"),
+            P(None, BOTH, None),
+            P(None, BOTH, None),
+            P(None, BOTH, None),
+            P(None, BOTH),
+            P(None, BOTH),
+            P(None, BOTH),
+            P(EX, None, HI),
+            P(EX, None, HI),
+            P(EX, None, HI),
+            P(EX, HI, None),
+            P(EX, HI, None),
+            P(EX, HI, None),
+            P(EX, None, None),
+            P(EX, None, None),
+            P(EX, None, None),
+            P(None, EX),
         ),
         check_vma=False,
     )

time: 924 us -> 412 us (0.45)
  waiting for transfers between devices: 508 us -> 0 us
  Pallas kernels: 0 us -> 363 us
  blocking collectives: 164 us -> 0 us
  matrix products: 89.8 us -> 0 us
  other arithmetic: 77.8 us -> 23.9 us
  local copies, waits for them, and re-layouts: 41.6 us -> 19.4 us
  between operations: 22.4 us -> 5.42 us
  starting transfers between devices: 13.1 us -> 0 us
    pallas_call x0 -> x3, Pallas kernels: none -> 363 us  [the longest x1 159 us: expert_layer(): pl.pallas_call(functools.partial(expert_kernel, depth, cap), out_shape=(j...]
    unnamed x9 -> x0, waiting for transfers between devices: 336 us -> none
    reduce_scatter x2 -> x0, waiting for transfers between devices: 94.7 us -> none  [the longest x1 60.6 us: shards(): lax.psum_scatter(d_rows.astype(jnp.bfloat16), 'hidden', scatter_dimension...]
    dot_general x22 -> x0, matrix products: 89.8 us -> none  [the longest x1 18 us: shards(): jnp.dot(expert_low, up_weight[0], preferred_element_type=jnp.float32)]
    all_gather x2 -> x0, blocking collectives: 82.6 us -> none  [the longest x1 69.7 us: shards(): lax.all_gather(norm_low, ('expert', 'hidden'), axis=1, tiled=True)]
    psum x2 -> x0, blocking collectives: 57.8 us -> none  [the longest x1 40.4 us: shards(): grad_norm = jnp.sqrt(lax.psum(local_square, ('expert', 'hidden')))]
    all_gather x3 -> x0, waiting for transfers between devices: 53.4 us -> none  [the longest x1 41.7 us: shards(): lax.all_gather(arrived, 'hidden', axis=0, tiled=True)]
    all_to_all x2 -> x0, blocking collectives: 23.9 us -> none  [the longest x1 15.7 us: shards(): lax.all_to_all(outgoing.reshape(experts_here, capacity, features), 'exper...]
  transfers between devices with their start and end apart: 10 -> 0, of which waited for: 9 -> 0; matrix products, arithmetic and copies ran while one was open for 14% -> 0% of each run, Pallas kernels for 0% -> 0%
where the time goes in v1:
time: 412 us; the launch traced here: 411 us
  Pallas kernels  363 us (88%)
  other arithmetic  23.9 us (6%)
  local copies, waits for them, and re-layouts  19.4 us (5%)
  between operations  5.42 us (1%)
    pallas_call x1, Pallas kernels, expert_layer(): pl.pallas_call(functools.partial(expert_kernel, depth, cap), out_shape=(j...  159 us
    pallas_call x1, Pallas kernels, attend_back(): pl.pallas_call(functools.partial(reduce_kernel, depth, cap), out_shape=(j...  136 us
    pallas_call x1, Pallas kernels, attend(): pl.pallas_call(functools.partial(attend_kernel, depth, cap), out_shape=(j...  68.1 us
    sub x4, other arithmetic, adam_step(): return (weight - rate * update, moment, square)  20.3 us
    unnamed x57, local copies, waits for them, and re-layouts  16.7 us

profile of v1, /device:TPU:0, one launch (start us, length us, event | category | flops | bytes accessed | tf_op | source)
XLA Modules:
  0.0 411.3 jit_solution(13503541490705245727)
XLA Ops:
  0.7 0.7 tile.4
  1.4 0.2 tile.10
  1.6 1.1 convert_element_type.22.w_own
  2.7 0.8 copy.37.route
  3.5 1.0 copy-done.2
  4.5 1.0 copy-done.3
  5.4 68.1 %shard_map.321 = (bf16[4,1024,1024]{2,1,0:T(8,128)(2,1)S(1)}, bf16[3,192,1024]{2,1,0:T(8,128)(2,1)S(1)}, bf16[192,1024]{1,0:T(8,128)(2,1)S(1)}, bf16[192,1024]{1...) custom-call(bf16[192,1024]{1,0:T(8,128)(2,1)S(1)} %copy-done.2, ...), custom_call_target="tpu_custom_call" | custom-call | tf_op jit(solution)/shard_map/pallas_call | solution.py:349
  73.6 3.3 copy-done
  76.8 1.1 copy-done.1
  78.0 1.0 copy-done.4
  79.0 0.9 copy-done.5
  79.9 0.7 copy-done.6
  80.6 0.7 copy-done.7
  81.4 0.7 copy-done.8
  82.1 0.6 copy-done.9
  82.7 0.6 copy-done.10
  83.3 0.7 copy.63
  84.1 0.6 pad.4.vec
  84.7 158.8 %shard_map.322 = (f32[192,1024]{1,0:T(8,128)}, bf16[1024,1024]{1,0:T(8,128)(2,1)}, bf16[1024,1024]{1,0:T(8,128)(2,1)}, bf16[4,8,48,1024]{3,2,1,0:T(8,128)(2,1)},...) custom-call(bf16[192,1024]{1,0:T(8,128)(2,1)} %copy-done.6, s32[4,8,256]{2,1,0:T(8,128)} %copy-done.9, ...), custom_call_target="tpu_custom_call" | custom-call | tf_op jit(solution)/shard_map/pallas_call | solution.py:643
  243.5 135.7 %shard_map.323 = (bf16[192,1024]{1,0:T(8,128)(2,1)}, bf16[192,1024]{1,0:T(8,128)(2,1)}, f32[4,32,1024]{2,1,0:T(8,128)}, f32[8,1024]{1,0:T(8,128)}, f32[8,1024]{1,0:T(8,128)}, /*index=5*/f32[8,128]{1,0:T(8,128)}) custom-call(f32[192,1024]{1,0:T(8,128)} %get-tuple-element.43.d_sum, bf16[192,1024]{1,0:T(8,128)(2,1)} %cot.3, bf16[4,1024,1024]{2,1,0:T(8,128)(2,1)} %copy-done, ...), custom_call_target="tpu_custom_call" | custom-call | tf_op jit(solution)/shard_map/pallas_call | solution.py:1003
  379.1 1.3 constant_dynamic-slice_fusion
  381.1 0.6 slice_reduce_fusion
  383.6 0.6 maximum_bitcast_fusion
  384.2 1.3 reduce_sum.18
  386.4 17.5 %convert_subtract_fusion = (f32[1,1024,1024]{2,1,0:T(8,128)}, f32[1,1024,1024]{2,1,0:T(8,128)}, f32[1,1024,1024]{2,1,0:T(8,128)}, f32[1,1024,1024]{2,1,0:T(8,128...) fusion(bf16[1,1024,1024]{2,1,0:T(8,128)(2,1)} %param.30, f32[]{:T(128)S(6)} %div.82, ...), kind=kLoop, calls=%fused_computation.2 | loop fusion | flops 37748736 | bytes 50331652 | tf_op jit(solution)/shard_map/sub | solution.py:46
  404.0 0.6 copy.42
  404.6 0.6 copy.43
  405.3 0.6 copy.44
  405.9 1.3 multiply_subtract_fusion.1
  407.2 1.4 multiply_subtract_fusion
  408.6 0.7 copy.66
  409.4 0.7 copy.67
  (42 shorter events, 0.2 us)
Async XLA Ops:
  3.4 1.0 copy-start.2
  4.5 1.0 copy-start.3
  73.6 3.3 copy-start
  76.8 1.1 copy-start.1
  78.0 1.0 copy-start.4
  79.0 0.9 copy-start.5
  79.9 0.7 copy-start.6
  80.6 0.7 copy-start.7
  81.4 0.7 copy-start.8
  82.1 0.6 copy-start.9
  82.7 0.6 copy-start.10
  243.5 137.6 %copy-start.18 = (f32[16,128]{1,0:T(8,128)S(1)}, f32[16,128]{1,0:T(8,128)}, u32[]{:S(2)}) copy-start(f32[16,128]{1,0:T(8,128)} %get-tuple-element.52.scal) | copy-start | bytes 24580
  386.3 17.7 %copy-start.17 = (f32[1,3,1024]{2,0,1:T(1,128)S(1)}, f32[1,3,1024]{2,0,1:T(1,128)}, u32[]{:S(2)}) copy-start(f32[1,3,1024]{2,0,1:T(1,128)} %param.33) | copy-start | bytes 36868
  386.3 17.7 %copy-start.19 = (f32[1,3,1024]{2,0,1:T(1,128)S(1)}, f32[1,3,1024]{2,0,1:T(1,128)}, u32[]{:S(2)}) copy-start(f32[1,3,1024]{2,0,1:T(1,128)} %param.34) | copy-start | bytes 36868
  386.3 17.7 %copy-start.20 = (f32[1,3,1024]{2,0,1:T(1,128)S(1)}, f32[1,3,1024]{2,0,1:T(1,128)}, u32[]{:S(2)}) copy-start(f32[1,3,1024]{2,0,1:T(1,128)} %param.35) | copy-start | bytes 36868
  386.3 17.7 %copy-start.21 = (f32[8,1024]{1,0:T(8,128)S(1)}, f32[8,1024]{1,0:T(8,128)}, u32[]{:S(2)}) copy-start(f32[8,1024]{1,0:T(8,128)} %get-tuple-element.60) | copy-start | bytes 98308
  386.3 19.6 %copy-start.22 = (f32[2,32]{1,0:T(2,128)S(1)}, f32[2,32]{1,0:T(2,128)}, u32[]{:S(2)}) copy-start(f32[2,32]{1,0:T(2,128)} %param.24) | copy-start | bytes 772
  386.3 19.6 %copy-start.23 = (f32[2,32]{1,0:T(2,128)S(1)}, f32[2,32]{1,0:T(2,128)}, u32[]{:S(2)}) copy-start(f32[2,32]{1,0:T(2,128)} %param.25) | copy-start | bytes 772
  386.3 19.5 %copy-start.24 = (f32[2,32]{1,0:T(2,128)S(1)}, f32[2,32]{1,0:T(2,128)}, u32[]{:S(2)}) copy-start(f32[2,32]{1,0:T(2,128)} %param.26) | copy-start | bytes 772
  386.3 20.9 %copy-start.11 = (f32[4,32,1024]{2,1,0:T(8,128)S(1)}, f32[4,32,1024]{2,1,0:T(8,128)}, u32[]{:S(2)}) copy-start(f32[4,32,1024]{2,1,0:T(8,128)} %param.21) | copy-start | bytes 1572868
  386.3 20.9 %copy-start.12 = (f32[4,32,1024]{2,1,0:T(8,128)S(1)}, f32[4,32,1024]{2,1,0:T(8,128)}, u32[]{:S(2)}) copy-start(f32[4,32,1024]{2,1,0:T(8,128)} %param.22) | copy-start | bytes 1572868
  386.4 20.9 %copy-start.13 = (f32[4,32,1024]{2,1,0:T(8,128)S(1)}, f32[4,32,1024]{2,1,0:T(8,128)}, u32[]{:S(2)}) copy-start(f32[4,32,1024]{2,1,0:T(8,128)} %param.23) | copy-start | bytes 1572868
  386.4 20.8 %copy-start.14 = (f32[4,32,1024]{2,1,0:T(8,128)S(1)}, f32[4,32,1024]{2,1,0:T(8,128)}, u32[]{:S(2)}) copy-start(f32[4,32,1024]{2,1,0:T(8,128)} %get-tuple-element.56) | copy-start | bytes 1572868
  386.4 22.3 %copy-start.16 = (bf16[192,1024]{1,0:T(8,128)(2,1)S(1)}, bf16[192,1024]{1,0:T(8,128)(2,1)}, u32[]{:S(2)}) copy-start(bf16[192,1024]{1,0:T(8,128)(2,1)} %get-tuple-element.117) | copy-start | bytes 1179652
  403.9 5.5 %copy-start.15 = (bf16[192,1024]{1,0:T(8,128)(2,1)S(1)}, bf16[192,1024]{1,0:T(8,128)(2,1)}, u32[]{:S(2)}) copy-start(bf16[192,1024]{1,0:T(8,128)(2,1)} %get-tuple-element.118) | copy-start | bytes 1179652

commit v2 on v1

v2 whole, which is shorter than its diff:
```python
import functools
import math

import jax
import jax.numpy as jnp
from jax import lax
from jax.experimental import pallas as pl
from jax.experimental.pallas import tpu as pltpu
from jax.sharding import PartitionSpec as P

HEADS = 16
STEP = 10


norm_eps = 1e-05
clip_level = 1.0
beta_one = 0.9
beta_two = 0.999
adam_eps = 1e-08
decay_rate = 0.1
rate_matrix = 0.05
rate_vector = 0.5
masked_fill = -1e30
EX, HI = "expert", "hidden"
BOTH = (EX, HI)


def layer_norm(inputs, gain_row, bias_row):
    average = jnp.mean(inputs, axis=-1, keepdims=True)
    centred = inputs - average
    variance = jnp.mean(centred * centred, axis=-1, keepdims=True)
    return centred * lax.rsqrt(variance + norm_eps) * gain_row + bias_row


def gelu_exact(values):
    return jax.nn.gelu(values, approximate=False)


def adam_step(weight, first, second, grad, clip_factor, rate, decay):
    clipped = grad * clip_factor
    moment = beta_one * first + (1.0 - beta_one) * clipped
    square = beta_two * second + (1.0 - beta_two) * clipped * clipped
    corr_one = 1.0 - beta_one**STEP
    corr_two = 1.0 - beta_two**STEP
    update = moment / corr_one / (jnp.sqrt(square / corr_two) + adam_eps) + decay * weight
    return (weight - rate * update, moment, square)


MESH = pl.DeviceIdType.MESH
VMEM_SPEC = pl.BlockSpec(memory_space=pltpu.VMEM)
ANY_SPEC = pl.BlockSpec(memory_space=pl.ANY)


class Place:
    def __init__(self):
        self.e = lax.axis_index(EX)
        self.z = lax.axis_index(HI)
        high, low = lax.div(self.z, 2), lax.rem(self.z, 2)
        self.middle = high + low == 1
        self.ends = jnp.logical_not(self.middle)
        self.line = [self.z, self.z + 1 - 2 * low, 2 - high, 3 - 3 * high]
        self.core = lax.rem(self.e, 2)
        self.x = lax.rem(lax.div(self.e, 2), 2)
        self.y = lax.div(self.e, 4)
        self.ex = self.e + 2 - 4 * self.x
        self.ey = self.e + 4 - 8 * self.y
        self.exy = self.ex + 4 - 8 * self.y
        self.twin = (self.e + 1 - 2 * self.core, self.z)
        self.over_x = (self.ex, self.z)
        self.over_y = (self.ey, self.z)
        self.partner = (self.e, self.line[1])
        self.mirror = (self.e, 3 - self.z)
        self.mates = [None, self.partner, (self.e, self.z + 2 - 4 * high), self.mirror]

    def across(self, k):
        c = lax.rem(self.core + k % 2, 2)
        x = lax.rem(self.x + (k // 2) % 2, 2)
        y = lax.rem(self.y + k // 4, 2)
        return 4 * y + 2 * x + c

    def everyone(self):
        plane = [(self.across(k), self.z) for k in range(1, 8)]
        return plane + self.mates[1:]

    def meet(self):
        barrier = pltpu.get_barrier_semaphore()
        for device in self.everyone():
            pl.semaphore_signal(barrier, inc=1, device_id=device, device_id_type=MESH)
        pl.semaphore_wait(barrier, len(self.everyone()))


class Wire:
    def __init__(self, send_sem, recv_sem):
        self.send_sem, self.recv_sem = send_sem, recv_sem
        self.count = 0
        self.tags = {}
        self.sent = []

    def next(self):
        self.count += 1
        return self.count - 1

    def send(self, src, dst, device, tag=None, when=None):
        i = self.next()
        if tag is not None:
            if tag not in self.tags:
                self.tags[tag] = self.next()
            j = self.tags[tag]
        else:
            j = i
        copy = pltpu.make_async_remote_copy(
            src_ref=src,
            dst_ref=dst,
            send_sem=self.send_sem.at[i],
            recv_sem=self.recv_sem.at[j],
            device_id=device,
            device_id_type=MESH,
        )
        if when is None:
            copy.start()
        else:
            pl.when(when)(copy.start)
        self.sent.append((copy, when))
        return copy

    def arrived(self, tag, dst, device):
        if tag not in self.tags:
            self.tags[tag] = self.next()
        j = self.tags[tag]
        pltpu.make_async_remote_copy(
            src_ref=dst,
            dst_ref=dst,
            send_sem=self.send_sem.at[j],
            recv_sem=self.recv_sem.at[j],
            device_id=device,
            device_id_type=MESH,
        ).wait_recv()

    def left(self, copy):
        copy.wait_send()
        self.sent = [one for one in self.sent if one[0] is not copy]

    def drain(self):
        for copy, when in self.sent:
            if when is None:
                copy.wait_send()
            else:
                pl.when(when)(copy.wait_send)
        self.sent = []


class Line:
    def __init__(self, wire, at, name, slot):
        self.wire, self.at, self.name, self.slot = wire, at, name, slot

    def begin(self, own=None):
        at = self.at
        here = self.slot(at.z)
        own = here if own is None else own
        self.wire.send(own, here, at.partner, (self.name, 1))
        self.wire.send(own, here, at.mirror, (self.name, 2), at.middle)

    def take(self, i, when=None):
        at = self.at
        block = self.slot(at.line[i])
        if when is None:
            self.wire.arrived((self.name, i), block, at.partner)
        else:
            pl.when(when)(lambda: self.wire.arrived((self.name, i), block, at.partner))
        if when is not at.ends:
            to, tag = (at.mirror, 3) if i == 1 else (at.partner, i)
            self.wire.send(block, block, to, (self.name, tag), at.middle)
        return block


class Fetch:
    def __init__(self, sem):
        self.sem = sem
        self.count = 0
        self.open = []

    def start(self, src, dst):
        copy = pltpu.make_async_copy(src, dst, self.sem.at[self.count])
        self.count += 1
        copy.start()
        self.open.append(copy)
        return copy

    def done(self, copy):
        copy.wait()
        self.open = [one for one in self.open if one is not copy]

    def drain(self):
        for copy in self.open:
            copy.wait()
        self.open = []


def dot(a, b, ca=1, cb=0):
    return lax.dot_general(a, b, (((ca,), (cb,)), ((), ())), preferred_element_type=jnp.float32)


def tile(i, size=256):
    return pl.ds(pl.multiple_of(i * size, size), size)


def pick(placed_row, slots):
    which = lax.broadcasted_iota(jnp.int32, (slots, placed_row.shape[1]), 0)
    return jnp.where(which == placed_row, 1.0, 0.0).astype(jnp.bfloat16)


def build(stage, source, placed_row):
    planes, cap, width = stage.shape
    onehot = pick(placed_row, planes * cap)

    @pl.loop(0, width // 512)
    def _(i):
        cols = tile(i, 512)
        value = dot(onehot, source[:, cols]).astype(jnp.bfloat16)
        for k in range(planes):
            stage[k, :, cols] = value[k * cap : (k + 1) * cap]


def attend_kernel(
    cap,
    tok,
    w_own,
    norm_in,
    route,
    cot,
    w_out,
    qkv_out,
    normed_out,
    ctx_out,
    resid_out,
    sent_out,
    placed_out,
    gains_out,
    cot_raw,
    cot_zero,
    w_low,
    wfull,
    norm_sum,
    norm_got,
    qkv,
    normed,
    ctx,
    resid,
    sent,
    placed,
    gains,
    stage,
    send_sem,
    recv_sem,
    local_sem,
):
    at = Place()
    e, z = at.e, at.z
    depth = 4
    count, width = tok.shape
    shard = w_own.shape[1]
    wire = Wire(send_sem, recv_sem)
    fetch = Fetch(local_sem)
    groups = [(0, 3), (3, 1)]
    fetch.start(cot, cot_raw.at[z])
    w_low[...] = w_own[...].astype(jnp.bfloat16)
    lanes = norm_in.shape[1]
    columns = lax.broadcasted_iota(jnp.int32, (lanes, width), 1)
    offset = columns - (e * depth + z) * lanes
    ours = lax.broadcasted_iota(jnp.int32, (lanes, width), 0) == offset
    low = norm_in[...].astype(jnp.bfloat16)
    norm_sum[0] = jnp.zeros((16, width), jnp.bfloat16)
    norm_sum[0, 0:2, :] = dot(low, jnp.where(ours, 1.0, 0.0).astype(jnp.bfloat16)).astype(
        jnp.bfloat16
    )
    at.meet()

    def block(g, who, zz):
        first, mats = groups[g]
        start = pl.multiple_of((who * depth + zz) * shard, shard)
        return wfull.at[pl.ds(first, mats), pl.ds(start, shard)]

    def mine(g):
        first, mats = groups[g]
        return w_low.at[pl.ds(first, mats)]

    lines = [Line(wire, at, g, lambda zz, g=g: block(g, e, zz)) for g in range(2)]
    lines[0].begin(mine(0))
    norm_to = [at.partner, at.mirror, at.over_x, at.over_y, at.twin]
    norm_copy = wire.send(norm_sum.at[0], norm_got.at[0], norm_to[0])
    own = [fetch.start(mine(g), block(g, e, z)) for g in range(2)]
    to_x, to_y, to_far, to_twin = {}, {}, {}, {}

    def norm_next(k):
        norm_copy.wait_recv()
        norm_sum[k] = norm_sum[k - 1] + norm_got[k - 1]
        return wire.send(norm_sum.at[k], norm_got.at[k], norm_to[k])

    def plane(g, i):
        here = block(g, e, at.line[i])
        if i == 0:
            fetch.done(own[g])
        else:
            lines[g].take(i)
        to_x[g, i] = wire.send(here, here, at.over_x)
        to_y[g, i] = wire.send(here, here, at.over_y)
        to_twin[g, i, 0] = wire.send(here, here, at.twin)

    def forward(g, i):
        zz = at.line[i]
        from_x, from_y = block(g, at.ex, zz), block(g, at.ey, zz)
        to_x[g, i].wait_recv()
        if i in (0, 3):
            to_far[g, i] = wire.send(from_x, from_x, at.over_y)
        to_twin[g, i, 1] = wire.send(from_x, from_x, at.twin)
        to_y[g, i].wait_recv()
        if i in (1, 2):
            to_far[g, i] = wire.send(from_y, from_y, at.over_x)
        to_twin[g, i, 2] = wire.send(from_y, from_y, at.twin)

    def far(g, i):
        to_far[g, i].wait_recv()
        there = block(g, at.exy, at.line[i])
        to_twin[g, i, 3] = wire.send(there, there, at.twin)

    def finish(g):
        for i in range(depth):
            for k in range(4):
                to_twin[g, i, k].wait_recv()

    plane(0, 0)
    lane = lax.broadcasted_iota(jnp.int32, (count, 128), 1)
    chosen = jnp.where(route[...] == lane, 1.0, 0.0)
    rows_i = lax.broadcasted_iota(jnp.int32, (count, count), 0)
    cols_i = lax.broadcasted_iota(jnp.int32, (count, count), 1)
    lower = jnp.where(rows_i >= cols_i, 1.0, 0.0)
    running = dot(lower.astype(jnp.bfloat16), chosen.astype(jnp.bfloat16))
    rank = jnp.sum((running - 1.0) * chosen, axis=1, keepdims=True)
    column = route[...].astype(jnp.float32) * float(cap) + rank
    wide_r = lax.broadcasted_iota(jnp.int32, (count, 256), 0)
    wide_c = lax.broadcasted_iota(jnp.int32, (count, 256), 1)
    row = jnp.sum(jnp.where(wide_r == wide_c, column + 1.0, 0.0), axis=0, keepdims=True) - 1.0
    placed[z] = jnp.broadcast_to(row, (8, 256)).astype(jnp.int32)
    plane(0, 1)
    norm_copy = norm_next(1)
    forward(0, 0)
    plane(0, 2)
    norm_copy = norm_next(2)
    forward(0, 1)
    far(0, 0)
    plane(0, 3)
    lines[1].begin(mine(1))
    build(stage, cot, placed[z, 0:1, :count])
    norm_copy = norm_next(3)
    far(0, 1)
    forward(0, 2)
    plane(1, 0)
    plane(1, 1)
    norm_copy = norm_next(4)
    norm_copy.wait_recv()
    gain_rows = norm_sum[4] + norm_got[4]
    tally = jnp.concatenate(
        [
            jnp.broadcast_to(jnp.sum(chosen, axis=0, keepdims=True), (16, 128)),
            jnp.zeros((16, width - 128), jnp.float32),
        ],
        axis=1,
    )
    third_row = lax.broadcasted_iota(jnp.int32, (16, width), 0) == 2
    gains[...] = jnp.where(third_row, tally, gain_rows.astype(jnp.float32)).astype(jnp.bfloat16)
    fetch.start(gains, gains_out)
    gain = gains[0:1, :].astype(jnp.float32)
    bias = gains[1:2, :].astype(jnp.float32)

    @pl.loop(0, count // 64)
    def _(i):
        rows = tile(i, 64)
        piece = tok[rows, :].astype(jnp.float32)
        average = jnp.mean(piece, axis=-1, keepdims=True)
        centred = piece - average
        variance = jnp.mean(centred * centred, axis=-1, keepdims=True)
        normed[rows, :] = (centred * lax.rsqrt(variance + norm_eps) * gain + bias).astype(
            jnp.bfloat16
        )

    fetch.start(normed, normed_out)
    far(0, 2)
    forward(0, 3)
    plane(1, 2)
    plane(1, 3)
    cots = Line(wire, at, "cot", lambda zz: cot_raw.at[zz])
    places = Line(wire, at, "place", lambda zz: placed.at[zz])
    cots.begin(cot)
    places.begin()
    far(0, 3)
    finish(0)
    fetch.start(wfull.at[pl.ds(0, 3)], w_out.at[pl.ds(0, 3)])
    tiles = width // 256

    @pl.loop(0, 3 * tiles)
    def _(i):
        m = lax.div(i, tiles)
        cols = tile(lax.rem(i, tiles))
        qkv[m, :, cols] = dot(normed[...], wfull[m, :, cols]).astype(jnp.bfloat16)

    fetch.start(qkv, qkv_out)
    for i in range(depth):
        forward(1, i)
    places.take(1)
    cots.take(1)
    places.take(2, at.middle)
    cots.take(2, at.middle)
    slots_out = [
        wire.send(stage.at[at.across(k)], cot_zero.at[k], (at.across(k), z)) for k in range(1, 8)
    ]
    fetch.start(stage.at[e], cot_zero.at[0])
    causal = rows_i >= cols_i
    left = lax.broadcasted_iota(jnp.int32, (count, 128), 1) < 64
    scaling = jnp.asarray(64 ** (-0.5), jnp.bfloat16)

    def pair(i):
        cols = tile(i, 128)
        query = qkv[0, :, cols] * scaling
        keys = qkv[1, :, cols]
        values = qkv[2, :, cols]
        halves = []
        for side in range(2):
            mask = left if side == 0 else jnp.logical_not(left)
            scores = dot(jnp.where(mask, query, jnp.zeros_like(query)), keys, 1, 1)
            scores = jnp.where(causal, scores, masked_fill)
            top = jnp.max(scores, axis=-1, keepdims=True)
            expo = jnp.exp(scores - top)
            probs = expo / jnp.sum(expo, axis=-1, keepdims=True)
            halves.append(dot(probs.astype(jnp.bfloat16), values))
        ctx[:, cols] = jnp.where(left, halves[0], halves[1]).astype(jnp.bfloat16)

    pl.loop(0, width // 256)(pair)
    for i in range(depth):
        far(1, i)
    places.take(2, at.ends)
    cots.take(2, at.ends)
    places.take(3, at.middle)
    cots.take(3, at.middle)
    pl.loop(width // 256, width // 128)(pair)
    fetch.start(ctx, ctx_out)
    finish(1)
    fetch.start(wfull.at[pl.ds(3, 1)], w_out.at[pl.ds(3, 1)])

    @pl.loop(0, tiles)
    def _(i):
        cols = tile(i)
        value = tok[:, cols].astype(jnp.float32) + dot(ctx[...], wfull[3, :, cols])
        resid[:, cols] = value
        sent[:, cols] = value.astype(jnp.bfloat16)

    fetch.start(sent, sent_out)
    fetch.start(resid, resid_out)
    places.take(3, at.ends)
    cots.take(3, at.ends)
    fetch.start(placed, placed_out)
    for copy in slots_out:
        copy.wait_recv()
    wire.drain()
    fetch.drain()


def attend(cap, tokens, w_own, norm_own, routes, cotangent):
    count, width = tokens.shape
    bf, full = jnp.bfloat16, jnp.float32
    copies = 128
    shapes = [
        ((4, width, width), bf),
        ((3, count, width), bf),
        ((count, width), bf),
        ((count, width), bf),
        ((count, width), full),
        ((count, width), bf),
        ((4, 8, 256), jnp.int32),
        ((16, width), bf),
        ((4, count, width), bf),
        ((8, cap, width), bf),
    ]
    return pl.pallas_call(
        functools.partial(attend_kernel, cap),
        out_shape=[jax.ShapeDtypeStruct(*one) for one in shapes],
        in_specs=[VMEM_SPEC] * 5,
        out_specs=[ANY_SPEC] * len(shapes),
        scratch_shapes=[
            pltpu.VMEM((4, w_own.shape[1], width), bf),
            pltpu.VMEM((4, width, width), bf),
            pltpu.VMEM((5, 16, width), bf),
            pltpu.VMEM((5, 16, width), bf),
            pltpu.VMEM((3, count, width), bf),
            pltpu.VMEM((count, width), bf),
            pltpu.VMEM((count, width), bf),
            pltpu.VMEM((count, width), full),
            pltpu.VMEM((count, width), bf),
            pltpu.VMEM((4, 8, 256), jnp.int32),
            pltpu.VMEM((16, width), bf),
            pltpu.VMEM((8, cap, width), bf),
            pltpu.SemaphoreType.DMA((copies,)),
            pltpu.SemaphoreType.DMA((copies,)),
            pltpu.SemaphoreType.DMA((16,)),
        ],
        compiler_params=pltpu.CompilerParams(
            collective_id=0, has_side_effects=True, vmem_limit_bytes=62 << 20
        ),
    )(tokens, w_own, norm_own, routes, cotangent)


def gelu_pair(v):
    cdf = 0.5 + 0.5 * lax.erf(v * (0.5**0.5))
    pdf = jnp.exp(-0.5 * v * v) * ((2.0 * math.pi) ** -0.5)
    return v * cdf, cdf + v * pdf


def fold(v):
    total = v[0:8]
    for i in range(8, v.shape[0], 8):
        total = total + v[i : i + 8]
    return total


def spread(column, lanes):
    return jnp.concatenate([column] * (lanes // 128), axis=1)


def square_lanes(v):
    total = v[:, 0:128] * v[:, 0:128]
    for i in range(128, v.shape[1], 128):
        total = total + v[:, i : i + 128] * v[:, i : i + 128]
    return total


def unslot(placed_row, slots, out):
    planes, cap, width = slots.shape
    onehot = pick(placed_row, planes * cap)

    @pl.loop(0, width // 256)
    def _(j):
        cols = tile(j)
        value = slots[:, :, cols].reshape(planes * cap, 256)
        out[:, cols] = dot(onehot, value, 0, 0).astype(jnp.bfloat16)


class Home:
    def __init__(self, wire, at, name, part, got):
        self.wire, self.at, self.name = wire, at, name
        self.part, self.got = part, got

    def add(self, i, k):
        part = self.part(i)
        part[...] = (part[...].astype(jnp.float32) + self.got[k].astype(jnp.float32)).astype(
            jnp.bfloat16
        )

    def push(self, i):
        here = self.part(i)
        at = self.at
        self.wire.send(here, self.got.at[i - 1], at.partner, (self.name, i), at.ends)

    def pass_on(self, i):
        at, wire, name = self.at, self.wire, self.name

        @pl.when(at.middle)
        def _():
            wire.arrived((name, i), self.got.at[i - 1], at.partner)
            self.add(i, i - 1)

        k = {3: 3, 2: 4}[i]
        wire.send(self.part(i), self.got.at[k], at.mirror, (name, k + 1), at.middle)

    def near(self):
        at, wire, name = self.at, self.wire, self.name

        @pl.when(at.middle)
        def _():
            wire.arrived((name, 4), self.got.at[3], at.mirror)
            self.add(1, 3)

        wire.send(self.part(1), self.got.at[0], at.partner, (name, 1))

    def last(self):
        self.wire.arrived((self.name, 1), self.got.at[0], self.at.partner)

        @pl.when(self.at.middle)
        def _():
            self.wire.arrived((self.name, 5), self.got.at[4], self.at.mirror)
            self.add(0, 4)

    def total(self, cols):
        return self.part(0)[:, cols].astype(jnp.float32) + self.got[0, :, cols].astype(jnp.float32)


def expert_kernel(
    cap,
    sent_in,
    placed_in,
    cot_raw,
    cot_zero,
    up_in,
    down_in,
    vec,
    d_sum,
    g_up,
    g_down,
    delta_out,
    vec_part,
    scal,
    sent,
    placed,
    cot_line,
    up,
    down,
    raw,
    stage,
    rows,
    cots,
    xn,
    act,
    slope,
    delta,
    d_slots,
    back,
    part,
    z_in,
    d_xn,
    gate,
    d_logit,
    g_stage,
    send_sem,
    recv_sem,
    local_sem,
):
    at = Place()
    e, z = at.e, at.z
    depth, planes = 4, 8
    count, width = sent.shape
    slots = planes * cap
    units = up.shape[1]
    wire = Wire(send_sem, recv_sem)
    fetch = Fetch(local_sem)
    in_sent = fetch.start(sent_in, sent)
    in_placed = fetch.start(placed_in, placed)
    in_up = fetch.start(up_in, up)
    in_down = fetch.start(down_in, down)
    in_cot = fetch.start(cot_raw, cot_line)
    in_zero = fetch.start(cot_zero, cots.at[0])
    at.meet()
    fetch.done(in_sent)
    line = Line(wire, at, "row", lambda zz: raw.at[zz])
    line.begin(sent)
    vec_part[...] = jnp.zeros_like(vec_part)
    scal[...] = jnp.zeros_like(scal)
    fetch.done(in_placed)
    centroid = lambda: vec[0:1, :]
    row_copies, cot_copies, ret_copies = {}, {}, {}

    def exchange(i, dst):
        copies = [
            wire.send(stage.at[i, at.across(k)], dst.at[i, k], (at.across(k), z))
            for k in range(1, planes)
        ]
        dst[i, 0] = stage[i, e]
        return copies

    def slot_row(i):
        return placed[at.line[i], 0:1, :count]

    def rows_out(i):
        source = sent if i == 0 else raw.at[at.line[i]]
        build(stage.at[i], source, slot_row(i))
        row_copies[i] = exchange(i, rows)

    def cots_out(i):
        for copy in row_copies[i]:
            wire.left(copy)
        build(stage.at[i], cot_line.at[at.line[i]], slot_row(i))
        cot_copies[i] = exchange(i, cots)

    def forward(i):
        for copy in row_copies[i]:
            copy.wait_recv()
        gain, bias = vec[1:2, :], vec[2:3, :]

        @pl.loop(0, planes)
        def _(k):
            r = rows[i, k].astype(jnp.float32)
            logit = jnp.sum(r * centroid(), axis=-1, keepdims=True)
            g = jax.nn.sigmoid(logit)
            wide = jnp.broadcast_to(g, (cap, 128))
            gate[i, k] = wide
            scal[0:8] += fold(wide)
            average = jnp.mean(r, axis=-1, keepdims=True)
            centred = r - average
            variance = jnp.mean(centred * centred, axis=-1, keepdims=True)
            xn[i, pl.ds(pl.multiple_of(k * cap, 16), cap), :] = (
                centred * lax.rsqrt(variance + norm_eps) * gain + bias
            ).astype(jnp.bfloat16)

        if i == 0:
            fetch.done(in_up)

        @pl.loop(0, units // 256)
        def _(j):
            cols = tile(j)
            value, rate = gelu_pair(dot(xn[i], up[:, cols]))
            act[i, :, cols] = value.astype(jnp.bfloat16)
            slope[i, :, cols] = rate.astype(jnp.bfloat16)

        if i == 0:
            fetch.done(in_down)

        @pl.loop(0, width // 256)
        def _(j):
            cols = tile(j)
            branch = dot(act[i], down[:, cols])
            wide = spread(gate[i].reshape(slots, 128), 256)
            value = (wide * branch).astype(jnp.bfloat16)
            for k in range(planes):
                delta[i, k, :, cols] = value[k * cap : (k + 1) * cap]

        fetch.start(delta.at[i], delta_out.at[i])

    def backward(i):
        for copy in cot_copies[i]:
            copy.wait_recv()
        if i == 0:
            wire.left(cot_copies[1][0])

        @pl.loop(0, planes)
        def _(k):
            c = cots[i, k].astype(jnp.float32)
            g = gate[i, k]
            inner = jnp.sum(c * delta[i, k].astype(jnp.float32), axis=-1, keepdims=True)
            dl = (1.0 - g) * inner
            d_logit[i, k] = dl
            cots[i, k] = (c * spread(g, width)).astype(jnp.bfloat16)
            vec_part[0] += fold(rows[i, k].astype(jnp.float32) * spread(dl, width))

        @pl.loop(0, units // 256)
        def _(j):
            cols = tile(j)
            d_act = dot(cots[i].reshape(slots, width), down[cols, :], 1, 1)
            slope[i, :, cols] = (d_act * slope[i, :, cols].astype(jnp.float32)).astype(
                jnp.bfloat16
            )

        @pl.loop(0, width // 256)
        def _(j):
            cols = tile(j)
            value = dot(slope[i], up[cols, :], 1, 1)
            for k in range(planes):
                d_xn[k, :, cols] = value[k * cap : (k + 1) * cap]

        @pl.loop(0, planes)
        def _(k):
            r = rows[i, k].astype(jnp.float32)
            average = jnp.mean(r, axis=-1, keepdims=True)
            centred = r - average
            variance = jnp.mean(centred * centred, axis=-1, keepdims=True)
            scale = lax.rsqrt(variance + norm_eps)
            hat = centred * scale
            dx = d_xn[k]
            vec_part[1] += fold(dx * hat)
            vec_part[2] += fold(dx)
            dh = dx * vec[1:2, :]
            first = jnp.mean(dh, axis=-1, keepdims=True)
            second = jnp.mean(dh * hat, axis=-1, keepdims=True)
            d_in = scale * (dh - first - hat * second)
            d_slots[i, k] = (d_in + spread(d_logit[i, k], width) * centroid()).astype(jnp.bfloat16)

        ret_copies[i] = [
            wire.send(d_slots.at[i, k], back.at[i, e], (at.across(k), z))
            for k in range(1, planes)
        ]
        back[i, e] = d_slots[i, 0]

    home = Home(wire, at, "home", lambda i: part.at[i], z_in)

    def collect(i):
        for copy in ret_copies[i]:
            copy.wait_recv()
        unslot(slot_row(i), back.at[i], part.at[i])

    def weight_grad(lhs, rhs, index, out):
        @pl.loop(0, lhs.shape[-1] // 256)
        def _(j):
            cols = tile(j)
            left = lhs[:, :, cols].reshape(depth * slots, 256)
            value = dot(left, rhs[...].reshape(depth * slots, rhs.shape[-1]), 0, 0)
            scal[8:16] += fold(square_lanes(value))
            g_stage[index, cols, :] = value.astype(jnp.bfloat16)

        fetch.start(g_stage.at[index], out)

    rows_out(0)
    line.take(1)
    line.take(2, at.middle)
    rows_out(1)
    forward(0)
    line.take(2, at.ends)
    line.take(3, at.middle)
    rows_out(2)
    forward(1)
    line.take(3, at.ends)
    rows_out(3)
    fetch.done(in_zero)
    cot_copies[0] = []
    cot_copies[1] = [wire.send(cots.at[0], cots.at[1], at.partner)]
    fetch.done(in_cot)
    forward(2)
    cots_out(3)
    forward(3)
    cots_out(2)
    backward(3)
    backward(2)
    collect(3)
    home.push(3)
    backward(1)
    collect(2)
    home.push(2)
    home.pass_on(3)
    backward(0)
    collect(1)
    home.pass_on(2)
    home.near()
    weight_grad(act, cots, 0, g_down)
    weight_grad(xn, slope, 1, g_up)
    collect(0)
    home.last()

    @pl.loop(0, width // 256)
    def _(j):
        cols = tile(j)
        d_sum[:, cols] = home.total(cols)

    wire.drain()
    fetch.drain()


def expert_layer(cap, sent, placed, cot_raw, cot_zero, up, down, vec):
    count, width = sent.shape
    units = up.shape[1]
    depth = 4
    bf, full = jnp.bfloat16, jnp.float32
    slots = 8 * cap
    copies = 3 * 7 * depth + 32
    shapes = [
        ((count, width), full),
        ((width, units), bf),
        ((units, width), bf),
        ((depth, 8, cap, width), bf),
        ((3, 8, width), full),
        ((16, 128), full),
    ]
    big = pltpu.VMEM((depth, 8, cap, width), bf)
    return pl.pallas_call(
        functools.partial(expert_kernel, cap),
        out_shape=[jax.ShapeDtypeStruct(*one) for one in shapes],
        in_specs=[ANY_SPEC] * 6 + [VMEM_SPEC],
        out_specs=[VMEM_SPEC, ANY_SPEC, ANY_SPEC, ANY_SPEC, VMEM_SPEC, VMEM_SPEC],
        scratch_shapes=[
            pltpu.VMEM((count, width), bf),
            pltpu.VMEM((depth, 8, 256), jnp.int32),
            pltpu.VMEM((depth, count, width), bf),
            pltpu.VMEM((width, units), bf),
            pltpu.VMEM((units, width), bf),
            pltpu.VMEM((depth, count, width), bf),
            big,
            big,
            big,
            pltpu.VMEM((depth, slots, width), bf),
            pltpu.VMEM((depth, slots, units), bf),
            pltpu.VMEM((depth, slots, units), bf),
            big,
            big,
            big,
            pltpu.VMEM((depth, count, width), bf),
            pltpu.VMEM((5, count, width), bf),
            pltpu.VMEM((8, cap, width), full),
            pltpu.VMEM((depth, 8, cap, 128), full),
            pltpu.VMEM((depth, 8, cap, 128), full),
            pltpu.VMEM((2, max(width, units), max(width, units)), bf),
            pltpu.SemaphoreType.DMA((copies,)),
            pltpu.SemaphoreType.DMA((copies,)),
            pltpu.SemaphoreType.DMA((16,)),
        ],
        compiler_params=pltpu.CompilerParams(
            collective_id=1, has_side_effects=True, vmem_limit_bytes=62 << 20
        ),
    )(sent, placed, cot_raw, cot_zero, up, down, vec)


def reduce_kernel(
    cap,
    d_sum,
    cot,
    w_in,
    qkv_in,
    normed_in,
    ctx,
    tok,
    gains,
    placed,
    delta_in,
    resid,
    vec_part,
    scal,
    block_out,
    token_grad,
    shard_out,
    norm_out,
    vec_out,
    square_out,
    wfull,
    qkv,
    normed,
    delta,
    d_resid,
    d_proj,
    d_ctx,
    d_qkv,
    d_norm,
    stage,
    twin_in,
    x_in,
    y_in,
    x_last,
    y_last,
    done,
    z_last,
    back,
    part,
    z_in,
    small,
    small_in,
    square,
    send_sem,
    recv_sem,
    local_sem,
):
    at = Place()
    e, z = at.e, at.z
    depth, planes = 4, 8
    count, width = tok.shape
    shard = shard_out.shape[1]
    column = depth * shard
    half = column // 2
    wire = Wire(send_sem, recv_sem)
    fetch = Fetch(local_sem)
    in_delta = {i: fetch.start(delta_in.at[i], delta.at[i]) for i in (3, 2, 1, 0)}
    in_w = {m: fetch.start(w_in.at[m], wfull.at[m]) for m in (3, 2, 1, 0)}
    in_qkv = fetch.start(qkv_in, qkv)
    in_normed = fetch.start(normed_in, normed)
    at.meet()
    ret = {}
    home = Home(wire, at, "home", lambda i: part.at[i], z_in)

    def give(i):
        fetch.done(in_delta[i])
        ret[i] = [
            wire.send(delta.at[i, k], back.at[i, e], (at.across(k), z)) for k in range(1, planes)
        ]
        back[i, e] = delta[i, 0]

    def collect(i):
        for copy in ret[i]:
            copy.wait_recv()
        unslot(placed[at.line[i], 0:1, :count], back.at[i], part.at[i])

    def weight_grad(m, left_ref, right):
        @pl.loop(0, planes)
        def _(i):
            cols = pl.ds(pl.multiple_of(i * column, column), column)
            value = dot(left_ref[:, cols], right[...], 0, 0).astype(jnp.bfloat16)
            stage[m, lax.div(i, 4), lax.rem(lax.div(i, 2), 2), lax.rem(i, 2)] = value

    other = 1 - at.core
    first, second, third, fourth = {}, {}, {}, {}

    def to_core(m):
        first[m] = wire.send(stage.at[m, :, :, other], twin_in.at[m], at.twin)

    def to_plane(m):
        first[m].wait_recv()
        for j in range(2):
            for i in range(2):
                twin_in[m, j, i] = twin_in[m, j, i] + stage[m, j, i, at.core]
        second[m] = (
            wire.send(twin_in.at[m, :, 1 - at.x, pl.ds(0, half)], x_in.at[m], at.over_x),
            wire.send(twin_in.at[m, 1 - at.y, :, pl.ds(half, half)], y_in.at[m], at.over_y),
        )

    def to_last(m):
        second[m][0].wait_recv()
        for j in range(2):
            x_in[m, j] = x_in[m, j] + twin_in[m, j, at.x, 0:half]
        one = wire.send(x_in.at[m, 1 - at.y], x_last.at[m], at.over_y)
        second[m][1].wait_recv()
        for i in range(2):
            y_in[m, i] = y_in[m, i] + twin_in[m, at.y, i, half:]
        two = wire.send(y_in.at[m, 1 - at.x], y_last.at[m], at.over_x)
        third[m] = (one, two)

    def to_owner(m):
        third[m][0].wait_recv()
        pair = (2, shard, width)
        done[m, 0:2] = (x_in[m, at.y] + x_last[m]).reshape(pair)
        third[m][1].wait_recv()
        done[m, 2:4] = (y_in[m, at.x] + y_last[m]).reshape(pair)
        fourth[m] = [
            wire.send(done.at[m, at.mates[k][1]], z_last.at[m, k - 1], at.mates[k])
            for k in range(1, depth)
        ]

    def own(m):
        total = done[m, z].astype(jnp.float32)
        for k in range(1, depth):
            fourth[m][k - 1].wait_recv()
            total = total + z_last[m, k - 1].astype(jnp.float32)
        shard_out[m] = total

    give(3)
    value = cot[...].astype(jnp.float32) + d_sum[...]
    d_resid[...] = value
    d_proj[...] = value.astype(jnp.bfloat16)
    weight_grad(3, ctx, d_proj)
    to_core(3)
    fetch.done(in_w[3])

    @pl.loop(0, width // 256)
    def _(j):
        cols = tile(j)
        d_ctx[:, cols] = dot(d_proj[...], wfull[3, cols, :], 1, 1).astype(jnp.bfloat16)

    to_plane(3)
    fetch.done(in_qkv)
    causal = lax.broadcasted_iota(jnp.int32, (count, count), 0) >= lax.broadcasted_iota(
        jnp.int32, (count, count), 1
    )
    left = lax.broadcasted_iota(jnp.int32, (count, 128), 1) < 64
    scaling = 64 ** (-0.5)

    def pair(i):
        cols = tile(i, 128)
        query = qkv[0, :, cols]
        keys = qkv[1, :, cols]
        values = qkv[2, :, cols]
        d_out = d_ctx[:, cols]
        zero = jnp.zeros_like(query)
        got = []
        for side in range(2):
            mask = left if side == 0 else jnp.logical_not(left)
            q_side = jnp.where(mask, query, zero)
            k_side = jnp.where(mask, keys, zero)
            o_side = jnp.where(mask, d_out, zero)
            scores = dot(q_side, keys, 1, 1) * scaling
            scores = jnp.where(causal, scores, masked_fill)
            top = jnp.max(scores, axis=-1, keepdims=True)
            expo = jnp.exp(scores - top)
            probs = expo / jnp.sum(expo, axis=-1, keepdims=True)
            d_probs = dot(o_side, values, 1, 1)
            inner = jnp.sum(d_probs * probs, axis=-1, keepdims=True)
            d_scores = (probs * (d_probs - inner)).astype(jnp.bfloat16)
            got.append(
                (
                    dot(d_scores, k_side),
                    dot(d_scores, q_side, 0, 0),
                    dot(probs.astype(jnp.bfloat16), o_side, 0, 0),
                )
            )
        d_qkv[0, :, cols] = ((got[0][0] + got[1][0]) * scaling).astype(jnp.bfloat16)
        d_qkv[1, :, cols] = ((got[0][1] + got[1][1]) * scaling).astype(jnp.bfloat16)
        d_qkv[2, :, cols] = (got[0][2] + got[1][2]).astype(jnp.bfloat16)

    pl.loop(0, width // 256)(pair)
    give(2)
    pl.loop(width // 256, width // 128)(pair)
    fetch.done(in_normed)
    weight_grad(2, normed, d_qkv.at[2])
    to_core(2)
    to_last(3)
    weight_grad(1, normed, d_qkv.at[1])
    to_core(1)
    to_plane(2)
    weight_grad(0, normed, d_qkv.at[0])
    to_core(0)
    collect(3)
    home.push(3)
    to_owner(3)
    to_plane(1)
    for m in (2, 1, 0):
        fetch.done(in_w[m])

    @pl.loop(0, width // 256)
    def _(j):
        cols = tile(j)
        d_norm[:, cols] = (
            dot(d_qkv[0], wfull[0, cols, :], 1, 1)
            + dot(d_qkv[1], wfull[1, cols, :], 1, 1)
            + dot(d_qkv[2], wfull[2, cols, :], 1, 1)
        )

    gain = gains[0:1, :].astype(jnp.float32)
    d_gain = jnp.zeros((8, width), jnp.float32)
    d_bias = jnp.zeros((8, width), jnp.float32)
    for i in range(0, count, 64):
        piece = tok[i : i + 64, :].astype(jnp.float32)
        average = jnp.mean(piece, axis=-1, keepdims=True)
        centred = piece - average
        variance = jnp.mean(centred * centred, axis=-1, keepdims=True)
        scale = lax.rsqrt(variance + norm_eps)
        hat = centred * scale
        dx = d_norm[i : i + 64, :]
        d_gain = d_gain + fold(dx * hat)
        d_bias = d_bias + fold(dx)
        dh = dx * gain
        mean_one = jnp.mean(dh, axis=-1, keepdims=True)
        mean_two = jnp.mean(dh * hat, axis=-1, keepdims=True)
        d_in = scale * (dh - mean_one - hat * mean_two)
        token_grad[i : i + 64, :] = (d_resid[i : i + 64, :] + d_in).astype(jnp.bfloat16)
    mine = small.at[0]
    mine[...] = jnp.zeros((16, width), jnp.float32)
    mine[2:3, :] = gains[2:3, :].astype(jnp.float32)
    mine[0:1, :] = jnp.sum(d_gain, axis=0, keepdims=True)
    mine[1:2, :] = jnp.sum(d_bias, axis=0, keepdims=True)
    for k in range(3):
        mine[8 + k : 9 + k, :] = jnp.sum(vec_part[k], axis=0, keepdims=True)
    small_to = [at.partner, at.mirror, at.over_x, at.over_y, at.twin]

    def small_send(k):
        rows = pl.ds(0, 16 if k < 2 else 8)
        return wire.send(small.at[k, rows], small_in.at[k, rows], small_to[k])

    def small_next(k, copy):
        copy.wait_recv()
        rows = slice(0, 16 if k < 3 else 8)
        small[k, rows] = small[k - 1, rows] + small_in[k - 1, rows]
        if k == 2:
            vec_out[...] = small[2, 8:16]
        return small_send(k) if k < 5 else None

    flow = small_send(0)
    to_plane(0)
    to_last(2)
    collect(2)
    home.push(2)
    home.pass_on(3)
    flow = small_next(1, flow)
    give(1)
    to_last(1)
    to_owner(2)
    flow = small_next(2, flow)
    own(3)
    home.pass_on(2)
    give(0)
    to_last(0)
    flow = small_next(3, flow)
    to_owner(1)
    own(2)
    flow = small_next(4, flow)
    to_owner(0)
    collect(1)
    home.near()
    small_next(5, flow)
    norm_out[...] = small[5, 0:8]
    own(1)
    collect(0)
    norm_rows = norm_out[0:2, :]
    vec_rows = vec_out[0:3, :]
    squares = jnp.sum(norm_rows * norm_rows, axis=0, keepdims=True) / (planes * depth) + jnp.sum(
        vec_rows * vec_rows, axis=0, keepdims=True
    ) / depth
    local = scal[8:16, :]
    for m in (3, 2, 1):
        local = local + fold(square_lanes(shard_out[m]))
    lane_squares = squares[:, 0:128]
    for i in range(128, width, 128):
        lane_squares = lane_squares + squares[:, i : i + 128]
    head = lax.broadcasted_iota(jnp.int32, (8, 128), 0) == 0
    local = local + jnp.where(head, jnp.broadcast_to(lane_squares, (8, 128)), 0.0)
    own(0)
    square[0, e] = local + fold(square_lanes(shard_out[0]))
    spot = square.at[0, e]
    copies = [wire.send(spot, spot, (at.across(k), z)) for k in range(1, planes)]
    home.last()

    @pl.loop(0, width // 256)
    def _(j):
        cols = tile(j)
        block_out[:, cols] = (resid[:, cols] + home.total(cols)).astype(jnp.bfloat16)

    for copy in copies:
        copy.wait_recv()
    total = square[0, 0]
    for k in range(1, planes):
        total = total + square[0, k]
    square[1, z] = total
    spot = square.at[1, z]
    copies = [wire.send(spot, spot, at.mates[k]) for k in range(1, depth)]
    for copy in copies:
        copy.wait_recv()
    total = square[1, 0]
    for d in range(1, depth):
        total = total + square[1, d]
    square_out[...] = total
    wire.drain()
    fetch.drain()


def attend_back(cap, shard, *args):
    tokens = args[6]
    count, width = tokens.shape
    depth = 4
    bf, full = jnp.bfloat16, jnp.float32
    column = depth * shard
    half = column // 2
    copies = 7 * depth + 96
    shapes = [
        ((count, width), bf),
        ((count, width), bf),
        ((4, shard, width), full),
        ((8, width), full),
        ((8, width), full),
        ((8, 128), full),
    ]
    return pl.pallas_call(
        functools.partial(reduce_kernel, cap),
        out_shape=[jax.ShapeDtypeStruct(*one) for one in shapes],
        in_specs=[VMEM_SPEC] * 2
        + [ANY_SPEC] * 3
        + [VMEM_SPEC] * 4
        + [ANY_SPEC]
        + [VMEM_SPEC] * 3,
        out_specs=[VMEM_SPEC] * 6,
        scratch_shapes=[
            pltpu.VMEM((4, width, width), bf),
            pltpu.VMEM((3, count, width), bf),
            pltpu.VMEM((count, width), bf),
            pltpu.VMEM((depth, 8, cap, width), bf),
            pltpu.VMEM((count, width), full),
            pltpu.VMEM((count, width), bf),
            pltpu.VMEM((count, width), bf),
            pltpu.VMEM((3, count, width), bf),
            pltpu.VMEM((count, width), full),
            pltpu.VMEM((4, 2, 2, 2, column, width), bf),
            pltpu.VMEM((4, 2, 2, column, width), bf),
            pltpu.VMEM((4, 2, half, width), bf),
            pltpu.VMEM((4, 2, half, width), bf),
            pltpu.VMEM((4, half, width), bf),
            pltpu.VMEM((4, half, width), bf),
            pltpu.VMEM((4, depth, shard, width), bf),
            pltpu.VMEM((4, depth - 1, shard, width), bf),
            pltpu.VMEM((depth, 8, cap, width), bf),
            pltpu.VMEM((depth, count, width), bf),
            pltpu.VMEM((5, count, width), bf),
            pltpu.VMEM((6, 16, width), full),
            pltpu.VMEM((5, 16, width), full),
            pltpu.VMEM((2, 8, 8, 128), full),
            pltpu.SemaphoreType.DMA((copies,)),
            pltpu.SemaphoreType.DMA((copies,)),
            pltpu.SemaphoreType.DMA((16,)),
        ],
        compiler_params=pltpu.CompilerParams(
            collective_id=2, has_side_effects=True, vmem_limit_bytes=62 << 20
        ),
    )(*args)


def adam_kernel(
    up,
    up_first,
    up_second,
    up_grad,
    down,
    down_first,
    down_second,
    down_grad,
    attn,
    attn_first,
    attn_second,
    attn_grad,
    squares,
    up_new,
    up_moment,
    up_square,
    down_new,
    down_moment,
    down_square,
    attn_new,
    attn_moment,
    attn_square,
):
    norm = jnp.sqrt(jnp.sum(squares[...], keepdims=True))
    clip = clip_level / jnp.maximum(norm, clip_level)
    sets = [
        (up, up_first, up_second, up_grad, up_new, up_moment, up_square),
        (down, down_first, down_second, down_grad, down_new, down_moment, down_square),
        (attn, attn_first, attn_second, attn_grad, attn_new, attn_moment, attn_square),
    ]
    for weight, first, second, grad, new, moment, square in sets:
        got = adam_step(
            weight[...].astype(jnp.float32),
            first[...],
            second[...],
            grad[...].astype(jnp.float32),
            clip,
            rate_matrix,
            decay_rate,
        )
        new[...], moment[...], square[...] = got


def adam_all(up, down, attn, squares):
    steps = 16
    full = jnp.float32
    in_specs, out_specs, shapes, aliases = [], [], [], {}
    for group in (up, down, attn):
        rows, width = group[0].shape
        spec = pl.BlockSpec((rows // steps, width), lambda i: (i, 0))
        in_specs += [spec] * 4
        out_specs += [spec] * 3
        shapes += [jax.ShapeDtypeStruct((rows, width), full)] * 3
    return pl.pallas_call(
        adam_kernel,
        grid=(steps,),
        out_shape=shapes,
        in_specs=in_specs + [pl.BlockSpec(squares.shape, lambda i: (0, 0))],
        out_specs=out_specs,
        compiler_params=pltpu.CompilerParams(vmem_limit_bytes=40 << 20),
    )(*up, *down, *attn, squares)


def shards(
    tokens,
    cotangent,
    routes,
    attn_weight,
    attn_first,
    attn_second,
    norm_param,
    norm_first,
    norm_second,
    up_weight,
    up_first,
    up_second,
    down_weight,
    down_first,
    down_second,
    expert_vector,
    vector_first,
    vector_second,
):
    experts_here = lax.axis_size(EX)
    hidden_size = lax.axis_size(HI)
    token_count = tokens.shape[0]
    features = tokens.shape[1]
    capacity = 2 * token_count // experts_here
    slot_rows = experts_here * capacity
    head_dim = features // HEADS
    scaling = head_dim ** (-0.5)
    attn_low = attn_weight.astype(jnp.bfloat16)
    norm_low = norm_param.astype(jnp.bfloat16)
    attn_full, norm_full = (
        lax.all_gather(attn_low, BOTH, axis=1, tiled=True),
        lax.all_gather(norm_low, BOTH, axis=1, tiled=True),
    )
    inputs = tokens.astype(jnp.float32)
    normed, norm_pull = jax.vjp(
        layer_norm, inputs, norm_full[0].astype(jnp.float32), norm_full[1].astype(jnp.float32)
    )
    normed_low = normed.astype(jnp.bfloat16)
    projected = jnp.einsum(
        "td,sde->ste", normed_low, attn_full[:3], preferred_element_type=jnp.float32
    ).astype(jnp.bfloat16)
    query = projected[0].reshape(token_count, HEADS, head_dim)
    keys_all = projected[1].reshape(token_count, HEADS, head_dim)
    values_all = projected[2].reshape(token_count, HEADS, head_dim)
    causal = jnp.arange(token_count)[:, None] >= jnp.arange(token_count)[None, :]

    def score_rows():
        raw = (
            jnp.einsum("qhe,khe->hqk", query, keys_all, preferred_element_type=jnp.float32)
            * scaling
        )
        return jnp.where(causal[None], raw, masked_fill)

    scores = score_rows()
    row_max = jnp.max(scores, axis=-1, keepdims=True)
    expo = jnp.exp(scores - row_max)
    row_total = jnp.sum(expo, axis=-1, keepdims=True)
    log_total = row_max + jnp.log(row_total)
    probs_low = (expo / row_total).astype(jnp.bfloat16)
    context = jnp.einsum("hqk,khe->qhe", probs_low, values_all, preferred_element_type=jnp.float32)
    context = context.reshape(token_count, features).astype(jnp.bfloat16)
    resid = inputs + jnp.dot(context, attn_full[3], preferred_element_type=jnp.float32)
    route = routes[:, 0]
    chosen = (route[:, None] == jnp.arange(experts_here, dtype=jnp.int32)[None, :]).astype(
        jnp.int32
    )
    ranked = jnp.sum((jnp.cumsum(chosen, axis=0) - 1) * chosen, axis=1)
    placed = route * capacity + ranked
    placing = (jnp.arange(slot_rows, dtype=jnp.int32)[:, None] == placed[None, :]).astype(
        jnp.bfloat16
    )
    outgoing = jnp.dot(
        placing, resid.astype(jnp.bfloat16), preferred_element_type=jnp.float32
    ).astype(jnp.bfloat16)
    occupied = jnp.sum(placing.astype(jnp.float32), axis=1).astype(jnp.bfloat16)
    arrived, arrived_mask = (
        lax.all_to_all(
            outgoing.reshape(experts_here, capacity, features),
            EX,
            split_axis=0,
            concat_axis=0,
            tiled=True,
        ),
        lax.all_to_all(
            occupied.reshape(experts_here, capacity),
            EX,
            split_axis=0,
            concat_axis=0,
            tiled=True,
        ),
    )
    gathered, gathered_mask = (
        lax.all_gather(arrived, HI, axis=0, tiled=True),
        lax.all_gather(arrived_mask, HI, axis=0, tiled=True),
    )
    rows_all = gathered.reshape(-1, features)
    mask_all = gathered_mask.reshape(-1).astype(jnp.float32)
    rows_float = rows_all.astype(jnp.float32)
    centroid = expert_vector[0, 0]
    gating = jax.nn.sigmoid(jnp.sum(rows_float * centroid, axis=-1))
    expert_normed, expert_pull = jax.vjp(
        layer_norm, rows_float, expert_vector[0, 1], expert_vector[0, 2]
    )
    expert_low = expert_normed.astype(jnp.bfloat16)
    before = jnp.dot(expert_low, up_weight[0], preferred_element_type=jnp.float32)
    after, gelu_pull = jax.vjp(gelu_exact, before)
    after_low = after.astype(jnp.bfloat16)
    branch_own = lax.psum_scatter(
        jnp.dot(after_low, down_weight[0], preferred_element_type=jnp.float32).astype(jnp.bfloat16),
        HI,
        scatter_dimension=0,
        tiled=True,
    ).astype(jnp.float32)
    own_start = lax.axis_index(HI) * slot_rows
    gating_own = lax.dynamic_slice_in_dim(gating, own_start, slot_rows, 0)
    delta = (gating_own[:, None] * branch_own).astype(jnp.bfloat16)
    returned = lax.all_to_all(
        delta.reshape(experts_here, capacity, features),
        EX,
        split_axis=0,
        concat_axis=0,
        tiled=True,
    )
    delta_tokens = jnp.einsum(
        "st,sd->td",
        placing,
        returned.reshape(slot_rows, features),
        preferred_element_type=jnp.float32,
    )
    block_out = (resid + delta_tokens).astype(jnp.bfloat16)
    routed_count = jnp.sum(mask_all)
    gate_total = jnp.sum(mask_all * gating)
    expert_stats = jnp.stack(
        [routed_count / (token_count * hidden_size), gate_total / routed_count]
    )[:, None]
    cot_slots = jnp.dot(placing, cotangent, preferred_element_type=jnp.float32).astype(jnp.bfloat16)
    cot_arrived = lax.all_to_all(
        cot_slots.reshape(experts_here, capacity, features),
        EX,
        split_axis=0,
        concat_axis=0,
        tiled=True,
    )
    cot_rows = lax.all_gather(cot_arrived, HI, axis=0, tiled=True).reshape(-1, features)
    d_branch = (gating[:, None] * cot_rows.astype(jnp.float32)).astype(jnp.bfloat16)
    grad_down = jnp.einsum("gf,gd->fd", after_low, d_branch, preferred_element_type=jnp.float32)
    d_after = jnp.einsum("gd,fd->gf", d_branch, down_weight[0], preferred_element_type=jnp.float32)
    d_before = gelu_pull(d_after)[0].astype(jnp.bfloat16)
    grad_up = jnp.einsum("gd,gf->df", expert_low, d_before, preferred_element_type=jnp.float32)
    d_expert_normed = jnp.einsum(
        "gf,df->gd", d_before, up_weight[0], preferred_element_type=jnp.float32
    )
    d_rows, d_expert_gain, d_expert_bias = expert_pull(d_expert_normed)
    d_rows_own = lax.psum_scatter(
        d_rows.astype(jnp.bfloat16), HI, scatter_dimension=0, tiled=True
    ).astype(jnp.float32)
    cot_own = lax.dynamic_slice_in_dim(cot_rows, own_start, slot_rows, 0).astype(jnp.float32)
    rows_own = lax.dynamic_slice_in_dim(rows_float, own_start, slot_rows, 0)
    d_gating = jnp.sum(cot_own * branch_own, axis=-1)
    d_logit = d_gating * gating_own * (1.0 - gating_own)
    d_centroid = jnp.sum(d_logit[:, None] * rows_own, axis=0)
    d_sent = (d_rows_own + d_logit[:, None] * centroid).astype(jnp.bfloat16)
    back_slots = lax.all_to_all(
        d_sent.reshape(experts_here, capacity, features),
        EX,
        split_axis=0,
        concat_axis=0,
        tiled=True,
    )
    d_resid = cotangent.astype(jnp.float32) + jnp.einsum(
        "st,sd->td",
        placing,
        back_slots.reshape(slot_rows, features),
        preferred_element_type=jnp.float32,
    )
    vector_grad = lax.psum(jnp.stack([d_centroid, d_expert_gain, d_expert_bias])[None], HI)
    d_project = d_resid.astype(jnp.bfloat16)
    grad_out_proj = jnp.einsum("td,te->de", context, d_project, preferred_element_type=jnp.float32)
    d_context = jnp.einsum(
        "te,de->td", d_project, attn_full[3], preferred_element_type=jnp.float32
    ).astype(jnp.bfloat16)
    d_context = d_context.reshape(token_count, HEADS, head_dim)
    attn_probs = jnp.exp(score_rows() - log_total)
    probs_again = attn_probs.astype(jnp.bfloat16)
    d_probs = jnp.einsum("qhe,khe->hqk", d_context, values_all, preferred_element_type=jnp.float32)
    d_values = jnp.einsum(
        "hqk,qhe->khe", probs_again, d_context, preferred_element_type=jnp.float32
    ).astype(jnp.bfloat16)
    d_scores = (
        attn_probs * (d_probs - jnp.sum(d_probs * attn_probs, axis=-1, keepdims=True))
    ).astype(jnp.bfloat16)
    d_query = (
        jnp.einsum("hqk,khe->qhe", d_scores, keys_all, preferred_element_type=jnp.float32) * scaling
    ).astype(jnp.bfloat16)
    d_keys = (
        jnp.einsum("hqk,qhe->khe", d_scores, query, preferred_element_type=jnp.float32) * scaling
    ).astype(jnp.bfloat16)
    d_projected = jnp.stack(
        [
            d_query.reshape(token_count, features),
            d_keys.reshape(token_count, features),
            d_values.reshape(token_count, features),
        ]
    )
    grad_qkv = jnp.einsum(
        "td,ste->sde", normed_low, d_projected, preferred_element_type=jnp.float32
    )
    d_normed = jnp.einsum(
        "ste,sde->td", d_projected, attn_full[:3], preferred_element_type=jnp.float32
    )
    d_inputs, d_norm_gain, d_norm_bias = norm_pull(d_normed)
    token_grad = (d_resid + d_inputs).astype(jnp.bfloat16)
    grad_attn = jnp.concatenate([grad_qkv, grad_out_proj[None]], axis=0)
    grad_norm_param = jnp.stack([d_norm_gain, d_norm_bias])
    attn_shard, norm_shard = (
        lax.psum_scatter(grad_attn, BOTH, scatter_dimension=1, tiled=True),
        lax.psum_scatter(grad_norm_param, BOTH, scatter_dimension=1, tiled=True),
    )
    local_square = (
        jnp.sum(attn_shard * attn_shard)
        + jnp.sum(norm_shard * norm_shard)
        + jnp.sum(grad_up * grad_up)
        + jnp.sum(grad_down * grad_down)
        + jnp.sum(vector_grad * vector_grad) / hidden_size
    )
    grad_norm = jnp.sqrt(lax.psum(local_square, BOTH))
    clip_factor = clip_level / jnp.maximum(grad_norm, clip_level)
    attn_new = adam_step(
        attn_weight, attn_first, attn_second, attn_shard, clip_factor, rate_matrix, decay_rate
    )
    norm_new = adam_step(
        norm_param, norm_first, norm_second, norm_shard, clip_factor, rate_vector, 0.0
    )
    up_new = adam_step(
        up_weight.astype(jnp.float32),
        up_first,
        up_second,
        grad_up[None],
        clip_factor,
        rate_matrix,
        decay_rate,
    )
    down_new = adam_step(
        down_weight.astype(jnp.float32),
        down_first,
        down_second,
        grad_down[None],
        clip_factor,
        rate_matrix,
        decay_rate,
    )
    vector_new = adam_step(
        expert_vector, vector_first, vector_second, vector_grad, clip_factor, rate_vector, 0.0
    )
    return (
        block_out,
        token_grad,
        grad_norm,
        attn_new[0],
        attn_new[1],
        attn_new[2],
        norm_new[0],
        norm_new[1],
        norm_new[2],
        up_new[0],
        up_new[1],
        up_new[2],
        down_new[0],
        down_new[1],
        down_new[2],
        vector_new[0],
        vector_new[1],
        vector_new[2],
        expert_stats,
    )


def fast_shards(
    tokens,
    cotangent,
    routes,
    attn_weight,
    attn_first,
    attn_second,
    norm_param,
    norm_first,
    norm_second,
    up_weight,
    up_first,
    up_second,
    down_weight,
    down_first,
    down_second,
    expert_vector,
    vector_first,
    vector_second,
):
    experts = lax.axis_size(EX)
    depth = lax.axis_size(HI)
    count, width = tokens.shape
    cap = 2 * count // experts
    shard = attn_weight.shape[1]
    lanes = norm_param.shape[1]
    place = lax.axis_index(EX) * depth + lax.axis_index(HI)
    w_full, qkv, normed, ctx, resid, sent, placed, gains, cot_raw, cot_zero = attend(
        cap, tokens, attn_weight, norm_param, routes, cotangent
    )
    vec = jnp.pad(expert_vector[0], ((0, 5), (0, 0)))
    d_sum, grad_up, grad_down, delta, vec_part, scal = expert_layer(
        cap, sent, placed, cot_raw, cot_zero, up_weight[0], down_weight[0], vec
    )
    block_out, token_grad, attn_shard, norm_grads, vec_grads, squares = attend_back(
        cap,
        shard,
        d_sum,
        cotangent,
        w_full,
        qkv,
        normed,
        ctx,
        tokens,
        gains,
        placed,
        delta,
        resid,
        vec_part,
        scal,
    )
    here = lax.axis_index(EX)
    routed = lax.dynamic_slice(norm_grads, (2, here), (1, 1))[0, 0]
    empty = depth * experts * cap - routed
    gate_total = jnp.sum(scal[0:8, 0]) - 0.5 * empty
    expert_stats = jnp.stack([routed / (count * depth), gate_total / routed])[:, None]
    norm_shard = lax.dynamic_slice(norm_grads, (0, place * lanes), (2, lanes))
    vector_grad = vec_grads[None, 0:3]
    grad_norm = jnp.sqrt(jnp.sum(squares))
    clip_factor = clip_level / jnp.maximum(grad_norm, clip_level)
    flat = lambda v: v.reshape(-1, v.shape[-1])
    new = adam_all(
        [flat(v) for v in (up_weight, up_first, up_second, grad_up)],
        [flat(v) for v in (down_weight, down_first, down_second, grad_down)],
        [flat(v) for v in (attn_weight, attn_first, attn_second, attn_shard)],
        squares,
    )
    up_new = [v.reshape(up_weight.shape) for v in new[0:3]]
    down_new = [v.reshape(down_weight.shape) for v in new[3:6]]
    attn_new = [v.reshape(attn_weight.shape) for v in new[6:9]]
    norm_new = adam_step(
        norm_param, norm_first, norm_second, norm_shard, clip_factor, rate_vector, 0.0
    )
    vector_new = adam_step(
        expert_vector, vector_first, vector_second, vector_grad, clip_factor, rate_vector, 0.0
    )
    return (
        block_out,
        token_grad,
        grad_norm,
        *attn_new,
        *norm_new,
        *up_new,
        *down_new,
        *vector_new,
        expert_stats,
    )


def solution(mesh):
    small = mesh.shape[EX] == 8 and mesh.shape[HI] == 4
    return jax.shard_map(
        fast_shards if small else shards,
        mesh=mesh,
        in_specs=(
            P(BOTH, None),
            P(BOTH, None),
            P(BOTH, None),
            P(None, BOTH, None),
            P(None, BOTH, None),
            P(None, BOTH, None),
            P(None, BOTH),
            P(None, BOTH),
            P(None, BOTH),
            P(EX, None, HI),
            P(EX, None, HI),
            P(EX, None, HI),
            P(EX, HI, None),
            P(EX, HI, None),
            P(EX, HI, None),
            P(EX, None, None),
            P(EX, None, None),
            P(EX, None, None),
        ),
        out_specs=(
            P(BOTH, None),
            P(BOTH, None),
            P(),
            P(None, BOTH, None),
            P(None, BOTH, None),
            P(None, BOTH, None),
            P(None, BOTH),
            P(None, BOTH),
            P(None, BOTH),
            P(EX, None, HI),
            P(EX, None, HI),
            P(EX, None, HI),
            P(EX, HI, None),
            P(EX, HI, None),
            P(EX, HI, None),
            P(EX, None, None),
            P(EX, None, None),
            P(EX, None, None),
            P(None, EX),
        ),
        check_vma=False,
    )
```

time: 412 us -> 316 us (0.77)
  Pallas kernels: 363 us -> 289 us
  other arithmetic: 23.9 us -> 5.28 us
    pallas_call x3 -> x4, Pallas kernels: 363 us -> 289 us  [the longest x1 102 us: expert_layer(): pl.pallas_call(functools.partial(expert_kernel, cap), out_shape=[jax.Shap...]
    sub x4 -> x2, other arithmetic: 20.3 us -> 2.14 us  [adam_step(): return (weight - rate * update, moment, square)]
    unnamed x57 -> x41, local copies, waits for them, and re-layouts: 16.7 us -> 13.6 us
where the time goes in v2:
time: 316 us; the launch traced here: 315 us
  Pallas kernels  289 us (91%)
  local copies, waits for them, and re-layouts  15.5 us (5%)
  between operations  5.29 us (2%)
  other arithmetic  5.28 us (2%)
    pallas_call x1, Pallas kernels, expert_layer(): pl.pallas_call(functools.partial(expert_kernel, cap), out_shape=[jax.Shap...  102 us
    pallas_call x1, Pallas kernels, attend_back(): pl.pallas_call(functools.partial(reduce_kernel, cap), out_shape=[jax.Shap...  95.7 us
    pallas_call x1, Pallas kernels, attend(): pl.pallas_call(functools.partial(attend_kernel, cap), out_shape=[jax.Shap...  70.3 us
    pallas_call x1, Pallas kernels, adam_all(): pl.pallas_call(adam_kernel, grid=(steps,), out_shape=shapes, in_specs=in_...  20.9 us
    unnamed x41, local copies, waits for them, and re-layouts  13.6 us

profile of v2, /device:TPU:0, one launch (start us, length us, event | category | flops | bytes accessed | tf_op | source)
XLA Modules:
  0.0 315.0 jit_solution(4813786984728938662)
XLA Ops:
  0.7 0.7 copy.63
  1.4 0.6 pad.4.vec
  2.0 1.4 copy.37.route
  3.4 70.3 %shard_map.321 = (bf16[4,1024,1024]{2,1,0:T(8,128)(2,1)}, bf16[3,192,1024]{2,1,0:T(8,128)(2,1)}, bf16[192,1024]{1,0:T(8,128)(2,1)}, bf16[192,1024]{1,0:T(8,128)(...) custom-call(bf16[192,1024]{1,0:T(8,128)(2,1)} %tok.3, ...), custom_call_target="tpu_custom_call" | custom-call | tf_op jit(solution)/shard_map/pallas_call | solution.py:483
  73.7 102.1 %shard_map.322 = (f32[192,1024]{1,0:T(8,128)}, bf16[1024,1024]{1,0:T(8,128)(2,1)}, bf16[1024,1024]{1,0:T(8,128)(2,1)}, bf16[4,8,48,1024]{3,2,1,0:T(8,128)(2,1)},...) custom-call(bf16[192,1024]{1,0:T(8,128)(2,1)} %get-tuple-element.50.sent_in, s32[4,8,256]{2,1,0:T(8,128)} %get-tuple-element.51.placed_in.placed, ...), custom_call_target="tpu_custom_call" | custom-call | tf_op jit(solution)/shard_map/pallas_call | solution.py:858
  175.8 1.3 slice_reduce_fusion
  177.1 0.0 copy-start.13
  177.1 0.0 copy-start.4
  177.1 0.0 copy-start.5
  177.2 0.0 copy-start.6
  177.2 95.7 %shard_map.323 = (bf16[192,1024]{1,0:T(8,128)(2,1)}, bf16[192,1024]{1,0:T(8,128)(2,1)}, f32[4,32,1024]{2,1,0:T(8,128)}, f32[8,1024]{1,0:T(8,128)}, f32[8,1024]{1,0:T(8,128)}, /*index=5*/f32[8,128]{1,0:T(8,128)}) custom-call(f32[192,1024]{1,0:T(8,128)} %get-tuple-element.54.d_sum, bf16[192,1024]{1,0:T(8,128)(2,1)} %cot.3, ...), custom_call_target="tpu_custom_call" | custom-call | tf_op jit(solution)/shard_map/pallas_call | solution.py:1228
  272.8 1.3 constant_dynamic-slice_fusion
  276.7 0.6 maximum_bitcast_fusion
  277.3 1.3 reduce_sum.18
  279.3 0.0 copy-done.14
  279.4 1.3 multiply_subtract_fusion
  280.7 0.0 copy-done.11
  280.7 0.8 copy_subtract_fusion
  281.5 0.6 copy.42
  282.1 0.6 copy.43
  282.7 0.6 copy.44
  283.4 0.0 copy-done.5
  283.4 1.6 copy-done
  285.0 1.6 copy-done.1
  286.6 1.6 copy-done.2
  288.1 1.6 copy-done.3
  289.7 1.0 copy-done.7
  290.8 0.7 copy-done.8
  291.5 20.9 %shard_map.324 = (f32[1024,1024]{1,0:T(8,128)}, f32[1024,1024]{1,0:T(8,128)}, f32[1024,1024]{1,0:T(8,128)}, f32[1024,1024]{1,0:T(8,128)}, f32[1024,1024]{1,0:T(8...) custom-call(bf16[1024,1024]{1,0:T(8,128)(2,1)S(1)} %bitcast.36, ...), custom_call_target="tpu_custom_call" | custom-call | tf_op jit(solution)/shard_map/pallas_call | solution.py:1325
  312.4 0.7 copy.66
  313.1 0.0 copy-done.9
  313.1 0.7 copy.67
  (20 shorter events, 0.0 us)
Async XLA Ops:
  177.1 102.2 %copy-start.14 = (f32[2,32]{1,0:T(2,128)S(1)}, f32[2,32]{1,0:T(2,128)}, u32[]{:S(2)}) copy-start(f32[2,32]{1,0:T(2,128)} %norm_in.1) | copy-start | bytes 772
  177.1 102.2 %copy-start.15 = (f32[2,32]{1,0:T(2,128)S(1)}, f32[2,32]{1,0:T(2,128)}, u32[]{:S(2)}) copy-start(f32[2,32]{1,0:T(2,128)} %param.25) | copy-start | bytes 772
  177.1 102.2 %copy-start.16 = (f32[2,32]{1,0:T(2,128)S(1)}, f32[2,32]{1,0:T(2,128)}, u32[]{:S(2)}) copy-start(f32[2,32]{1,0:T(2,128)} %param.26) | copy-start | bytes 772
  177.1 103.6 %copy-start.11 = (f32[1,3,1024]{2,0,1:T(1,128)S(1)}, f32[1,3,1024]{2,0,1:T(1,128)}, u32[]{:S(2)}) copy-start(f32[1,3,1024]{2,0,1:T(1,128)} %param.33) | copy-start | bytes 36868
  177.1 103.6 %copy-start.12 = (f32[1,3,1024]{2,0,1:T(1,128)S(1)}, f32[1,3,1024]{2,0,1:T(1,128)}, u32[]{:S(2)}) copy-start(f32[1,3,1024]{2,0,1:T(1,128)} %param.34) | copy-start | bytes 36868
  177.1 103.6 %copy-start.13 = (f32[1,3,1024]{2,0,1:T(1,128)S(1)}, f32[1,3,1024]{2,0,1:T(1,128)}, u32[]{:S(2)}) copy-start(f32[1,3,1024]{2,0,1:T(1,128)} %param.35) | copy-start | bytes 36868
  177.1 106.2 %copy-start.4 = (f32[4,32,1024]{2,1,0:T(8,128)S(1)}, f32[4,32,1024]{2,1,0:T(8,128)}, u32[]{:S(2)}) copy-start(f32[4,32,1024]{2,1,0:T(8,128)} %w_own.1) | copy-start | bytes 1572868
  177.1 106.2 %copy-start.5 = (f32[4,32,1024]{2,1,0:T(8,128)S(1)}, f32[4,32,1024]{2,1,0:T(8,128)}, u32[]{:S(2)}) copy-start(f32[4,32,1024]{2,1,0:T(8,128)} %param.22) | copy-start | bytes 1572868
  177.2 106.2 %copy-start.6 = (f32[4,32,1024]{2,1,0:T(8,128)S(1)}, f32[4,32,1024]{2,1,0:T(8,128)}, u32[]{:S(2)}) copy-start(f32[4,32,1024]{2,1,0:T(8,128)} %param.23) | copy-start | bytes 1572868
  283.4 1.6 copy-start
  285.0 1.6 copy-start.1
  286.5 1.6 copy-start.2
  288.1 1.6 copy-start.3
  289.7 1.0 copy-start.7
  290.8 0.7 copy-start.8
  291.4 20.9 %copy-start.10 = (bf16[192,1024]{1,0:T(8,128)(2,1)S(1)}, bf16[192,1024]{1,0:T(8,128)(2,1)}, u32[]{:S(2)}) copy-start(bf16[192,1024]{1,0:T(8,128)(2,1)} %get-tuple-element.125) | copy-start | bytes 1179652
  291.5 21.7 %copy-start.9 = (bf16[192,1024]{1,0:T(8,128)(2,1)S(1)}, bf16[192,1024]{1,0:T(8,128)(2,1)}, u32[]{:S(2)}) copy-start(bf16[192,1024]{1,0:T(8,128)(2,1)} %get-tuple-element.126) | copy-start | bytes 1179652

commit v3 on v2

--- a/solution.py
+++ b/solution.py
@@ -153,12 +153,15 @@
     def __init__(self, wire, at, name, slot):
         self.wire, self.at, self.name, self.slot = wire, at, name, slot
 
-    def begin(self, own=None):
+    def begin(self, own=None, outer=1, inner=True):
         at = self.at
         here = self.slot(at.z)
         own = here if own is None else own
-        self.wire.send(own, here, at.partner, (self.name, 1))
-        self.wire.send(own, here, at.mirror, (self.name, 2), at.middle)
+        if outer:
+            when = {1: None, 2: at.ends, 3: at.middle}[outer]
+            self.wire.send(own, here, at.partner, (self.name, 1), when)
+        if inner:
+            self.wire.send(own, here, at.mirror, (self.name, 2), at.middle)
 
     def take(self, i, when=None):
         at = self.at
@@ -240,8 +243,8 @@
     cot_zero,
     w_low,
     wfull,
-    norm_sum,
-    norm_got,
+    norm_low,
+    pieces,
     qkv,
     normed,
     ctx,
@@ -265,58 +268,68 @@
     fetch.start(cot, cot_raw.at[z])
     w_low[...] = w_own[...].astype(jnp.bfloat16)
     lanes = norm_in.shape[1]
-    columns = lax.broadcasted_iota(jnp.int32, (lanes, width), 1)
-    offset = columns - (e * depth + z) * lanes
-    ours = lax.broadcasted_iota(jnp.int32, (lanes, width), 0) == offset
+    offset = lax.broadcasted_iota(jnp.int32, (lanes, 128), 1) - z * lanes
+    ours = lax.broadcasted_iota(jnp.int32, (lanes, 128), 0) == offset
     low = norm_in[...].astype(jnp.bfloat16)
-    norm_sum[0] = jnp.zeros((16, width), jnp.bfloat16)
-    norm_sum[0, 0:2, :] = dot(low, jnp.where(ours, 1.0, 0.0).astype(jnp.bfloat16)).astype(
+    norm_low[...] = jnp.zeros((16, 128), jnp.bfloat16)
+    norm_low[0:2, :] = dot(low, jnp.where(ours, 1.0, 0.0).astype(jnp.bfloat16)).astype(
         jnp.bfloat16
     )
     at.meet()
 
     def block(g, who, zz):
+        if g == 2:
+            return pieces.at[who, zz]
         first, mats = groups[g]
         start = pl.multiple_of((who * depth + zz) * shard, shard)
         return wfull.at[pl.ds(first, mats), pl.ds(start, shard)]
 
     def mine(g):
+        if g == 2:
+            return norm_low
         first, mats = groups[g]
         return w_low.at[pl.ds(first, mats)]
 
-    lines = [Line(wire, at, g, lambda zz, g=g: block(g, e, zz)) for g in range(2)]
+    lines = [Line(wire, at, g, lambda zz, g=g: block(g, e, zz)) for g in range(3)]
+    lines[2].begin(mine(2))
     lines[0].begin(mine(0))
-    norm_to = [at.partner, at.mirror, at.over_x, at.over_y, at.twin]
-    norm_copy = wire.send(norm_sum.at[0], norm_got.at[0], norm_to[0])
-    own = [fetch.start(mine(g), block(g, e, z)) for g in range(2)]
+    lines[1].begin(mine(1), outer=2, inner=False)
+    cots = Line(wire, at, "cot", lambda zz: cot_raw.at[zz])
+    cots.begin(cot, outer=2, inner=False)
+    own = [fetch.start(mine(g), block(g, e, z)) for g in range(3)]
     to_x, to_y, to_far, to_twin = {}, {}, {}, {}
 
-    def norm_next(k):
-        norm_copy.wait_recv()
-        norm_sum[k] = norm_sum[k - 1] + norm_got[k - 1]
-        return wire.send(norm_sum.at[k], norm_got.at[k], norm_to[k])
-
-    def plane(g, i):
+    def over_x(g, i):
         here = block(g, e, at.line[i])
-        if i == 0:
-            fetch.done(own[g])
-        else:
-            lines[g].take(i)
         to_x[g, i] = wire.send(here, here, at.over_x)
+        to_twin[g, i, 0] = wire.send(here, here, at.twin)
+
+    def over_y(g, i):
+        here = block(g, e, at.line[i])
         to_y[g, i] = wire.send(here, here, at.over_y)
-        to_twin[g, i, 0] = wire.send(here, here, at.twin)
 
     def forward(g, i):
         zz = at.line[i]
-        from_x, from_y = block(g, at.ex, zz), block(g, at.ey, zz)
-        to_x[g, i].wait_recv()
         if i in (0, 3):
-            to_far[g, i] = wire.send(from_x, from_x, at.over_y)
-        to_twin[g, i, 1] = wire.send(from_x, from_x, at.twin)
-        to_y[g, i].wait_recv()
-        if i in (1, 2):
-            to_far[g, i] = wire.send(from_y, from_y, at.over_x)
-        to_twin[g, i, 2] = wire.send(from_y, from_y, at.twin)
+            to_x[g, i].wait_recv()
+            block_x = block(g, at.ex, zz)
+            to_far[g, i] = wire.send(block_x, block_x, at.over_y)
+            to_twin[g, i, 1] = wire.send(block_x, block_x, at.twin)
+        else:
+            to_y[g, i].wait_recv()
+            block_y = block(g, at.ey, zz)
+            to_far[g, i] = wire.send(block_y, block_y, at.over_x)
+            to_twin[g, i, 1] = wire.send(block_y, block_y, at.twin)
+
+    def side(g, i):
+        zz = at.line[i]
+        if i in (0, 3):
+            to_y[g, i].wait_recv()
+            there = block(g, at.ey, zz)
+        else:
+            to_x[g, i].wait_recv()
+            there = block(g, at.ex, zz)
+        to_twin[g, i, 2] = wire.send(there, there, at.twin)
 
     def far(g, i):
         to_far[g, i].wait_recv()
@@ -328,37 +341,78 @@
             for k in range(4):
                 to_twin[g, i, k].wait_recv()
 
-    plane(0, 0)
+    def both(step, i):
+        step(2, i)
+        step(0, i)
+
+    def take(i):
+        lines[2].take(i)
+        lines[0].take(i)
+
+    for copy in (own[2], own[0]):
+        fetch.done(copy)
+    both(over_x, 0)
+    both(over_y, 0)
+    wide_r = lax.broadcasted_iota(jnp.int32, (count, count), 0)
+    wide_c = lax.broadcasted_iota(jnp.int32, (count, count), 1)
+    route_row = route[...].astype(jnp.float32)
+    route_col = jnp.sum(jnp.where(wide_r == wide_c, route_row, 0.0), axis=1, keepdims=True)
     lane = lax.broadcasted_iota(jnp.int32, (count, 128), 1)
-    chosen = jnp.where(route[...] == lane, 1.0, 0.0)
+    chosen = jnp.where(route_col.astype(jnp.int32) == lane, 1.0, 0.0)
     rows_i = lax.broadcasted_iota(jnp.int32, (count, count), 0)
     cols_i = lax.broadcasted_iota(jnp.int32, (count, count), 1)
     lower = jnp.where(rows_i >= cols_i, 1.0, 0.0)
     running = dot(lower.astype(jnp.bfloat16), chosen.astype(jnp.bfloat16))
     rank = jnp.sum((running - 1.0) * chosen, axis=1, keepdims=True)
-    column = route[...].astype(jnp.float32) * float(cap) + rank
-    wide_r = lax.broadcasted_iota(jnp.int32, (count, 256), 0)
-    wide_c = lax.broadcasted_iota(jnp.int32, (count, 256), 1)
-    row = jnp.sum(jnp.where(wide_r == wide_c, column + 1.0, 0.0), axis=0, keepdims=True) - 1.0
+    column = route_col * float(cap) + rank
+    row = jnp.sum(jnp.where(wide_r == wide_c, column, 0.0), axis=0, keepdims=True)
+    row = jnp.concatenate([row, jnp.full((1, 256 - count), -1.0, jnp.float32)], axis=1)
     placed[z] = jnp.broadcast_to(row, (8, 256)).astype(jnp.int32)
-    plane(0, 1)
-    norm_copy = norm_next(1)
-    forward(0, 0)
-    plane(0, 2)
-    norm_copy = norm_next(2)
-    forward(0, 1)
-    far(0, 0)
-    plane(0, 3)
-    lines[1].begin(mine(1))
+    take(1)
+    both(over_x, 1)
+    both(over_y, 1)
     build(stage, cot, placed[z, 0:1, :count])
-    norm_copy = norm_next(3)
-    far(0, 1)
-    forward(0, 2)
-    plane(1, 0)
-    plane(1, 1)
-    norm_copy = norm_next(4)
-    norm_copy.wait_recv()
-    gain_rows = norm_sum[4] + norm_got[4]
+    both(forward, 0)
+    take(2)
+    lines[1].begin(mine(1), outer=3)
+    both(forward, 1)
+    both(over_y, 2)
+    take(3)
+    lines[1].take(1, at.middle)
+    lines[1].take(2, at.middle)
+    both(over_x, 3)
+    both(over_x, 2)
+    both(over_y, 3)
+    both(side, 0)
+    both(side, 1)
+    both(far, 0)
+    both(far, 1)
+    lines[1].take(3, at.middle)
+    cots.begin(cot, outer=0)
+    both(forward, 2)
+    both(forward, 3)
+    cots.take(1, at.middle)
+    places = Line(wire, at, "place", lambda zz: placed.at[zz])
+    places.begin()
+    fetch.done(own[1])
+    for i in range(depth):
+        if i:
+            lines[1].take(i, at.ends)
+        over_x(1, i)
+        over_y(1, i)
+    both(side, 3)
+    both(side, 2)
+    both(far, 2)
+    both(far, 3)
+    finish(2)
+    cots.take(2, at.middle)
+    gain_rows = jnp.concatenate(
+        [
+            sum([pieces[who, zz] for zz in range(1, depth)], pieces[who, 0])
+            for who in range(8)
+        ],
+        axis=1,
+    )
     tally = jnp.concatenate(
         [
             jnp.broadcast_to(jnp.sum(chosen, axis=0, keepdims=True), (16, 128)),
@@ -384,36 +438,29 @@
         )
 
     fetch.start(normed, normed_out)
-    far(0, 2)
-    forward(0, 3)
-    plane(1, 2)
-    plane(1, 3)
-    cots = Line(wire, at, "cot", lambda zz: cot_raw.at[zz])
-    places = Line(wire, at, "place", lambda zz: placed.at[zz])
-    cots.begin(cot)
-    places.begin()
-    far(0, 3)
     finish(0)
     fetch.start(wfull.at[pl.ds(0, 3)], w_out.at[pl.ds(0, 3)])
     tiles = width // 256
 
-    @pl.loop(0, 3 * tiles)
-    def _(i):
-        m = lax.div(i, tiles)
-        cols = tile(lax.rem(i, tiles))
-        qkv[m, :, cols] = dot(normed[...], wfull[m, :, cols]).astype(jnp.bfloat16)
-
-    fetch.start(qkv, qkv_out)
-    for i in range(depth):
-        forward(1, i)
-    places.take(1)
-    cots.take(1)
-    places.take(2, at.middle)
-    cots.take(2, at.middle)
     slots_out = [
         wire.send(stage.at[at.across(k)], cot_zero.at[k], (at.across(k), z)) for k in range(1, 8)
     ]
     fetch.start(stage.at[e], cot_zero.at[0])
+    def project(i):
+        m = lax.div(i, tiles)
+        cols = tile(lax.rem(i, tiles))
+        qkv[m, :, cols] = dot(normed[...], wfull[m, :, cols]).astype(jnp.bfloat16)
+
+    pl.loop(0, tiles)(project)
+    for i in range(depth):
+        forward(1, i)
+    places.take(1)
+    cots.take(3, at.middle)
+    pl.loop(tiles, 3 * tiles)(project)
+    fetch.start(qkv, qkv_out)
+    for i in range(depth):
+        side(1, i)
+    places.take(2, at.middle)
     causal = rows_i >= cols_i
     left = lax.broadcasted_iota(jnp.int32, (count, 128), 1) < 64
     scaling = jnp.asarray(64 ** (-0.5), jnp.bfloat16)
@@ -434,14 +481,12 @@
             halves.append(dot(probs.astype(jnp.bfloat16), values))
         ctx[:, cols] = jnp.where(left, halves[0], halves[1]).astype(jnp.bfloat16)
 
-    pl.loop(0, width // 256)(pair)
+    pl.loop(0, 6)(pair)
     for i in range(depth):
         far(1, i)
     places.take(2, at.ends)
-    cots.take(2, at.ends)
     places.take(3, at.middle)
-    cots.take(3, at.middle)
-    pl.loop(width // 256, width // 128)(pair)
+    pl.loop(6, width // 128)(pair)
     fetch.start(ctx, ctx_out)
     finish(1)
     fetch.start(wfull.at[pl.ds(3, 1)], w_out.at[pl.ds(3, 1)])
@@ -456,6 +501,7 @@
     fetch.start(sent, sent_out)
     fetch.start(resid, resid_out)
     places.take(3, at.ends)
+    cots.take(2, at.ends)
     cots.take(3, at.ends)
     fetch.start(placed, placed_out)
     for copy in slots_out:
@@ -467,7 +513,7 @@
 def attend(cap, tokens, w_own, norm_own, routes, cotangent):
     count, width = tokens.shape
     bf, full = jnp.bfloat16, jnp.float32
-    copies = 128
+    copies = 176
     shapes = [
         ((4, width, width), bf),
         ((3, count, width), bf),
@@ -488,8 +534,8 @@
         scratch_shapes=[
             pltpu.VMEM((4, w_own.shape[1], width), bf),
             pltpu.VMEM((4, width, width), bf),
-            pltpu.VMEM((5, 16, width), bf),
-            pltpu.VMEM((5, 16, width), bf),
+            pltpu.VMEM((16, 128), bf),
+            pltpu.VMEM((8, 4, 16, 128), bf),
             pltpu.VMEM((3, count, width), bf),
             pltpu.VMEM((count, width), bf),
             pltpu.VMEM((count, width), bf),
@@ -579,6 +625,25 @@
             self.add(1, 3)
 
         wire.send(self.part(1), self.got.at[0], at.partner, (name, 1))
+
+    def relay_far(self):
+        at, wire, name = self.at, self.wire, self.name
+        far = self.got.at[3]
+        pl.when(at.middle)(lambda: wire.arrived((name, 4), far, at.mirror))
+        wire.send(far, self.got.at[0], at.partner, (name, 1), at.middle)
+
+    def finish(self):
+        at, wire, name = self.at, self.wire, self.name
+
+        @pl.when(at.ends)
+        def _():
+            wire.arrived((name, 1), self.got.at[0], at.partner)
+            self.add(0, 0)
+
+        @pl.when(at.middle)
+        def _():
+            wire.arrived((name, 5), self.got.at[4], at.mirror)
+            self.add(0, 4)
 
     def last(self):
         self.wire.arrived((self.name, 1), self.got.at[0], self.at.partner)
@@ -913,6 +978,7 @@
     norm_out,
     vec_out,
     square_out,
+    norm_shard,
     wfull,
     qkv,
     normed,
@@ -933,6 +999,7 @@
     back,
     part,
     z_in,
+    near_in,
     small,
     small_in,
     square,
@@ -949,7 +1016,7 @@
     half = column // 2
     wire = Wire(send_sem, recv_sem)
     fetch = Fetch(local_sem)
-    in_delta = {i: fetch.start(delta_in.at[i], delta.at[i]) for i in (3, 2, 1, 0)}
+    in_delta = {i: fetch.start(delta_in.at[i], delta.at[i]) for i in (1, 3, 2, 0)}
     in_w = {m: fetch.start(w_in.at[m], wfull.at[m]) for m in (3, 2, 1, 0)}
     in_qkv = fetch.start(qkv_in, qkv)
     in_normed = fetch.start(normed_in, normed)
@@ -958,7 +1025,8 @@
     home = Home(wire, at, "home", lambda i: part.at[i], z_in)
 
     def give(i):
-        fetch.done(in_delta[i])
+        if i in in_delta:
+            fetch.done(in_delta.pop(i))
         ret[i] = [
             wire.send(delta.at[i, k], back.at[i, e], (at.across(k), z)) for k in range(1, planes)
         ]
@@ -977,7 +1045,7 @@
             stage[m, lax.div(i, 4), lax.rem(lax.div(i, 2), 2), lax.rem(i, 2)] = value
 
     other = 1 - at.core
-    first, second, third, fourth = {}, {}, {}, {}
+    first, second, third, fourth, fifth = {}, {}, {}, {}, {}
 
     def to_core(m):
         first[m] = wire.send(stage.at[m, :, :, other], twin_in.at[m], at.twin)
@@ -1009,18 +1077,27 @@
         done[m, 0:2] = (x_in[m, at.y] + x_last[m]).reshape(pair)
         third[m][1].wait_recv()
         done[m, 2:4] = (y_in[m, at.x] + y_last[m]).reshape(pair)
-        fourth[m] = [
-            wire.send(done.at[m, at.mates[k][1]], z_last.at[m, k - 1], at.mates[k])
-            for k in range(1, depth)
-        ]
+        theirs = at.partner[1]
+        fourth[m] = (
+            wire.send(done.at[m, theirs], z_last.at[m, 0], at.partner),
+            wire.send(done.at[m, 3 - theirs], z_last.at[m, 1], at.partner),
+        )
+
+    def cross(m):
+        fourth[m][1].wait_recv()
+        done[m, 3 - z] = done[m, 3 - z] + z_last[m, 1]
+        fifth[m] = wire.send(done.at[m, 3 - z], z_last.at[m, 2], at.mirror)
 
     def own(m):
+        fourth[m][0].wait_recv()
+        fifth[m].wait_recv()
         total = done[m, z].astype(jnp.float32)
-        for k in range(1, depth):
-            fourth[m][k - 1].wait_recv()
-            total = total + z_last[m, k - 1].astype(jnp.float32)
+        for k in (0, 2):
+            total = total + z_last[m, k].astype(jnp.float32)
         shard_out[m] = total
 
+    fetch.done(in_delta[1])
+    near_copy = wire.send(delta.at[1], near_in, at.partner)
     give(3)
     value = cot[...].astype(jnp.float32) + d_sum[...]
     d_resid[...] = value
@@ -1077,6 +1154,8 @@
     pl.loop(0, width // 256)(pair)
     give(2)
     pl.loop(width // 256, width // 128)(pair)
+    collect(3)
+    home.push(3)
     fetch.done(in_normed)
     weight_grad(2, normed, d_qkv.at[2])
     to_core(2)
@@ -1086,10 +1165,11 @@
     to_plane(2)
     weight_grad(0, normed, d_qkv.at[0])
     to_core(0)
-    collect(3)
-    home.push(3)
+    home.pass_on(3)
     to_owner(3)
     to_plane(1)
+    collect(2)
+    home.push(2)
     for m in (2, 1, 0):
         fetch.done(in_w[m])
 
@@ -1121,54 +1201,65 @@
         d_in = scale * (dh - mean_one - hat * mean_two)
         token_grad[i : i + 64, :] = (d_resid[i : i + 64, :] + d_in).astype(jnp.bfloat16)
     mine = small.at[0]
-    mine[...] = jnp.zeros((16, width), jnp.float32)
+    mine[...] = jnp.zeros((8, width), jnp.float32)
     mine[2:3, :] = gains[2:3, :].astype(jnp.float32)
     mine[0:1, :] = jnp.sum(d_gain, axis=0, keepdims=True)
     mine[1:2, :] = jnp.sum(d_bias, axis=0, keepdims=True)
     for k in range(3):
-        mine[8 + k : 9 + k, :] = jnp.sum(vec_part[k], axis=0, keepdims=True)
-    small_to = [at.partner, at.mirror, at.over_x, at.over_y, at.twin]
-
-    def small_send(k):
-        rows = pl.ds(0, 16 if k < 2 else 8)
-        return wire.send(small.at[k, rows], small_in.at[k, rows], small_to[k])
-
-    def small_next(k, copy):
-        copy.wait_recv()
-        rows = slice(0, 16 if k < 3 else 8)
-        small[k, rows] = small[k - 1, rows] + small_in[k - 1, rows]
-        if k == 2:
-            vec_out[...] = small[2, 8:16]
-        return small_send(k) if k < 5 else None
-
-    flow = small_send(0)
+        mine[3 + k : 4 + k, :] = jnp.sum(vec_part[k], axis=0, keepdims=True)
+    small_copy = wire.send(mine, small.at[1], at.partner)
+    to_last(2)
+    home.relay_far()
+    home.pass_on(2)
+    near_copy.wait_recv()
+    fetch.done(in_delta.pop(0))
+
+    @pl.loop(0, planes)
+    def _(k):
+        delta[0, k] = (delta[0, k].astype(jnp.float32) + near_in[k].astype(jnp.float32)).astype(
+            jnp.bfloat16
+        )
+
     to_plane(0)
-    to_last(2)
-    collect(2)
-    home.push(2)
-    home.pass_on(3)
-    flow = small_next(1, flow)
-    give(1)
+    cross(3)
+    small_copy.wait_recv()
+    small[2] = small[0] + small[1]
+    small_copy = wire.send(small.at[2], small.at[3], at.mirror)
     to_last(1)
     to_owner(2)
-    flow = small_next(2, flow)
     own(3)
-    home.pass_on(2)
+    to_last(0)
+    cross(2)
+    small_copy.wait_recv()
+    total = small[2] + small[3]
+    vec_out[...] = total
+    small_in[e] = total
+    spot = small_in.at[e]
+    plane_copies = [wire.send(spot, spot, (at.across(k), z)) for k in range(1, planes)]
     give(0)
-    to_last(0)
-    flow = small_next(3, flow)
     to_owner(1)
     own(2)
-    flow = small_next(4, flow)
     to_owner(0)
-    collect(1)
-    home.near()
-    small_next(5, flow)
-    norm_out[...] = small[5, 0:8]
+    cross(1)
+    cross(0)
     own(1)
-    collect(0)
+    for copy in plane_copies:
+        copy.wait_recv()
+    total = small_in[0]
+    for k in range(1, planes):
+        total = total + small_in[k]
+    norm_out[...] = total
     norm_rows = norm_out[0:2, :]
-    vec_rows = vec_out[0:3, :]
+    mine = norm_out[0:2, tile(e, 128)]
+    lanes = norm_shard.shape[1]
+    value = mine[:, 0:lanes]
+    for k in range(1, depth):
+        value = jnp.where(z == k, mine[:, k * lanes : (k + 1) * lanes], value)
+    norm_shard[...] = value
+    lane = lax.broadcasted_iota(jnp.int32, (1, 128), 1)
+    routed = jnp.sum(jnp.where(lane == e, norm_out[2:3, 0:128], 0.0), keepdims=True)
+    gates = jnp.sum(scal[0:8, 0:1], keepdims=True) - 0.5 * (depth * planes * cap - routed)
+    vec_rows = vec_out[3:6, :]
     squares = jnp.sum(norm_rows * norm_rows, axis=0, keepdims=True) / (planes * depth) + jnp.sum(
         vec_rows * vec_rows, axis=0, keepdims=True
     ) / depth
@@ -1184,12 +1275,15 @@
     square[0, e] = local + fold(square_lanes(shard_out[0]))
     spot = square.at[0, e]
     copies = [wire.send(spot, spot, (at.across(k), z)) for k in range(1, planes)]
-    home.last()
+    collect(0)
+    home.finish()
 
     @pl.loop(0, width // 256)
     def _(j):
         cols = tile(j)
-        block_out[:, cols] = (resid[:, cols] + home.total(cols)).astype(jnp.bfloat16)
+        block_out[:, cols] = (resid[:, cols] + part[0, :, cols].astype(jnp.float32)).astype(
+            jnp.bfloat16
+        )
 
     for copy in copies:
         copy.wait_recv()
@@ -1204,7 +1298,11 @@
     total = square[1, 0]
     for d in range(1, depth):
         total = total + square[1, d]
-    square_out[...] = total
+    norm = jnp.sqrt(jnp.sum(total, keepdims=True))
+    which = lax.broadcasted_iota(jnp.int32, (8, 128), 0)
+    stats = jnp.where(which == 0, routed / (count * depth), gates / routed)
+    clip = clip_level / jnp.maximum(norm, clip_level)
+    square_out[...] = jnp.where(which < 2, stats, jnp.where(which == 2, norm, clip))
     wire.drain()
     fetch.drain()
 
@@ -1224,6 +1322,7 @@
         ((8, width), full),
         ((8, width), full),
         ((8, 128), full),
+        ((2, width // 32), full),
     ]
     return pl.pallas_call(
         functools.partial(reduce_kernel, cap),
@@ -1233,7 +1332,7 @@
         + [VMEM_SPEC] * 4
         + [ANY_SPEC]
         + [VMEM_SPEC] * 3,
-        out_specs=[VMEM_SPEC] * 6,
+        out_specs=[VMEM_SPEC] * 7,
         scratch_shapes=[
             pltpu.VMEM((4, width, width), bf),
             pltpu.VMEM((3, count, width), bf),
@@ -1255,8 +1354,9 @@
             pltpu.VMEM((depth, 8, cap, width), bf),
             pltpu.VMEM((depth, count, width), bf),
             pltpu.VMEM((5, count, width), bf),
-            pltpu.VMEM((6, 16, width), full),
-            pltpu.VMEM((5, 16, width), full),
+            pltpu.VMEM((8, cap, width), bf),
+            pltpu.VMEM((4, 8, width), full),
+            pltpu.VMEM((8, 8, width), full),
             pltpu.VMEM((2, 8, 8, 128), full),
             pltpu.SemaphoreType.DMA((copies,)),
             pltpu.SemaphoreType.DMA((copies,)),
@@ -1266,6 +1366,15 @@
             collective_id=2, has_side_effects=True, vmem_limit_bytes=62 << 20
         ),
     )(*args)
+
+
+def adam_quick(weight, first, second, grad, clip_factor, rate, decay):
+    clipped = grad * clip_factor
+    moment = beta_one * first + (1.0 - beta_one) * clipped
+    square = beta_two * second + (1.0 - beta_two) * clipped * clipped
+    root = jnp.sqrt(square * (1.0 / (1.0 - beta_two**STEP))) + adam_eps
+    step = moment * (rate / (1.0 - beta_one**STEP)) / root
+    return (weight * (1.0 - rate * decay) - step, moment, square)
 
 
 def adam_kernel(
@@ -1281,7 +1390,7 @@
     attn_first,
     attn_second,
     attn_grad,
-    squares,
+    facts,
     up_new,
     up_moment,
     up_square,
@@ -1292,15 +1401,14 @@
     attn_moment,
     attn_square,
 ):
-    norm = jnp.sqrt(jnp.sum(squares[...], keepdims=True))
-    clip = clip_level / jnp.maximum(norm, clip_level)
+    clip = facts[3:4, 0:1]
     sets = [
         (up, up_first, up_second, up_grad, up_new, up_moment, up_square),
         (down, down_first, down_second, down_grad, down_new, down_moment, down_square),
         (attn, attn_first, attn_second, attn_grad, attn_new, attn_moment, attn_square),
     ]
     for weight, first, second, grad, new, moment, square in sets:
-        got = adam_step(
+        got = adam_quick(
             weight[...].astype(jnp.float32),
             first[...],
             second[...],
@@ -1312,8 +1420,8 @@
         new[...], moment[...], square[...] = got
 
 
-def adam_all(up, down, attn, squares):
-    steps = 16
+def adam_all(up, down, attn, facts):
+    steps = 8
     full = jnp.float32
     in_specs, out_specs, shapes, aliases = [], [], [], {}
     for group in (up, down, attn):
@@ -1326,10 +1434,10 @@
         adam_kernel,
         grid=(steps,),
         out_shape=shapes,
-        in_specs=in_specs + [pl.BlockSpec(squares.shape, lambda i: (0, 0))],
+        in_specs=in_specs + [pl.BlockSpec(facts.shape, lambda i: (0, 0))],
         out_specs=out_specs,
-        compiler_params=pltpu.CompilerParams(vmem_limit_bytes=40 << 20),
-    )(*up, *down, *attn, squares)
+        compiler_params=pltpu.CompilerParams(vmem_limit_bytes=60 << 20),
+    )(*up, *down, *attn, facts)
 
 
 def shards(
@@ -1631,20 +1739,17 @@
     vector_second,
 ):
     experts = lax.axis_size(EX)
-    depth = lax.axis_size(HI)
     count, width = tokens.shape
     cap = 2 * count // experts
     shard = attn_weight.shape[1]
-    lanes = norm_param.shape[1]
-    place = lax.axis_index(EX) * depth + lax.axis_index(HI)
     w_full, qkv, normed, ctx, resid, sent, placed, gains, cot_raw, cot_zero = attend(
-        cap, tokens, attn_weight, norm_param, routes, cotangent
+        cap, tokens, attn_weight, norm_param, routes.reshape(1, count), cotangent
     )
     vec = jnp.pad(expert_vector[0], ((0, 5), (0, 0)))
     d_sum, grad_up, grad_down, delta, vec_part, scal = expert_layer(
         cap, sent, placed, cot_raw, cot_zero, up_weight[0], down_weight[0], vec
     )
-    block_out, token_grad, attn_shard, norm_grads, vec_grads, squares = attend_back(
+    block_out, token_grad, attn_shard, norm_grads, vec_grads, facts, norm_shard = attend_back(
         cap,
         shard,
         d_sum,
@@ -1661,21 +1766,16 @@
         vec_part,
         scal,
     )
-    here = lax.axis_index(EX)
-    routed = lax.dynamic_slice(norm_grads, (2, here), (1, 1))[0, 0]
-    empty = depth * experts * cap - routed
-    gate_total = jnp.sum(scal[0:8, 0]) - 0.5 * empty
-    expert_stats = jnp.stack([routed / (count * depth), gate_total / routed])[:, None]
-    norm_shard = lax.dynamic_slice(norm_grads, (0, place * lanes), (2, lanes))
-    vector_grad = vec_grads[None, 0:3]
-    grad_norm = jnp.sqrt(jnp.sum(squares))
-    clip_factor = clip_level / jnp.maximum(grad_norm, clip_level)
+    expert_stats = facts[0:2, 0:1]
+    grad_norm = facts[2, 0]
+    clip_factor = facts[3, 0]
+    vector_grad = vec_grads[None, 3:6]
     flat = lambda v: v.reshape(-1, v.shape[-1])
     new = adam_all(
         [flat(v) for v in (up_weight, up_first, up_second, grad_up)],
         [flat(v) for v in (down_weight, down_first, down_second, grad_down)],
         [flat(v) for v in (attn_weight, attn_first, attn_second, attn_shard)],
-        squares,
+        facts,
     )
     up_new = [v.reshape(up_weight.shape) for v in new[0:3]]
     down_new = [v.reshape(down_weight.shape) for v in new[3:6]]

time: 316 us -> 285 us (0.902)
  Pallas kernels: 289 us -> 276 us
  local copies, waits for them, and re-layouts: 15.5 us -> 5.84 us
  between operations: 5.29 us -> 0.81 us
  other arithmetic: 5.28 us -> 1.93 us
    pallas_call x1, Pallas kernels: 95.7 us -> 86.2 us  [attend_back(): pl.pallas_call(functools.partial(reduce_kernel, cap), out_shape=[jax.Shap...]
    unnamed x41 -> x29, local copies, waits for them, and re-layouts: 13.6 us -> 4.7 us
    pallas_call x1, Pallas kernels: 70.3 us -> 64.9 us  [attend(): pl.pallas_call(functools.partial(attend_kernel, cap), out_shape=[jax.Shap...]
where the time goes in v3:
time: 285 us; the launch traced here: 284 us
  Pallas kernels  276 us (97%)
  local copies, waits for them, and re-layouts  5.84 us (2%)
    pallas_call x1, Pallas kernels, expert_layer(): pl.pallas_call(functools.partial(expert_kernel, cap), out_shape=[jax.Shap...  103 us
    pallas_call x1, Pallas kernels, attend_back(): pl.pallas_call(functools.partial(reduce_kernel, cap), out_shape=[jax.Shap...  86.2 us
    pallas_call x1, Pallas kernels, attend(): pl.pallas_call(functools.partial(attend_kernel, cap), out_shape=[jax.Shap...  64.9 us
    pallas_call x1, Pallas kernels, adam_all(): pl.pallas_call(adam_kernel, grid=(steps,), out_shape=shapes, in_specs=in_...  21.4 us

profile of v3, /device:TPU:0, one launch (start us, length us, event | category | flops | bytes accessed | tf_op | source)
XLA Modules:
  0.0 284.3 jit_solution(8761065975298459082)
XLA Ops:
  0.7 64.9 %shard_map.321 = (bf16[4,1024,1024]{2,1,0:T(8,128)(2,1)}, bf16[3,192,1024]{2,1,0:T(8,128)(2,1)}, bf16[192,1024]{1,0:T(8,128)(2,1)}, bf16[192,1024]{1,0:T(8,128)(...) custom-call(bf16[192,1024]{1,0:T(8,128)(2,1)} %tok.3, ...), custom_call_target="tpu_custom_call" | custom-call | tf_op jit(solution)/shard_map/pallas_call | solution.py:529
  65.5 0.7 copy.63
  66.2 0.6 pad.4.vec
  66.9 103.3 %shard_map.322 = (f32[192,1024]{1,0:T(8,128)}, bf16[1024,1024]{1,0:T(8,128)(2,1)}, bf16[1024,1024]{1,0:T(8,128)(2,1)}, bf16[4,8,48,1024]{3,2,1,0:T(8,128)(2,1)},...) custom-call(bf16[192,1024]{1,0:T(8,128)(2,1)} %get-tuple-element.50.sent_in, s32[4,8,256]{2,1,0:T(8,128)} %get-tuple-element.51.placed_in.placed, ...), custom_call_target="tpu_custom_call" | custom-call | tf_op jit(solution)/shard_map/pallas_call | solution.py:923
  170.1 86.2 %shard_map.323 = (bf16[192,1024]{1,0:T(8,128)(2,1)}, bf16[192,1024]{1,0:T(8,128)(2,1)}, f32[4,32,1024]{2,1,0:T(8,128)}, f32[8,1024]{1,0:T(8,128)}, f32[8,1024]{1...) custom-call(f32[192,1024]{1,0:T(8,128)} %get-tuple-element.54.d_sum, bf16[192,1024]{1,0:T(8,128)(2,1)} %cot.3, ...), custom_call_target="tpu_custom_call" | custom-call | tf_op jit(solution)/shard_map/pallas_call | solution.py:1327
  256.3 0.0 copy-start.5
  256.3 0.0 copy-start.2
  256.3 0.0 copy-start.3
  256.3 0.0 copy-start.4
  256.3 0.0 copy-start.6
  256.4 0.0 copy-start.7
  256.4 0.0 copy-start.8
  256.4 0.0 copy-start.9
  256.4 0.0 copy-start.10
  256.4 0.0 copy-start.1
  256.4 0.0 copy-start
  256.4 21.4 %shard_map.324 = (f32[1024,1024]{1,0:T(8,128)}, f32[1024,1024]{1,0:T(8,128)}, f32[1024,1024]{1,0:T(8,128)}, f32[1024,1024]{1,0:T(8,128)}, f32[1024,1024]{1,0:T(8...) custom-call(bf16[1024,1024]{1,0:T(8,128)(2,1)} %bitcast.34, ...), custom_call_target="tpu_custom_call" | custom-call | tf_op jit(solution)/shard_map/pallas_call | solution.py:1433
  277.9 0.0 copy-done.5
  277.9 0.5 fusion.7
  278.4 0.0 copy-done.2
  278.4 0.0 copy-done.3
  278.4 0.0 copy-done.4
  278.4 0.0 copy-done.6
  278.4 0.7 copy_subtract_fusion
  279.1 0.6 copy.41
  279.7 0.6 copy.42
  280.3 0.6 copy.43
  280.9 0.0 copy-done.10
  281.0 1.2 multiply_subtract_fusion
  282.2 0.6 copy.44
  282.8 0.7 copy.66
  283.5 0.7 copy.67
  (6 shorter events, 0.0 us)
Async XLA Ops:
  256.3 21.6 %copy-start.5 = (f32[8,128]{1,0:T(8,128)S(1)}, f32[8,128]{1,0:T(8,128)}, u32[]{:S(2)}) copy-start(f32[8,128]{1,0:T(8,128)} %get-tuple-element.66.facts) | copy-start | bytes 12292
  256.3 22.1 %copy-start.2 = (f32[1,3,1024]{2,0,1:T(1,128)S(1)}, f32[1,3,1024]{2,0,1:T(1,128)}, u32[]{:S(2)}) copy-start(f32[1,3,1024]{2,0,1:T(1,128)} %param.33) | copy-start | bytes 36868
  256.3 22.1 %copy-start.3 = (f32[1,3,1024]{2,0,1:T(1,128)S(1)}, f32[1,3,1024]{2,0,1:T(1,128)}, u32[]{:S(2)}) copy-start(f32[1,3,1024]{2,0,1:T(1,128)} %param.34) | copy-start | bytes 36868
  256.3 22.1 %copy-start.4 = (f32[1,3,1024]{2,0,1:T(1,128)S(1)}, f32[1,3,1024]{2,0,1:T(1,128)}, u32[]{:S(2)}) copy-start(f32[1,3,1024]{2,0,1:T(1,128)} %param.35) | copy-start | bytes 36868
  256.3 22.1 %copy-start.6 = (f32[8,1024]{1,0:T(8,128)S(1)}, f32[8,1024]{1,0:T(8,128)}, u32[]{:S(2)}) copy-start(f32[8,1024]{1,0:T(8,128)} %get-tuple-element.80) | copy-start | bytes 98308
  256.4 24.6 %copy-start.7 = (f32[2,32]{1,0:T(2,128)S(1)}, f32[2,32]{1,0:T(2,128)}, u32[]{:S(2)}) copy-start(f32[2,32]{1,0:T(2,128)} %norm_in.1) | copy-start | bytes 772
  256.4 24.6 %copy-start.8 = (f32[2,32]{1,0:T(2,128)S(1)}, f32[2,32]{1,0:T(2,128)}, u32[]{:S(2)}) copy-start(f32[2,32]{1,0:T(2,128)} %param.25) | copy-start | bytes 772
  256.4 24.6 %copy-start.9 = (f32[2,32]{1,0:T(2,128)S(1)}, f32[2,32]{1,0:T(2,128)}, u32[]{:S(2)}) copy-start(f32[2,32]{1,0:T(2,128)} %param.26) | copy-start | bytes 772
  256.4 24.6 %copy-start.10 = (f32[2,32]{1,0:T(2,128)S(1)}, f32[2,32]{1,0:T(2,128)}, u32[]{:S(2)}) copy-start(f32[2,32]{1,0:T(2,128)} %get-tuple-element.73) | copy-start | bytes 772
  256.4 26.4 %copy-start.1 = (bf16[192,1024]{1,0:T(8,128)(2,1)S(1)}, bf16[192,1024]{1,0:T(8,128)(2,1)}, u32[]{:S(2)}) copy-start(bf16[192,1024]{1,0:T(8,128)(2,1)} %get-tuple-element.127) | copy-start | bytes 1179652
  256.4 27.1 %copy-start = (bf16[192,1024]{1,0:T(8,128)(2,1)S(1)}, bf16[192,1024]{1,0:T(8,128)(2,1)}, u32[]{:S(2)}) copy-start(bf16[192,1024]{1,0:T(8,128)(2,1)} %get-tuple-element.128) | copy-start | bytes 1179652

commit v4 on v3

--- a/solution.py
+++ b/solution.py
@@ -481,12 +481,12 @@
             halves.append(dot(probs.astype(jnp.bfloat16), values))
         ctx[:, cols] = jnp.where(left, halves[0], halves[1]).astype(jnp.bfloat16)
 
-    pl.loop(0, 6)(pair)
+    pl.loop(0, 6, unroll=2)(pair)
     for i in range(depth):
         far(1, i)
     places.take(2, at.ends)
     places.take(3, at.middle)
-    pl.loop(6, width // 128)(pair)
+    pl.loop(6, width // 128, unroll=2)(pair)
     fetch.start(ctx, ctx_out)
     finish(1)
     fetch.start(wfull.at[pl.ds(3, 1)], w_out.at[pl.ds(3, 1)])
@@ -593,65 +593,79 @@
     def __init__(self, wire, at, name, part, got):
         self.wire, self.at, self.name = wire, at, name
         self.part, self.got = part, got
-
-    def add(self, i, k):
+        half = got.shape[1] // 2
+        self.halves = [pl.ds(0, half), pl.ds(half, half)]
+
+    def add(self, i, k, half):
         part = self.part(i)
-        part[...] = (part[...].astype(jnp.float32) + self.got[k].astype(jnp.float32)).astype(
-            jnp.bfloat16
-        )
+        part[half, :] = (
+            part[half, :].astype(jnp.float32) + self.got[k, half, :].astype(jnp.float32)
+        ).astype(jnp.bfloat16)
+
+    def arrived(self, tag, k, n, device):
+        half = self.halves[n]
+        self.wire.arrived((self.name, tag, n), self.got.at[k, half], device)
+
+    def send(self, src, k, n, device, tag, when=None):
+        half = self.halves[n]
+        self.wire.send(src.at[half], self.got.at[k, half], device, (self.name, tag, n), when)
 
     def push(self, i):
-        here = self.part(i)
+        for n in range(2):
+            self.send(self.part(i), i - 1, n, self.at.partner, i, self.at.ends)
+
+    def pass_on(self, i):
         at = self.at
-        self.wire.send(here, self.got.at[i - 1], at.partner, (self.name, i), at.ends)
-
-    def pass_on(self, i):
-        at, wire, name = self.at, self.wire, self.name
-
-        @pl.when(at.middle)
-        def _():
-            wire.arrived((name, i), self.got.at[i - 1], at.partner)
-            self.add(i, i - 1)
-
         k = {3: 3, 2: 4}[i]
-        wire.send(self.part(i), self.got.at[k], at.mirror, (name, k + 1), at.middle)
+        for n, half in enumerate(self.halves):
+
+            @pl.when(at.middle)
+            def _():
+                self.arrived(i, i - 1, n, at.partner)
+                self.add(i, i - 1, half)
+
+            self.send(self.part(i), k, n, at.mirror, k + 1, at.middle)
 
     def near(self):
-        at, wire, name = self.at, self.wire, self.name
-
-        @pl.when(at.middle)
-        def _():
-            wire.arrived((name, 4), self.got.at[3], at.mirror)
-            self.add(1, 3)
-
-        wire.send(self.part(1), self.got.at[0], at.partner, (name, 1))
+        at = self.at
+        for n, half in enumerate(self.halves):
+
+            @pl.when(at.middle)
+            def _():
+                self.arrived(4, 3, n, at.mirror)
+                self.add(1, 3, half)
+
+            self.send(self.part(1), 0, n, at.partner, 1)
 
     def relay_far(self):
-        at, wire, name = self.at, self.wire, self.name
-        far = self.got.at[3]
-        pl.when(at.middle)(lambda: wire.arrived((name, 4), far, at.mirror))
-        wire.send(far, self.got.at[0], at.partner, (name, 1), at.middle)
+        at = self.at
+        for n in range(2):
+            pl.when(at.middle)(lambda: self.arrived(4, 3, n, at.mirror))
+            self.send(self.got.at[3], 0, n, at.partner, 1, at.middle)
 
     def finish(self):
-        at, wire, name = self.at, self.wire, self.name
-
-        @pl.when(at.ends)
-        def _():
-            wire.arrived((name, 1), self.got.at[0], at.partner)
-            self.add(0, 0)
-
-        @pl.when(at.middle)
-        def _():
-            wire.arrived((name, 5), self.got.at[4], at.mirror)
-            self.add(0, 4)
+        at = self.at
+        for n, half in enumerate(self.halves):
+
+            @pl.when(at.ends)
+            def _():
+                self.arrived(1, 0, n, at.partner)
+                self.add(0, 0, half)
+
+            @pl.when(at.middle)
+            def _():
+                self.arrived(5, 4, n, at.mirror)
+                self.add(0, 4, half)
 
     def last(self):
-        self.wire.arrived((self.name, 1), self.got.at[0], self.at.partner)
-
-        @pl.when(self.at.middle)
-        def _():
-            self.wire.arrived((self.name, 5), self.got.at[4], self.at.mirror)
-            self.add(0, 4)
+        at = self.at
+        for n, half in enumerate(self.halves):
+            self.arrived(1, 0, n, at.partner)
+
+            @pl.when(at.middle)
+            def _():
+                self.arrived(5, 4, n, at.mirror)
+                self.add(0, 4, half)
 
     def total(self, cols):
         return self.part(0)[:, cols].astype(jnp.float32) + self.got[0, :, cols].astype(jnp.float32)
@@ -718,16 +732,13 @@
     vec_part[...] = jnp.zeros_like(vec_part)
     scal[...] = jnp.zeros_like(scal)
     fetch.done(in_placed)
-    centroid = lambda: vec[0:1, :]
+    centroid = lambda: vec[0]
     row_copies, cot_copies, ret_copies = {}, {}, {}
 
-    def exchange(i, dst):
-        copies = [
-            wire.send(stage.at[i, at.across(k)], dst.at[i, k], (at.across(k), z))
-            for k in range(1, planes)
+    def exchange(i, dst, s, offsets=range(1, planes)):
+        return [
+            wire.send(stage.at[s, at.across(k)], dst.at[i, k], (at.across(k), z)) for k in offsets
         ]
-        dst[i, 0] = stage[i, e]
-        return copies
 
     def slot_row(i):
         return placed[at.line[i], 0:1, :count]
@@ -735,20 +746,24 @@
     def rows_out(i):
         source = sent if i == 0 else raw.at[at.line[i]]
         build(stage.at[i], source, slot_row(i))
-        row_copies[i] = exchange(i, rows)
-
-    def cots_out(i):
-        for copy in row_copies[i]:
-            wire.left(copy)
-        build(stage.at[i], cot_line.at[at.line[i]], slot_row(i))
-        cot_copies[i] = exchange(i, cots)
+        row_copies[i] = exchange(i, rows, i)
+        rows[i, 0] = stage[i, e]
+
+    def cots_out(i, s, offsets):
+        if i not in cot_copies:
+            for copy in row_copies[s]:
+                wire.left(copy)
+            build(stage.at[s], cot_line.at[at.line[i]], slot_row(i))
+            cot_copies[i] = []
+            cots[i, 0] = stage[s, e]
+        cot_copies[i] += exchange(i, cots, s, offsets)
 
     def forward(i):
         for copy in row_copies[i]:
             copy.wait_recv()
-        gain, bias = vec[1:2, :], vec[2:3, :]
-
-        @pl.loop(0, planes)
+        gain, bias = vec[1], vec[2]
+
+        @pl.loop(0, planes, unroll=2)
         def _(k):
             r = rows[i, k].astype(jnp.float32)
             logit = jnp.sum(r * centroid(), axis=-1, keepdims=True)
@@ -766,9 +781,9 @@
         if i == 0:
             fetch.done(in_up)
 
-        @pl.loop(0, units // 256)
+        @pl.loop(0, units // 512)
         def _(j):
-            cols = tile(j)
+            cols = tile(j, 512)
             value, rate = gelu_pair(dot(xn[i], up[:, cols]))
             act[i, :, cols] = value.astype(jnp.bfloat16)
             slope[i, :, cols] = rate.astype(jnp.bfloat16)
@@ -776,11 +791,11 @@
         if i == 0:
             fetch.done(in_down)
 
-        @pl.loop(0, width // 256)
+        @pl.loop(0, width // 512)
         def _(j):
-            cols = tile(j)
+            cols = tile(j, 512)
             branch = dot(act[i], down[:, cols])
-            wide = spread(gate[i].reshape(slots, 128), 256)
+            wide = spread(gate[i].reshape(slots, 128), 512)
             value = (wide * branch).astype(jnp.bfloat16)
             for k in range(planes):
                 delta[i, k, :, cols] = value[k * cap : (k + 1) * cap]
@@ -790,10 +805,8 @@
     def backward(i):
         for copy in cot_copies[i]:
             copy.wait_recv()
-        if i == 0:
-            wire.left(cot_copies[1][0])
-
-        @pl.loop(0, planes)
+
+        @pl.loop(0, planes, unroll=2)
         def _(k):
             c = cots[i, k].astype(jnp.float32)
             g = gate[i, k]
@@ -803,22 +816,23 @@
             cots[i, k] = (c * spread(g, width)).astype(jnp.bfloat16)
             vec_part[0] += fold(rows[i, k].astype(jnp.float32) * spread(dl, width))
 
-        @pl.loop(0, units // 256)
+        @pl.loop(0, units // 512)
         def _(j):
-            cols = tile(j)
+            cols = tile(j, 512)
             d_act = dot(cots[i].reshape(slots, width), down[cols, :], 1, 1)
             slope[i, :, cols] = (d_act * slope[i, :, cols].astype(jnp.float32)).astype(
                 jnp.bfloat16
             )
 
-        @pl.loop(0, width // 256)
+    def backward_in(i):
+        @pl.loop(0, width // 512)
         def _(j):
-            cols = tile(j)
+            cols = tile(j, 512)
             value = dot(slope[i], up[cols, :], 1, 1)
             for k in range(planes):
                 d_xn[k, :, cols] = value[k * cap : (k + 1) * cap]
 
-        @pl.loop(0, planes)
+        @pl.loop(0, planes, unroll=2)
         def _(k):
             r = rows[i, k].astype(jnp.float32)
             average = jnp.mean(r, axis=-1, keepdims=True)
@@ -829,12 +843,13 @@
             dx = d_xn[k]
             vec_part[1] += fold(dx * hat)
             vec_part[2] += fold(dx)
-            dh = dx * vec[1:2, :]
+            dh = dx * vec[1]
             first = jnp.mean(dh, axis=-1, keepdims=True)
             second = jnp.mean(dh * hat, axis=-1, keepdims=True)
             d_in = scale * (dh - first - hat * second)
             d_slots[i, k] = (d_in + spread(d_logit[i, k], width) * centroid()).astype(jnp.bfloat16)
 
+    def give(i):
         ret_copies[i] = [
             wire.send(d_slots.at[i, k], back.at[i, e], (at.across(k), z))
             for k in range(1, planes)
@@ -849,10 +864,10 @@
         unslot(slot_row(i), back.at[i], part.at[i])
 
     def weight_grad(lhs, rhs, index, out):
-        @pl.loop(0, lhs.shape[-1] // 256)
+        @pl.loop(0, lhs.shape[-1] // 512)
         def _(j):
-            cols = tile(j)
-            left = lhs[:, :, cols].reshape(depth * slots, 256)
+            cols = tile(j, 512)
+            left = lhs[:, :, cols].reshape(depth * slots, 512)
             value = dot(left, rhs[...].reshape(depth * slots, rhs.shape[-1]), 0, 0)
             scal[8:16] += fold(square_lanes(value))
             g_stage[index, cols, :] = value.astype(jnp.bfloat16)
@@ -863,6 +878,8 @@
     line.take(1)
     line.take(2, at.middle)
     rows_out(1)
+    fetch.done(in_cot)
+    cots_out(3, 0, (2, 4, 6))
     forward(0)
     line.take(2, at.ends)
     line.take(3, at.middle)
@@ -872,25 +889,32 @@
     rows_out(3)
     fetch.done(in_zero)
     cot_copies[0] = []
-    cot_copies[1] = [wire.send(cots.at[0], cots.at[1], at.partner)]
-    fetch.done(in_cot)
+    cot_copies[1] = [wire.send(cot_zero, cots.at[1], at.partner)]
+    cots_out(3, 0, (3, 5, 7, 1))
     forward(2)
-    cots_out(3)
+    cots_out(2, 1, range(1, planes))
     forward(3)
-    cots_out(2)
     backward(3)
+    backward_in(3)
+    give(3)
     backward(2)
+    backward_in(2)
+    give(2)
+    backward(1)
+    backward_in(1)
+    give(1)
+    backward(0)
     collect(3)
     home.push(3)
-    backward(1)
+    backward_in(0)
+    give(0)
     collect(2)
     home.push(2)
     home.pass_on(3)
-    backward(0)
+    weight_grad(act, cots, 0, g_down)
     collect(1)
+    home.near()
     home.pass_on(2)
-    home.near()
-    weight_grad(act, cots, 0, g_down)
     weight_grad(xn, slope, 1, g_up)
     collect(0)
     home.last()
@@ -910,7 +934,7 @@
     depth = 4
     bf, full = jnp.bfloat16, jnp.float32
     slots = 8 * cap
-    copies = 3 * 7 * depth + 32
+    copies = 3 * 7 * depth + 56
     shapes = [
         ((count, width), full),
         ((width, units), bf),
@@ -1151,9 +1175,9 @@
         d_qkv[1, :, cols] = ((got[0][1] + got[1][1]) * scaling).astype(jnp.bfloat16)
         d_qkv[2, :, cols] = (got[0][2] + got[1][2]).astype(jnp.bfloat16)
 
-    pl.loop(0, width // 256)(pair)
+    pl.loop(0, width // 256, unroll=2)(pair)
     give(2)
-    pl.loop(width // 256, width // 128)(pair)
+    pl.loop(width // 256, width // 128, unroll=2)(pair)
     collect(3)
     home.push(3)
     fetch.done(in_normed)
@@ -1377,38 +1401,14 @@
     return (weight * (1.0 - rate * decay) - step, moment, square)
 
 
-def adam_kernel(
-    up,
-    up_first,
-    up_second,
-    up_grad,
-    down,
-    down_first,
-    down_second,
-    down_grad,
-    attn,
-    attn_first,
-    attn_second,
-    attn_grad,
-    facts,
-    up_new,
-    up_moment,
-    up_square,
-    down_new,
-    down_moment,
-    down_square,
-    attn_new,
-    attn_moment,
-    attn_square,
-):
+def adam_kernel(*refs):
+    ins, outs = refs[:23], refs[23:]
+    facts, block_in, token_in = ins[20:23]
     clip = facts[3:4, 0:1]
-    sets = [
-        (up, up_first, up_second, up_grad, up_new, up_moment, up_square),
-        (down, down_first, down_second, down_grad, down_new, down_moment, down_square),
-        (attn, attn_first, attn_second, attn_grad, attn_new, attn_moment, attn_square),
-    ]
-    for weight, first, second, grad, new, moment, square in sets:
-        got = adam_quick(
+    for k in range(3):
+        weight, first, second, grad = ins[4 * k : 4 * k + 4]
+        new, moment, square = outs[3 * k : 3 * k + 3]
+        new[...], moment[...], square[...] = adam_quick(
             weight[...].astype(jnp.float32),
             first[...],
             second[...],
@@ -1417,27 +1417,67 @@
             rate_matrix,
             decay_rate,
         )
-        new[...], moment[...], square[...] = got
-
-
-def adam_all(up, down, attn, facts):
+
+    @pl.when(pl.program_id(0) == 0)
+    def _():
+        weight, first, second, grad = ins[12:16]
+        for k in range(3):
+            got = adam_quick(
+                weight[k], first[k], second[k], grad[3 + k : 4 + k, :], clip, rate_vector, 0.0
+            )
+            for out, value in zip(outs[9:12], got):
+                out[k] = value
+        weight, first, second, grad = ins[16:20]
+        got = adam_quick(
+            weight[...], first[...], second[...], grad[...], clip, rate_vector, 0.0
+        )
+        for out, value in zip(outs[12:15], got):
+            out[...] = value
+        outs[15][...] = block_in[...]
+        outs[16][...] = token_in[...]
+        outs[17][...] = facts[2:3, 0:1]
+        outs[18][...] = jnp.concatenate([facts[0:1, 0:1], facts[1:2, 0:1]], axis=1)
+
+
+def adam_all(up, down, attn, vector, norm, facts, block_out, token_grad):
     steps = 8
     full = jnp.float32
-    in_specs, out_specs, shapes, aliases = [], [], [], {}
+
+    def whole(shape):
+        return pl.BlockSpec(shape, lambda i: (0,) * len(shape))
+
+    def cut(v):
+        return pl.BlockSpec((v.shape[0] // steps, v.shape[1]), lambda i: (i, 0))
+
+    args, in_specs, out_specs, shapes = [], [], [], []
     for group in (up, down, attn):
-        rows, width = group[0].shape
-        spec = pl.BlockSpec((rows // steps, width), lambda i: (i, 0))
-        in_specs += [spec] * 4
-        out_specs += [spec] * 3
-        shapes += [jax.ShapeDtypeStruct((rows, width), full)] * 3
+        args += group
+        in_specs += [cut(v) for v in group]
+        out_specs += [cut(group[0])] * 3
+        shapes += [jax.ShapeDtypeStruct(group[0].shape, full)] * 3
+    for group in (vector, norm):
+        args += group
+        in_specs += [whole(v.shape) for v in group]
+        out_specs += [whole(group[0].shape)] * 3
+        shapes += [jax.ShapeDtypeStruct(group[0].shape, full)] * 3
+    args += [facts]
+    in_specs += [whole(facts.shape)]
+    for v in (block_out, token_grad):
+        args += [v]
+        in_specs += [whole(v.shape)]
+        out_specs += [whole(v.shape)]
+        shapes += [jax.ShapeDtypeStruct(v.shape, v.dtype)]
+    for shape in ((1, 1), (1, 2)):
+        out_specs += [whole(shape)]
+        shapes += [jax.ShapeDtypeStruct(shape, full)]
     return pl.pallas_call(
         adam_kernel,
         grid=(steps,),
         out_shape=shapes,
-        in_specs=in_specs + [pl.BlockSpec(facts.shape, lambda i: (0, 0))],
+        in_specs=in_specs,
         out_specs=out_specs,
         compiler_params=pltpu.CompilerParams(vmem_limit_bytes=60 << 20),
-    )(*up, *down, *attn, facts)
+    )(*args)
 
 
 def shards(
@@ -1745,9 +1785,9 @@
     w_full, qkv, normed, ctx, resid, sent, placed, gains, cot_raw, cot_zero = attend(
         cap, tokens, attn_weight, norm_param, routes.reshape(1, count), cotangent
     )
-    vec = jnp.pad(expert_vector[0], ((0, 5), (0, 0)))
+    rows = lambda v: v.reshape(3, 1, width)
     d_sum, grad_up, grad_down, delta, vec_part, scal = expert_layer(
-        cap, sent, placed, cot_raw, cot_zero, up_weight[0], down_weight[0], vec
+        cap, sent, placed, cot_raw, cot_zero, up_weight[0], down_weight[0], rows(expert_vector)
     )
     block_out, token_grad, attn_shard, norm_grads, vec_grads, facts, norm_shard = attend_back(
         cap,
@@ -1766,26 +1806,25 @@
         vec_part,
         scal,
     )
-    expert_stats = facts[0:2, 0:1]
-    grad_norm = facts[2, 0]
-    clip_factor = facts[3, 0]
-    vector_grad = vec_grads[None, 3:6]
     flat = lambda v: v.reshape(-1, v.shape[-1])
     new = adam_all(
         [flat(v) for v in (up_weight, up_first, up_second, grad_up)],
         [flat(v) for v in (down_weight, down_first, down_second, grad_down)],
         [flat(v) for v in (attn_weight, attn_first, attn_second, attn_shard)],
+        [rows(v) for v in (expert_vector, vector_first, vector_second)] + [vec_grads],
+        [norm_param, norm_first, norm_second, norm_shard],
         facts,
+        block_out,
+        token_grad,
     )
     up_new = [v.reshape(up_weight.shape) for v in new[0:3]]
     down_new = [v.reshape(down_weight.shape) for v in new[3:6]]
     attn_new = [v.reshape(attn_weight.shape) for v in new[6:9]]
-    norm_new = adam_step(
-        norm_param, norm_first, norm_second, norm_shard, clip_factor, rate_vector, 0.0
-    )
-    vector_new = adam_step(
-        expert_vector, vector_first, vector_second, vector_grad, clip_factor, rate_vector, 0.0
-    )
+    vector_new = [v.reshape(expert_vector.shape) for v in new[9:12]]
+    norm_new = new[12:15]
+    block_out, token_grad = new[15:17]
+    grad_norm = new[17].reshape(())
+    expert_stats = new[18].reshape(2, 1)
     return (
         block_out,
         token_grad,

time: 285 us -> 273 us (0.958)
  local copies, waits for them, and re-layouts: 5.84 us -> 0 us
  Pallas kernels: 276 us -> 272 us
    unnamed x29 -> x0, local copies, waits for them, and re-layouts: 4.7 us -> none
    pallas_call x1, Pallas kernels: 21.4 us -> 25.8 us  [adam_all(): pl.pallas_call(adam_kernel, grid=(steps,), out_shape=shapes, in_specs=in_...]
    pallas_call x1, Pallas kernels: 86.2 us -> 82.2 us  [attend_back(): pl.pallas_call(functools.partial(reduce_kernel, cap), out_shape=[jax.Shap...]
    pallas_call x1, Pallas kernels: 103 us -> 99.4 us  [expert_layer(): pl.pallas_call(functools.partial(expert_kernel, cap), out_shape=[jax.Shap...]
where the time goes in v4:
time: 273 us; the launch traced here: 272 us
  Pallas kernels  272 us (100%)
    pallas_call x1, Pallas kernels, expert_layer(): pl.pallas_call(functools.partial(expert_kernel, cap), out_shape=[jax.Shap...  99.4 us
    pallas_call x1, Pallas kernels, attend_back(): pl.pallas_call(functools.partial(reduce_kernel, cap), out_shape=[jax.Shap...  82.2 us
    pallas_call x1, Pallas kernels, attend(): pl.pallas_call(functools.partial(attend_kernel, cap), out_shape=[jax.Shap...  64.2 us
    pallas_call x1, Pallas kernels, adam_all(): pl.pallas_call(adam_kernel, grid=(steps,), out_shape=shapes, in_specs=in_...  25.8 us

profile of v4, /device:TPU:0, one launch (start us, length us, event | category | flops | bytes accessed | tf_op | source)
XLA Modules:
  0.0 272.5 jit_solution(11750478650560452926)
XLA Ops:
  0.7 64.2 %shard_map.321 = (bf16[4,1024,1024]{2,1,0:T(8,128)(2,1)}, bf16[3,192,1024]{2,1,0:T(8,128)(2,1)}, bf16[192,1024]{1,0:T(8,128)(2,1)}, bf16[192,1024]{1,0:T(8,128)(...) custom-call(bf16[192,1024]{1,0:T(8,128)(2,1)} %tok.3, ...), custom_call_target="tpu_custom_call" | custom-call | tf_op jit(solution)/shard_map/pallas_call | solution.py:529
  64.8 99.4 %shard_map.322 = (f32[192,1024]{1,0:T(8,128)}, bf16[1024,1024]{1,0:T(8,128)(2,1)}, bf16[1024,1024]{1,0:T(8,128)(2,1)}, bf16[4,8,48,1024]{3,2,1,0:T(8,128)(2,1)},...) custom-call(bf16[192,1024]{1,0:T(8,128)(2,1)} %get-tuple-element.60.sent_in, s32[4,8,256]{2,1,0:T(8,128)} %get-tuple-element.61.placed_in.placed, ...), custom_call_target="tpu_custom_call" | custom-call | tf_op jit(solution)/shard_map/pallas_call | solution.py:947
  164.3 82.2 %shard_map.323 = (bf16[192,1024]{1,0:T(8,128)(2,1)}, bf16[192,1024]{1,0:T(8,128)(2,1)}, f32[4,32,1024]{2,1,0:T(8,128)}, f32[8,1024]{1,0:T(8,128)}, f32[8,1024]{1...) custom-call(f32[192,1024]{1,0:T(8,128)} %get-tuple-element.66.d_sum, bf16[192,1024]{1,0:T(8,128)(2,1)} %cot.3, ...), custom_call_target="tpu_custom_call" | custom-call | tf_op jit(solution)/shard_map/pallas_call | solution.py:1351
  246.5 25.8 %shard_map.324 = (f32[1024,1024]{1,0:T(8,128)}, f32[1024,1024]{1,0:T(8,128)}, f32[1024,1024]{1,0:T(8,128)}, f32[1024,1024]{1,0:T(8,128)}, f32[1024,1024]{1,0:T(8...) custom-call(bf16[1024,1024]{1,0:T(8,128)(2,1)} %bitcast.29, ...), custom_call_target="tpu_custom_call" | custom-call | tf_op jit(solution)/shard_map/pallas_call | solution.py:1473

commit v5 on v4

--- a/solution.py
+++ b/solution.py
@@ -404,8 +404,9 @@
     both(side, 2)
     both(far, 2)
     both(far, 3)
+    cots.take(2, at.middle)
     finish(2)
-    cots.take(2, at.middle)
+    cots.take(3, at.middle)
     gain_rows = jnp.concatenate(
         [
             sum([pieces[who, zz] for zz in range(1, depth)], pieces[who, 0])
@@ -442,20 +443,19 @@
     fetch.start(wfull.at[pl.ds(0, 3)], w_out.at[pl.ds(0, 3)])
     tiles = width // 256
 
+    def project(i):
+        m = lax.div(i, tiles)
+        cols = tile(lax.rem(i, tiles))
+        qkv[m, :, cols] = dot(normed[...], wfull[m, :, cols]).astype(jnp.bfloat16)
+
+    pl.loop(0, tiles)(project)
+    for i in range(depth):
+        forward(1, i)
     slots_out = [
         wire.send(stage.at[at.across(k)], cot_zero.at[k], (at.across(k), z)) for k in range(1, 8)
     ]
     fetch.start(stage.at[e], cot_zero.at[0])
-    def project(i):
-        m = lax.div(i, tiles)
-        cols = tile(lax.rem(i, tiles))
-        qkv[m, :, cols] = dot(normed[...], wfull[m, :, cols]).astype(jnp.bfloat16)
-
-    pl.loop(0, tiles)(project)
-    for i in range(depth):
-        forward(1, i)
     places.take(1)
-    cots.take(3, at.middle)
     pl.loop(tiles, 3 * tiles)(project)
     fetch.start(qkv, qkv_out)
     for i in range(depth):

time: 273 us -> 267 us (0.978)
  Pallas kernels: 272 us -> 266 us
    pallas_call x1, Pallas kernels: 64.2 us -> 60.7 us  [attend(): pl.pallas_call(functools.partial(attend_kernel, cap), out_shape=[jax.Shap...]
where the time goes in v5:
time: 267 us
  Pallas kernels  266 us (100%)
    pallas_call x1, Pallas kernels, expert_layer(): pl.pallas_call(functools.partial(expert_kernel, cap), out_shape=[jax.Shap...  97.1 us
    pallas_call x1, Pallas kernels, attend_back(): pl.pallas_call(functools.partial(reduce_kernel, cap), out_shape=[jax.Shap...  82.3 us
    pallas_call x1, Pallas kernels, attend(): pl.pallas_call(functools.partial(attend_kernel, cap), out_shape=[jax.Shap...  60.7 us
    pallas_call x1, Pallas kernels, adam_all(): pl.pallas_call(adam_kernel, grid=(steps,), out_shape=shapes, in_specs=in_...  25.8 us

profile of v5, /device:TPU:0, one launch (start us, length us, event | category | flops | bytes accessed | tf_op | source)
XLA Modules:
  0.0 266.8 jit_solution(13383350381341106997)
XLA Ops:
  0.7 60.7 %shard_map.321 = (bf16[4,1024,1024]{2,1,0:T(8,128)(2,1)}, bf16[3,192,1024]{2,1,0:T(8,128)(2,1)}, bf16[192,1024]{1,0:T(8,128)(2,1)}, bf16[192,1024]{1,0:T(8,128)(...) custom-call(bf16[192,1024]{1,0:T(8,128)(2,1)} %tok.3, ...), custom_call_target="tpu_custom_call" | custom-call | tf_op jit(solution)/shard_map/pallas_call | solution.py:529
  61.4 97.1 %shard_map.322 = (f32[192,1024]{1,0:T(8,128)}, bf16[1024,1024]{1,0:T(8,128)(2,1)}, bf16[1024,1024]{1,0:T(8,128)(2,1)}, bf16[4,8,48,1024]{3,2,1,0:T(8,128)(2,1)},...) custom-call(bf16[192,1024]{1,0:T(8,128)(2,1)} %get-tuple-element.60.sent_in, s32[4,8,256]{2,1,0:T(8,128)} %get-tuple-element.61.placed_in.placed, ...), custom_call_target="tpu_custom_call" | custom-call | tf_op jit(solution)/shard_map/pallas_call | solution.py:947
  158.5 82.3 %shard_map.323 = (bf16[192,1024]{1,0:T(8,128)(2,1)}, bf16[192,1024]{1,0:T(8,128)(2,1)}, f32[4,32,1024]{2,1,0:T(8,128)}, f32[8,1024]{1,0:T(8,128)}, f32[8,1024]{1...) custom-call(f32[192,1024]{1,0:T(8,128)} %get-tuple-element.66.d_sum, bf16[192,1024]{1,0:T(8,128)(2,1)} %cot.3, ...), custom_call_target="tpu_custom_call" | custom-call | tf_op jit(solution)/shard_map/pallas_call | solution.py:1351
  240.8 25.8 %shard_map.324 = (f32[1024,1024]{1,0:T(8,128)}, f32[1024,1024]{1,0:T(8,128)}, f32[1024,1024]{1,0:T(8,128)}, f32[1024,1024]{1,0:T(8,128)}, f32[1024,1024]{1,0:T(8...) custom-call(bf16[1024,1024]{1,0:T(8,128)(2,1)} %bitcast.29, ...), custom_call_target="tpu_custom_call" | custom-call | tf_op jit(solution)/shard_map/pallas_call | solution.py:1473

commit v6 on v5

--- a/solution.py
+++ b/solution.py
@@ -441,11 +441,11 @@
     fetch.start(normed, normed_out)
     finish(0)
     fetch.start(wfull.at[pl.ds(0, 3)], w_out.at[pl.ds(0, 3)])
-    tiles = width // 256
+    tiles = width // 512
 
     def project(i):
         m = lax.div(i, tiles)
-        cols = tile(lax.rem(i, tiles))
+        cols = tile(lax.rem(i, tiles), 512)
         qkv[m, :, cols] = dot(normed[...], wfull[m, :, cols]).astype(jnp.bfloat16)
 
     pl.loop(0, tiles)(project)
@@ -481,7 +481,7 @@
             halves.append(dot(probs.astype(jnp.bfloat16), values))
         ctx[:, cols] = jnp.where(left, halves[0], halves[1]).astype(jnp.bfloat16)
 
-    pl.loop(0, 6, unroll=2)(pair)
+    pl.loop(0, 6, unroll=3)(pair)
     for i in range(depth):
         far(1, i)
     places.take(2, at.ends)
@@ -493,7 +493,7 @@
 
     @pl.loop(0, tiles)
     def _(i):
-        cols = tile(i)
+        cols = tile(i, 512)
         value = tok[:, cols].astype(jnp.float32) + dot(ctx[...], wfull[3, :, cols])
         resid[:, cols] = value
         sent[:, cols] = value.astype(jnp.bfloat16)
@@ -1062,7 +1062,7 @@
         unslot(placed[at.line[i], 0:1, :count], back.at[i], part.at[i])
 
     def weight_grad(m, left_ref, right):
-        @pl.loop(0, planes)
+        @pl.loop(0, planes, unroll=2)
         def _(i):
             cols = pl.ds(pl.multiple_of(i * column, column), column)
             value = dot(left_ref[:, cols], right[...], 0, 0).astype(jnp.bfloat16)
@@ -1130,9 +1130,9 @@
     to_core(3)
     fetch.done(in_w[3])
 
-    @pl.loop(0, width // 256)
+    @pl.loop(0, width // 512)
     def _(j):
-        cols = tile(j)
+        cols = tile(j, 512)
         d_ctx[:, cols] = dot(d_proj[...], wfull[3, cols, :], 1, 1).astype(jnp.bfloat16)
 
     to_plane(3)
@@ -1175,9 +1175,9 @@
         d_qkv[1, :, cols] = ((got[0][1] + got[1][1]) * scaling).astype(jnp.bfloat16)
         d_qkv[2, :, cols] = (got[0][2] + got[1][2]).astype(jnp.bfloat16)
 
-    pl.loop(0, width // 256, unroll=2)(pair)
+    pl.loop(0, width // 256, unroll=4)(pair)
     give(2)
-    pl.loop(width // 256, width // 128, unroll=2)(pair)
+    pl.loop(width // 256, width // 128, unroll=4)(pair)
     collect(3)
     home.push(3)
     fetch.done(in_normed)
@@ -1197,9 +1197,9 @@
     for m in (2, 1, 0):
         fetch.done(in_w[m])
 
-    @pl.loop(0, width // 256)
+    @pl.loop(0, width // 512)
     def _(j):
-        cols = tile(j)
+        cols = tile(j, 512)
         d_norm[:, cols] = (
             dot(d_qkv[0], wfull[0, cols, :], 1, 1)
             + dot(d_qkv[1], wfull[1, cols, :], 1, 1)

time: 267 us -> 267 us (level)
  no operation moved by 1% of the time
where the time goes in v6:
time: 267 us; the launch traced here: 266 us
  Pallas kernels  266 us (100%)
    pallas_call x1, Pallas kernels, expert_layer(): pl.pallas_call(functools.partial(expert_kernel, cap), out_shape=[jax.Shap...  97.2 us
    pallas_call x1, Pallas kernels, attend_back(): pl.pallas_call(functools.partial(reduce_kernel, cap), out_shape=[jax.Shap...  82.3 us
    pallas_call x1, Pallas kernels, attend(): pl.pallas_call(functools.partial(attend_kernel, cap), out_shape=[jax.Shap...  60.4 us
    pallas_call x1, Pallas kernels, adam_all(): pl.pallas_call(adam_kernel, grid=(steps,), out_shape=shapes, in_specs=in_...  25.8 us

profile of v6, /device:TPU:0, one launch (start us, length us, event | category | flops | bytes accessed | tf_op | source)
XLA Modules:
  0.0 266.5 jit_solution(16556023103438913612)
XLA Ops:
  0.7 60.4 %shard_map.321 = (bf16[4,1024,1024]{2,1,0:T(8,128)(2,1)}, bf16[3,192,1024]{2,1,0:T(8,128)(2,1)}, bf16[192,1024]{1,0:T(8,128)(2,1)}, bf16[192,1024]{1,0:T(8,128)(...) custom-call(bf16[192,1024]{1,0:T(8,128)(2,1)} %tok.3, ...), custom_call_target="tpu_custom_call" | custom-call | tf_op jit(solution)/shard_map/pallas_call | solution.py:529
  61.1 97.2 %shard_map.322 = (f32[192,1024]{1,0:T(8,128)}, bf16[1024,1024]{1,0:T(8,128)(2,1)}, bf16[1024,1024]{1,0:T(8,128)(2,1)}, bf16[4,8,48,1024]{3,2,1,0:T(8,128)(2,1)},...) custom-call(bf16[192,1024]{1,0:T(8,128)(2,1)} %get-tuple-element.60.sent_in, s32[4,8,256]{2,1,0:T(8,128)} %get-tuple-element.61.placed_in.placed, ...), custom_call_target="tpu_custom_call" | custom-call | tf_op jit(solution)/shard_map/pallas_call | solution.py:947
  158.2 82.3 %shard_map.323 = (bf16[192,1024]{1,0:T(8,128)(2,1)}, bf16[192,1024]{1,0:T(8,128)(2,1)}, f32[4,32,1024]{2,1,0:T(8,128)}, f32[8,1024]{1,0:T(8,128)}, f32[8,1024]{1...) custom-call(f32[192,1024]{1,0:T(8,128)} %get-tuple-element.66.d_sum, bf16[192,1024]{1,0:T(8,128)(2,1)} %cot.3, ...), custom_call_target="tpu_custom_call" | custom-call | tf_op jit(solution)/shard_map/pallas_call | solution.py:1351
  240.5 25.8 %shard_map.324 = (f32[1024,1024]{1,0:T(8,128)}, f32[1024,1024]{1,0:T(8,128)}, f32[1024,1024]{1,0:T(8,128)}, f32[1024,1024]{1,0:T(8,128)}, f32[1024,1024]{1,0:T(8...) custom-call(bf16[1024,1024]{1,0:T(8,128)(2,1)} %bitcast.29, ...), custom_call_target="tpu_custom_call" | custom-call | tf_op jit(solution)/shard_map/pallas_call | solution.py:1473
